TPU v7x, 32 devices: a whole 2x2x4 slice. The times are simulated.
32 devices in a mesh: member: 2 (over y), tile: 8 (over z, x), comp: 2 (over core).
Axes of the slice: x: 2, y: 2, z: 4, core: 2. Of those that a mesh axis runs over, the one named last changes fastest.
Arguments:
- atmosphere: bfloat16 [16384, 227], P(('member', 'tile', 'comp')), parts along dimension 0, may hold values from -6 to 6
- mesh_state: bfloat16 [10240, 512], P(('member', 'tile', 'comp')), parts along dimension 0, may hold values from -6 to 6
- edge_geometry: bfloat16 [4, 81920], P(None, ('member', 'tile', 'comp')), parts along dimension 1, may hold values from -6 to 6
- neighbours: int32 [10240, 8], P(('member', 'tile', 'comp')), parts along dimension 0, may hold values from 0 to 960, as said below
- grid_node: int32 [16384], P(('member', 'tile', 'comp')), parts along dimension 0, may hold values from 0 to 319
- ocean_heat_field: float32 [8, 288, 384], P(None, ('member', 'tile', 'comp')), parts along dimension 1, may hold values from -3.5 to 3.5
- east_velocity: float32 [8, 288, 384], P(None, ('member', 'tile', 'comp')), parts along dimension 1, may hold values from -0.3 to 0.3
- north_velocity: float32 [8, 288, 384], P(None, ('member', 'tile', 'comp')), parts along dimension 1, may hold values from -0.3 to 0.3
- ocean_mask: int32 [288, 384], P(('member', 'tile', 'comp')), parts along dimension 0, may hold values from 0 to 1
- intersection_points: int32 [32, 4, 192], P(('member', 'tile', 'comp')), parts along dimension 0, may hold values from 0 to 512, as said below
- intersection_counts: int32 [32, 4], P(('member', 'tile', 'comp')), parts along dimension 0, may hold values from 1 to 192, as said below
- w_geometry: bfloat16 [4, 512], replicated, may hold values from -3 to 3
- w_encode: bfloat16 [227, 512], replicated, may hold values from -0.375 to 0.375
- w_edge_in: bfloat16 [1536, 512], replicated, may hold values from -0.15625 to 0.15625
- w_edge_out: bfloat16 [512, 512], replicated, may hold values from -0.25 to 0.25
- w_node_in: bfloat16 [1024, 512], replicated, may hold values from -0.1875 to 0.1875
- w_node_out: bfloat16 [512, 512], replicated, may hold values from -0.25 to 0.25
- w_decode: bfloat16 [512, 227], replicated, may hold values from -0.25 to 0.25
- gain_edge: float32 [512], replicated, may hold values from 0.25 to 1.75
- gain_node: float32 [512], replicated, may hold values from 0.25 to 1.75
Outputs:
- atmosphere_new: bfloat16 [16384, 227], P(('member', 'tile', 'comp')), parts along dimension 0
- ocean_new: float32 [8, 288, 384], P(None, ('member', 'tile', 'comp')), parts along dimension 1
There are 2 independent parts, one for each index of `member`. A program takes and returns all parts, laid end to end along the dimension named above; an argument that names none is the same for every part. Nothing has to cross between parts.
Inputs may be any that keep to these rules, and one draw needn't show every extreme that they name: `neighbours`: each row holds between 5 and 8 entries below 960 first, then entries equal to 960, which mark empty slots. `intersection_counts`: each row sums to 384 and reaches 192. `intersection_points`: entry [s, o, j] is below 512 exactly when j < intersection_counts[(s - o + 2) mod 16, o], and equals 512 otherwise.
All inputs are finite; a program needn't handle non-finite values.
Results may differ from a plain program's by a relative error of at most 0.0075.
Values may be sent and summed in bfloat16 or wider, within the bound.
No kernel may reach another device: no remote copies, remote signals or barrier semaphores. Data moves between devices by JAX's collectives and lax.ppermute only.
A program may use at most 64 MiB of HBM per device.

v0:
```python
import jax
import jax.numpy as jnp
from jax import lax
from jax.sharding import PartitionSpec as P

K = 8
STEPS = 4
W = 4
OB = 384
BLOCK_LIMIT = 192


COEFF_H = 0.15
COEFF_V = 0.1
COEFF_Q = 0.5
EPSILON = 1e-05


def padded(block, sides, width):
    for axis, dim in sides:
        count = lax.axis_size(axis)
        forward = [(i, i + 1) for i in range(count - 1)]
        forward.append((count - 1, 0))
        backward = [(target, source) for source, target in forward]
        low = lax.ppermute(
            lax.slice_in_dim(block, block.shape[dim] - width, None, axis=dim), axis, forward
        )
        high = lax.ppermute(lax.slice_in_dim(block, 0, width, axis=dim), axis, backward)
        block = jnp.concatenate([low, block, high], axis=dim)
    return block


def from_behind(block, axis, distance):
    devices = range(lax.axis_size(axis))
    route = [((i - distance) % len(devices), i) for i in devices]
    return lax.ppermute(block, axis, route)


def layer_norm(values, gain_row):
    average = jnp.mean(values, axis=-1, keepdims=True)
    centred = values - average
    variance = jnp.mean(centred * centred, axis=-1, keepdims=True)
    return centred * lax.rsqrt(variance + EPSILON) * gain_row


def ocean_step(field_wide, east_wide, north_wide, wet_wide, forcing_wide):
    east_open = wet_wide[:-1] * wet_wide[1:]
    east_face = 0.5 * (east_wide[:, :-1] + east_wide[:, 1:])
    east_flux = east_open * (
        east_face * 0.5 * (field_wide[:, :-1] + field_wide[:, 1:])
        - COEFF_H * (field_wide[:, 1:] - field_wide[:, :-1])
    )
    east_change = east_flux[:, 1:] - east_flux[:, :-1]
    centre = field_wide[:, 1:-1]
    north_here = north_wide[:, 1:-1]
    wet_here = wet_wide[1:-1]
    north_open = wet_here[:, :-1] * wet_here[:, 1:]
    north_face = 0.5 * (north_here[:, :, :-1] + north_here[:, :, 1:])
    north_flux = north_open * (
        north_face * 0.5 * (centre[:, :, :-1] + centre[:, :, 1:])
        - COEFF_H * (centre[:, :, 1:] - centre[:, :, :-1])
    )
    wall_zeros = jnp.zeros(north_flux.shape[:2] + (1,), north_flux.dtype)
    north_flux = jnp.concatenate([wall_zeros, north_flux, wall_zeros], axis=2)
    north_change = north_flux[:, :, 1:] - north_flux[:, :, :-1]
    mixing = COEFF_V * (centre[1:] - centre[:-1]) * wet_here
    level_zeros = jnp.zeros((1,) + mixing.shape[1:], mixing.dtype)
    mixing = jnp.concatenate([level_zeros, mixing, level_zeros], axis=0)
    vertical = mixing[1:] - mixing[:-1]
    tendency = vertical - east_change - north_change
    surface = COEFF_Q * forcing_wide[1:-1] * wet_here
    tendency = jnp.concatenate([tendency[:1] + surface[None], tendency[1:]], axis=0)
    return wet_here * (centre + tendency)


def block_totals(grid_field):
    rows_x, rows_y = grid_field.shape
    return grid_field.reshape(rows_x // 3, 3, rows_y // 3, 3).sum(axis=(1, 3)).reshape(-1)


def spread_blocks(values, rows_x, rows_y):
    blocks = values.reshape(rows_x // 3, 1, rows_y // 3, 1)
    return jnp.broadcast_to(blocks, (rows_x // 3, 3, rows_y // 3, 3)).reshape(rows_x, rows_y)


def body(
    atmosphere,
    mesh_state,
    edge_geometry,
    neighbours,
    grid_node,
    ocean_heat_field,
    east_velocity,
    north_velocity,
    ocean_mask,
    intersection_points,
    intersection_counts,
    w_geometry,
    w_encode,
    w_edge_in,
    w_edge_out,
    w_node_in,
    w_node_out,
    w_decode,
    gain_edge,
    gain_node,
):
    levels, columns, rows_y = ocean_heat_field.shape
    wet_fraction = ocean_mask.astype(jnp.float32)
    statics = jnp.concatenate([east_velocity, north_velocity, wet_fraction[None]], axis=0)
    margin = 1
    statics_wide = padded(statics.astype(jnp.bfloat16), ((("tile", "comp"), 1),), margin).astype(
        statics.dtype
    )
    east_wide = statics_wide[:levels]
    north_wide = statics_wide[levels : 2 * levels]
    wet_wide = statics_wide[2 * levels]
    wet_point_count = block_totals(wet_fraction)
    block_surface_temps = block_totals(ocean_heat_field[0] * wet_fraction) / jnp.maximum(
        wet_point_count, 1.0
    )
    block_wet = jnp.where(wet_point_count > 0.5, 1.0, 0.0)
    counts_row = intersection_counts[0]
    start_positions = jnp.cumsum(counts_row) - counts_row
    slot_index = jnp.arange(BLOCK_LIMIT, dtype=jnp.int32)
    pad_amount = jnp.zeros((BLOCK_LIMIT,), jnp.float32)
    surface_temp_extended = jnp.concatenate([block_surface_temps, pad_amount])
    wet_long = jnp.concatenate([block_wet, pad_amount])
    point_lists = intersection_points[0]
    points_here = atmosphere.shape[0]
    received = []
    for shift_amount in range(W):
        active_positions = slot_index < counts_row[shift_amount]
        surface_temp_portion = jnp.where(
            active_positions,
            lax.dynamic_slice_in_dim(
                surface_temp_extended, start_positions[shift_amount], BLOCK_LIMIT
            ),
            0.0,
        )
        wet_portion = jnp.where(
            active_positions,
            lax.dynamic_slice_in_dim(wet_long, start_positions[shift_amount], BLOCK_LIMIT),
            0.0,
        )
        bundle_portion = jnp.stack([surface_temp_portion, wet_portion])
        received.append(from_behind(bundle_portion, ("tile", "comp"), shift_amount - W // 2))
    arrived = jnp.stack(received, axis=1).reshape(2, -1)
    target_points = point_lists.reshape(-1)
    surface_temp_sum = (
        jnp.zeros((points_here + 1,), jnp.float32).at[target_points].add(arrived[0])[:points_here]
    )
    surface_temp_count = (
        jnp.zeros((points_here + 1,), jnp.float32).at[target_points].add(arrived[1])[:points_here]
    )
    starting_state = atmosphere[:, 0].astype(jnp.float32)
    surface_temp_updated = jnp.where(
        surface_temp_count > 0.5,
        surface_temp_sum / jnp.maximum(surface_temp_count, 1.0),
        starting_state,
    )
    coupled_system = atmosphere.at[:, 0].set(surface_temp_updated.astype(jnp.bfloat16))
    encoded = jnp.dot(coupled_system, w_encode, preferred_element_type=jnp.float32).astype(
        jnp.bfloat16
    )
    node_count = mesh_state.shape[0]
    features = mesh_state.shape[1]
    member = grid_node[None, :] == jnp.arange(node_count, dtype=jnp.int32)[:, None]
    pooled = jnp.dot(member.astype(jnp.bfloat16), encoded, preferred_element_type=jnp.float32)
    pooled_count = jnp.sum(member.astype(jnp.float32), axis=1)
    latent = (
        mesh_state.astype(jnp.float32) + pooled / jnp.maximum(pooled_count, 1.0)[:, None]
    ).astype(jnp.bfloat16)
    edge_latent = jax.nn.silu(
        lax.dot_general(
            edge_geometry, w_geometry, (((0,), (0,)), ((), ())), preferred_element_type=jnp.float32
        )
    ).astype(jnp.bfloat16)
    real_edge = neighbours < 3 * node_count
    sender_pos = jnp.where(real_edge, neighbours, node_count).reshape(-1)
    latent_wide = padded(latent, ((("tile", "comp"), 0),), node_count)
    senders = jnp.take(latent_wide, sender_pos, axis=0)
    receivers = jnp.repeat(latent, K, axis=0)
    joined = jnp.concatenate([edge_latent, senders, receivers], axis=1)
    edge_pre = jnp.dot(joined, w_edge_in, preferred_element_type=jnp.float32)
    edge_hidden = jax.nn.silu(edge_pre).astype(jnp.bfloat16)
    edge_out = jnp.dot(edge_hidden, w_edge_out, preferred_element_type=jnp.float32)
    edge_new = edge_latent.astype(jnp.float32) + layer_norm(edge_out, gain_edge)
    edge_new = edge_new * real_edge.reshape(-1, 1).astype(jnp.float32)
    aggregate = jnp.sum(edge_new.reshape(node_count, K, features), axis=1).astype(jnp.bfloat16)
    node_input = jnp.concatenate([latent, aggregate], axis=1)
    node_hidden = jax.nn.silu(
        jnp.dot(node_input, w_node_in, preferred_element_type=jnp.float32)
    ).astype(jnp.bfloat16)
    node_out = jnp.dot(node_hidden, w_node_out, preferred_element_type=jnp.float32)
    node_new = (latent.astype(jnp.float32) + layer_norm(node_out, gain_node)).astype(jnp.bfloat16)
    picked = jnp.take(node_new, grid_node, axis=0)
    atmosphere_new = (
        coupled_system.astype(jnp.float32)
        + jnp.dot(picked, w_decode, preferred_element_type=jnp.float32)
    ).astype(jnp.bfloat16)
    flux_long = jnp.concatenate([atmosphere_new[:, 1], jnp.zeros((1,), jnp.bfloat16)])
    block_flux = jnp.zeros((OB + 1,), jnp.float32)
    for shift_amount in range(W):
        bundle_portion = jnp.take(flux_long, point_lists[shift_amount])
        landed = from_behind(bundle_portion, ("tile", "comp"), W // 2 - shift_amount)
        active_positions = slot_index < counts_row[shift_amount]
        block_labels = jnp.where(active_positions, start_positions[shift_amount] + slot_index, OB)
        block_flux = block_flux.at[block_labels].add(
            jnp.where(active_positions, landed.astype(jnp.float32), 0.0)
        )
    forcing = spread_blocks(block_flux[:OB], columns, rows_y)
    current = ocean_heat_field
    forcing_wide = jnp.pad(forcing, ((1, 1), (0, 0)))
    for step_index in range(STEPS):
        current_wide = padded(current.astype(jnp.bfloat16), ((("tile", "comp"), 1),), 1).astype(
            current.dtype
        )
        current = ocean_step(current_wide, east_wide, north_wide, wet_wide, forcing_wide)
    return (atmosphere_new, current)


def solution(mesh):
    placed = (
        P(("member", "tile", "comp"), None),
        P(("member", "tile", "comp"), None),
        P(None, ("member", "tile", "comp")),
        P(("member", "tile", "comp"), None),
        P(("member", "tile", "comp")),
        P(None, ("member", "tile", "comp"), None),
        P(None, ("member", "tile", "comp"), None),
        P(None, ("member", "tile", "comp"), None),
        P(("member", "tile", "comp"), None),
        P(("member", "tile", "comp"), None, None),
        P(("member", "tile", "comp"), None),
        P(),
        P(),
        P(),
        P(),
        P(),
        P(),
        P(),
        P(),
        P(),
    )
    return jax.shard_map(
        body,
        mesh=mesh,
        in_specs=placed,
        out_specs=(P(("member", "tile", "comp"), None), P(None, ("member", "tile", "comp"), None)),
        check_vma=False,
    )
```

profile of v0, /device:TPU:0, one launch (start us, length us, event | category | flops | bytes accessed | tf_op | source)
XLA Modules:
  0.0 157.7 jit_solution(4897517491396657531)
XLA Ops:
  16.6 2.6 %fusion.57 = (f32[192]{0:T(256)S(1)}, f32[192]{0:T(256)S(1)}, f32[192]{0:T(256)S(1)}, f32[192]{0:T(256)S(1)}, f32[192]{0:T(256)S(1)}, /*index=5*/f32[192]{0:T(256)S(1)}, f32[192]{0:T(256)S(1)}, f32[192]{0:T(256)S(1)}) fusion(s32[]{:T(128)S(6)} %select_n.197, f32[384]{0:T(512)S(1)} %get-tuple-element.51, s32[]{:T(128)} %bitcast, s32[]{:T(128)S(6)} %select_n.202, ...), kind=kLoop, calls=%fused_computation.175 | loop fusion | flops 2304 | bytes 9248 | tf_op jit(solution)/shard_map/jit(_where)/select_n | solution.py:134
  19.2 6.0 %collective-permute-start = (f32[2,192]{1,0:T(2,128)S(1)}, f32[2,192]{1,0:T(2,128)S(1)}, u32[]{:S(2)}, u32[]{:S(2)}) collective-permute-start(f32[2,192]{1,0:T(2,128)S(1)} %pad_maximum_fusion.5), channel_id=1, source_target_pairs={{2,0},{3,1},{4,2},{5,3},{6,4},{7,5},{8,6},{9,7},{10,8},{11,9},{12,... | collective-permute-start | bytes 4616 | tf_op jit(solution)/shard_map/ppermute | solution.py:36
  34.8 1.8 %compare_select_fusion.7 = s32[192,1]{0,1:T(1,128)} fusion(s32[]{:T(128)} %bitcast.6, s32[]{:T(128)} %bitcast), kind=kLoop, calls=%fused_computation.133 | loop fusion | flops 1152 | bytes 776 | tf_op jit(solution)/shard_map/select_n | solution.py:209
  40.4 3.9 %multiply_convert_fusion.1 = bf16[2560,512]{1,0:T(8,128)(2,1)} fusion(bf16[4,2560]{1,0:T(4,128)(2,1)} %param.26, bf16[4,512]{1,0:T(4,128)(2,1)} %param.35), kind=kOutput, calls=%fused_computation.21 | convolution fusion | flops 17039360 | bytes 2646016 | tf_op jit(solution)/shard_map/dot_general | solution.py:175
  46.4 3.7 %collective-permute-start.7 = (bf16[17,1,384]{2,0,1:T(8,128)(2,1)S(1)}, bf16[17,1,384]{2,0,1:T(8,128)(2,1)S(1)}, u32[]{:S(2)}, u32[]{:S(2)}) collective-permute-start(bf16[17,1,384]{2,0,1:T(8,128)(2,1)S(1)} %get-tuple-element.28), channel_id=1, source_target_pairs={{1,0},{2,1},{3,2},{4,3},{5,4},{6,5},{7,6},{8,7},{9,8},{10,9},{11,1... | collective-permute-start | bytes 39176 | tf_op jit(solution)/shard_map/ppermute | solution.py:28
  50.0 4.4 %collective-permute-start.9 = (bf16[8,1,384]{2,0,1:T(8,128)(2,1)S(1)}, bf16[8,1,384]{2,0,1:T(8,128)(2,1)S(1)}, u32[]{:S(2)}, u32[]{:S(2)}) collective-permute-start(bf16[8,1,384]{2,0,1:T(8,128)(2,1)S(1)} %get-tuple-element.36), channel_id=1, source_target_pairs={{1,0},{2,1},{3,2},{4,3},{5,4},{6,5},{7,6},{8,7},{9,8},{10,9},{11,1... | collective-permute-start | bytes 18440 | tf_op jit(solution)/shard_map/ppermute | solution.py:28
  54.7 5.8 %scatter_custom_fusion = f32[513]{0:T(1024)S(1)} fusion(s32[768]{0:T(1024)S(1)} %fusion.51, f32[768]{0:T(1024)S(1)} %reshape.405, f32[]{:T(128)} %constant.110.clone.1), kind=kCustom, calls=%fused_computation.165 | custom fusion | flops 768 | bytes 2056 | tf_op jit(solution)/shard_map/scatter-add | solution.py:154
  60.5 5.9 %scatter_custom_fusion.1 = f32[513]{0:T(1024)S(1)} fusion(s32[768]{0:T(1024)S(1)} %fusion.51, f32[768]{0:T(1024)S(1)} %reshape.413, f32[]{:T(128)} %constant.110.clone.1), kind=kCustom, calls=%fused_computation.163 | custom fusion | flops 768 | bytes 2056 | tf_op jit(solution)/shard_map/scatter-add | solution.py:151
  67.8 1.9 %broadcast_bitcast_fusion = bf16[2560,512]{1,0:T(8,128)(2,1)} fusion(bf16[320,512]{1,0:T(8,128)(2,1)S(1)} %fusion.8), kind=kLoop, calls=%fused_computation.24 | loop fusion | bytes 2949120 | tf_op jit(solution)/shard_map/reshape | solution.py:183
  69.7 4.4 %collective-permute-start.5 = (bf16[320,512]{1,0:T(8,128)(2,1)S(1)}, bf16[320,512]{1,0:T(8,128)(2,1)S(1)}, u32[]{:S(2)}, u32[]{:S(2)}) collective-permute-start(bf16[320,512]{1,0:T(8,128)(2,1)S(1)} %fusion.8), channel_id=1, source_target_pairs={{1,0},{2,1},{3,2},{4,3},{5,4},{6,5},{7,6},{8,7},{9,8},{10,9},{11,1... | collective-permute-start | bytes 983048 | tf_op jit(solution)/shard_map/ppermute | solution.py:28
  75.4 1.6 %collective-permute-done.4 = bf16[320,512]{1,0:T(8,128)(2,1)S(1)} collective-permute-done((bf16[320,512]{1,0:T(8,128)(2,1)S(1)}, bf16[320,512]{1,0:T(8,128)(2,1)S(1)}, u32[]{:S(2)}, u32[]{:S(2)}) %collective-permute-start.4) | collective-permute-done | bytes 327712 | tf_op jit(solution)/shard_map/ppermute | solution.py:25
  77.0 1.7 %collective-permute-done.5 = bf16[320,512]{1,0:T(8,128)(2,1)S(1)} collective-permute-done((bf16[320,512]{1,0:T(8,128)(2,1)S(1)}, bf16[320,512]{1,0:T(8,128)(2,1)S(1)}, u32[]{:S(2)}, u32[]{:S(2)}) %collective-permute-start.5) | collective-permute-done | bytes 327712 | tf_op jit(solution)/shard_map/ppermute | solution.py:28
  78.8 8.2 %gather_fusion = bf16[2560,512]{1,0:T(8,128)(2,1)} fusion(bf16[960,512]{1,0:T(8,128)(2,1)S(1)} %pad_maximum_fusion, s32[3072]{0:T(1024)S(1)} %pad_clamp_fusion), kind=kCustom, calls=%fused_computation.4 | custom fusion | bytes 5253120 | tf_op jit(solution)/shard_map/jit(_take)/gather | solution.py:182
  87.0 3.8 %broadcast_select_fusion = bf16[2560,512]{1,0:T(8,128)(2,1)} fusion(bf16[2560,512]{1,0:T(8,128)(2,1)} %gather_fusion, pred[2560]{0:T(1024)(128)(4,1)S(1)} %compare_and_fusion), kind=kLoop, calls=%fused_computation.23 | loop fusion | flops 1310720 | bytes 5245440 | tf_op jit(solution)/shard_map/jit(_take)/select_n | solution.py:182
  90.8 9.9 %fusion.83 = (f32[2560]{0:T(1024)S(1)}, f32[2560,512]{1,0:T(8,128)}) fusion(bf16[512,512]{1,0:T(8,128)(2,1)S(1)} %copy-done.9, bf16[1536,512]{1,0:T(8,128)(2,1)S(1)} %copy-done, bf16[2560,512]{1,0:T(8,128)(2,1)} %broadcast_bitcast_fusion, bf16[2560,512]{1,0:T(8,128)(2,1)} %broadcast_select_fusion, bf16[2560,512]{1,0:T(8,128)(2,1)} %multiply_convert_fusion.1), kind=kOutput, calls=%fused_computation.208 | convolution fusion | flops 5400163840 | bytes 15214592 | tf_op jit(solution)/shard_map/dot_general | solution.py:187
  100.8 3.5 %multiply_reduce_fusion = f32[2560]{0:T(1024)S(1)} fusion(f32[2560,512]{1,0:T(8,128)} %get-tuple-element.62, f32[2560]{0:T(1024)S(1)} %broadcast_multiply_fusion.1), kind=kLoop, calls=%fused_computation.19 | loop fusion | flops 3929600 | bytes 5263360 | tf_op jit(solution)/shard_map/reduce_sum | solution.py:42
  104.8 4.1 %bitcast_reduce_fusion = bf16[320,512]{1,0:T(8,128)(2,1)S(1)} fusion(bf16[2560,512]{1,0:T(8,128)(2,1)} %multiply_convert_fusion.1, f32[2560,512]{1,0:T(8,128)S(1)} %copy-done.1, f32[2560]{0:T(1024)S(1)} %reshape.352, f32[512]{0:T(512)S(1)} %copy-done.6, f32[2560]{0:T(1024)S(1)} %add_rsqrt_fusion, f32[2560]{0:T(1024)S(1)} %broadcast_multiply_fusion.1), kind=kLoop, calls=%fused_computation.18 | loop fusion | flops 9011200 | bytes 8224768 | tf_op jit(solution)/shard_map/reduce_sum | solution.py:190
  108.9 2.3 %fusion.86 = (f32[320]{0:T(512)S(1)}, f32[320,512]{1,0:T(8,128)S(1)}) fusion(bf16[512,512]{1,0:T(8,128)(2,1)} %param.40, bf16[1024,512]{1,0:T(8,128)(2,1)} %param.39, bf16[320,512]{1,0:T(8,128)(2,1)S(1)} %bitcast_reduce_fusion, bf16[320,512]{1,0:T(8,128)(2,1)S(1)} %fusion.8), kind=kOutput, calls=%fused_computation.209 | convolution fusion | flops 505609920 | bytes 2884864 | tf_op jit(solution)/shard_map/dot_general | solution.py:195
  111.7 2.0 %gather_fusion.1 = bf16[512,512]{1,0:T(8,128)(2,1)S(1)} fusion(bf16[320,512]{1,0:T(8,128)(2,1)S(1)} %add_convert_fusion, s32[1024]{0:T(1024)S(1)} %pad_clamp_fusion.5), kind=kCustom, calls=%fused_computation.5 | custom fusion | bytes 1050624 | tf_op jit(solution)/shard_map/jit(_take)/gather | solution.py:197
  113.7 1.5 fusion.13
  115.9 1.6 %gather_fusion.2 = bf16[192]{0:T(256)(128)(2,1)S(1)} fusion(bf16[513]{0:T(1024)(128)(2,1)S(1)} %pad_maximum_fusion.9, s32[1024]{0:T(1024)S(1)} %pad_clamp_fusion.4), kind=kCustom, calls=%fused_computation.clone | custom fusion | bytes 1536 | tf_op jit(solution)/shard_map/jit(_take)/gather | solution.py:205
  117.6 1.6 %gather_fusion.3 = bf16[192]{0:T(256)(128)(2,1)S(1)} fusion(bf16[513]{0:T(1024)(128)(2,1)S(1)} %pad_maximum_fusion.9, s32[1024]{0:T(1024)S(1)} %pad_clamp_fusion.3), kind=kCustom, calls=%fused_computation.1.clone | custom fusion | bytes 1536 | tf_op jit(solution)/shard_map/jit(_take)/gather | solution.py:205
  119.3 1.6 %gather_fusion.4 = bf16[192]{0:T(256)(128)(2,1)S(1)} fusion(bf16[513]{0:T(1024)(128)(2,1)S(1)} %pad_maximum_fusion.9, s32[1024]{0:T(1024)S(1)} %pad_clamp_fusion.2), kind=kCustom, calls=%fused_computation.2.clone | custom fusion | bytes 1536 | tf_op jit(solution)/shard_map/jit(_take)/gather | solution.py:205
  120.9 1.6 %gather_fusion.5 = bf16[192]{0:T(256)(128)(2,1)S(1)} fusion(bf16[513]{0:T(1024)(128)(2,1)S(1)} %pad_maximum_fusion.9, s32[1024]{0:T(1024)S(1)} %pad_clamp_fusion.1), kind=kCustom, calls=%fused_computation.3.clone | custom fusion | bytes 1536 | tf_op jit(solution)/shard_map/jit(_take)/gather | solution.py:205
  122.5 4.7 %collective-permute-start.13 = (bf16[192]{0:T(256)(128)(2,1)S(1)}, bf16[192]{0:T(256)(128)(2,1)S(1)}, u32[]{:S(2)}, u32[]{:S(2)}) collective-permute-start(bf16[192]{0:T(256)(128)(2,1)S(1)} %and_select_fusion), channel_id=1, source_target_pairs={{1,0},{2,1},{3,2},{4,3},{5,4},{6,5},{7,6},{8,7},{9,8},{10,9},{11,1... | collective-permute-start | bytes 1160 | tf_op jit(solution)/shard_map/ppermute | solution.py:36
  129.2 2.0 %scatter_custom_fusion.2 = f32[385]{0:T(512)S(1)} fusion(s32[192]{0:T(256)} %bitcast.103, f32[192]{0:T(256)S(1)} %convert_select_fusion.3, f32[]{:T(128)} %constant.110.clone.1), kind=kCustom, calls=%fused_computation.187 | custom fusion | flops 192 | bytes 2052 | tf_op jit(solution)/shard_map/scatter-add | solution.py:209
  131.2 2.1 %scatter_fusion = f32[385]{0:T(512)S(1)} fusion(f32[385]{0:T(512)S(1)} %scatter_custom_fusion.2, s32[192]{0:T(256)S(1)} %bitcast.89, f32[192]{0:T(256)S(1)} %convert_select_fusion.2), kind=kCustom, calls=%fused_computation.9 | custom fusion | flops 192 | bytes 3072 | tf_op jit(solution)/shard_map/scatter-add | solution.py:209
  133.3 1.9 %scatter_fusion.1 = f32[385]{0:T(512)S(1)} fusion(f32[385]{0:T(512)S(1)} %scatter_fusion, s32[192]{0:T(256)S(1)} %bitcast.88, f32[192]{0:T(256)S(1)} %convert_select_fusion.1), kind=kCustom, calls=%fused_computation.10 | custom fusion | flops 192 | bytes 3072 | tf_op jit(solution)/shard_map/scatter-add | solution.py:209
  135.7 1.9 %scatter_fusion.2 = f32[385]{0:T(512)S(1)} fusion(f32[385]{0:T(512)S(1)} %scatter_fusion.1, s32[192]{0:T(256)S(1)} %bitcast.90, f32[192]{0:T(256)S(1)} %convert_select_fusion), kind=kCustom, calls=%fused_computation.11 | custom fusion | flops 192 | bytes 3072 | tf_op jit(solution)/shard_map/scatter-add | solution.py:209
  138.3 4.4 %collective-permute-start.15 = (bf16[8,1,384]{2,0,1:T(8,128)(2,1)S(1)}, bf16[8,1,384]{2,0,1:T(8,128)(2,1)S(1)}, u32[]{:S(2)}, u32[]{:S(2)}) collective-permute-start(bf16[8,1,384]{2,0,1:T(8,128)(2,1)S(1)} %get-tuple-element.34), channel_id=1, source_target_pairs={{1,0},{2,1},{3,2},{4,3},{5,4},{6,5},{7,6},{8,7},{9,8},{10,9},{11,1... | collective-permute-start | bytes 18440 | tf_op jit(solution)/shard_map/ppermute | solution.py:28
  144.6 4.5 %collective-permute-start.17 = (bf16[8,1,384]{2,0,1:T(8,128)(2,1)S(1)}, bf16[8,1,384]{2,0,1:T(8,128)(2,1)S(1)}, u32[]{:S(2)}, u32[]{:S(2)}) collective-permute-start(bf16[8,1,384]{2,0,1:T(8,128)(2,1)S(1)} %get-tuple-element.32), channel_id=1, source_target_pairs={{1,0},{2,1},{3,2},{4,3},{5,4},{6,5},{7,6},{8,7},{9,8},{10,9},{11,1... | collective-permute-start | bytes 18440 | tf_op jit(solution)/shard_map/ppermute | solution.py:28
  150.9 4.5 %collective-permute-start.19 = (bf16[8,1,384]{2,0,1:T(8,128)(2,1)S(1)}, bf16[8,1,384]{2,0,1:T(8,128)(2,1)S(1)}, u32[]{:S(2)}, u32[]{:S(2)}) collective-permute-start(bf16[8,1,384]{2,0,1:T(8,128)(2,1)S(1)} %get-tuple-element.30), channel_id=1, source_target_pairs={{1,0},{2,1},{3,2},{4,3},{5,4},{6,5},{7,6},{8,7},{9,8},{10,9},{11,1... | collective-permute-start | bytes 18440 | tf_op jit(solution)/shard_map/ppermute | solution.py:28
  (178 shorter events, 37.2 us)
Async XLA Ops:
  0.6 90.2 %copy-start = (bf16[1536,512]{1,0:T(8,128)(2,1)S(1)}, bf16[1536,512]{1,0:T(8,128)(2,1)}, u32[]{:S(2)}) copy-start(bf16[1536,512]{1,0:T(8,128)(2,1)} %param.37) | copy-start | bytes 4718596
  19.2 27.2 %collective-permute-start = (f32[2,192]{1,0:T(2,128)S(1)}, f32[2,192]{1,0:T(2,128)S(1)}, u32[]{:S(2)}, u32[]{:S(2)}) collective-permute-start(f32[2,192]{1,0:T(2,128)S(1)} %pad_maximum_fusion.5), channel_id=1, source_target_pairs={{2,0},{3,1},{4,2},{5,3},{6,4},{7,5},{8,6},{9,7},{10,8},{11,9},{12,... | collective-permute-start | bytes 4616 | tf_op jit(solution)/shard_map/ppermute | solution.py:36
  25.2 24.8 %collective-permute-start.1 = (f32[2,192]{1,0:T(2,128)S(1)}, f32[2,192]{1,0:T(2,128)S(1)}, u32[]{:S(2)}, u32[]{:S(2)}) collective-permute-start(f32[2,192]{1,0:T(2,128)S(1)} %pad_maximum_fusion.6), channel_id=1, source_target_pairs={{1,0},{2,1},{3,2},{4,3},{5,4},{6,5},{7,6},{8,7},{9,8},{10,9},{11,1... | collective-permute-start | bytes 4616 | tf_op jit(solution)/shard_map/ppermute | solution.py:36
  25.3 24.7 %collective-permute-start.2 = (f32[2,192]{1,0:T(2,128)S(1)}, f32[2,192]{1,0:T(2,128)S(1)}, u32[]{:S(2)}, u32[]{:S(2)}) collective-permute-start(f32[2,192]{1,0:T(2,128)S(1)} %pad_maximum_fusion.7), channel_id=1, source_target_pairs={{0,0},{1,1},{2,2},{3,3},{4,4},{5,5},{6,6},{7,7},{8,8},{9,9},{10,10... | collective-permute-start | bytes 4616 | tf_op jit(solution)/shard_map/ppermute | solution.py:36
  25.3 29.1 %collective-permute-start.3 = (f32[2,192]{1,0:T(2,128)S(1)}, f32[2,192]{1,0:T(2,128)S(1)}, u32[]{:S(2)}, u32[]{:S(2)}) collective-permute-start(f32[2,192]{1,0:T(2,128)S(1)} %pad_maximum_fusion.8), channel_id=1, source_target_pairs={{15,0},{0,1},{1,2},{2,3},{3,4},{4,5},{5,6},{6,7},{7,8},{8,9},{9,10... | collective-permute-start | bytes 4616 | tf_op jit(solution)/shard_map/ppermute | solution.py:36
  27.7 46.5 %collective-permute-start.6 = (bf16[17,1,384]{2,0,1:T(8,128)(2,1)S(1)}, bf16[17,1,384]{2,0,1:T(8,128)(2,1)S(1)}, u32[]{:S(2)}, u32[]{:S(2)}) collective-permute-start(bf16[17,1,384]{2,0,1:T(8,128)(2,1)S(1)} %get-tuple-element.27), channel_id=1, source_target_pairs={{0,1},{1,2},{2,3},{3,4},{4,5},{5,6},{6,7},{7,8},{8,9},{9,10},{10,1... | collective-permute-start | bytes 39176 | tf_op jit(solution)/shard_map/ppermute | solution.py:25
  40.3 26.8 %copy-start.4 = (s32[512]{0:T(512)S(1)}, s32[512]{0:T(512)}, u32[]{:S(2)}) copy-start(s32[512]{0:T(512)} %param.28) | copy-start | bytes 6148
  40.3 26.8 %copy-start.10 = (bf16[320,512]{1,0:T(8,128)(2,1)S(1)}, bf16[320,512]{1,0:T(8,128)(2,1)}, u32[]{:S(2)}) copy-start(bf16[320,512]{1,0:T(8,128)(2,1)} %param.25) | copy-start | bytes 983044
  40.3 26.8 %copy-start.11 = (bf16[227,512]{1,0:T(8,128)(2,1)S(1)}, bf16[227,512]{1,0:T(8,128)(2,1)}, u32[]{:S(2)}) copy-start(bf16[227,512]{1,0:T(8,128)(2,1)} %param.36) | copy-start | bytes 697348
  46.4 27.8 %collective-permute-start.7 = (bf16[17,1,384]{2,0,1:T(8,128)(2,1)S(1)}, bf16[17,1,384]{2,0,1:T(8,128)(2,1)S(1)}, u32[]{:S(2)}, u32[]{:S(2)}) collective-permute-start(bf16[17,1,384]{2,0,1:T(8,128)(2,1)S(1)} %get-tuple-element.28), channel_id=1, source_target_pairs={{1,0},{2,1},{3,2},{4,3},{5,4},{6,5},{7,6},{8,7},{9,8},{10,9},{11,1... | collective-permute-start | bytes 39176 | tf_op jit(solution)/shard_map/ppermute | solution.py:28
  50.0 19.7 %collective-permute-start.8 = (bf16[8,1,384]{2,0,1:T(8,128)(2,1)S(1)}, bf16[8,1,384]{2,0,1:T(8,128)(2,1)S(1)}, u32[]{:S(2)}, u32[]{:S(2)}) collective-permute-start(bf16[8,1,384]{2,0,1:T(8,128)(2,1)S(1)} %get-tuple-element.35), channel_id=1, source_target_pairs={{0,1},{1,2},{2,3},{3,4},{4,5},{5,6},{6,7},{7,8},{8,9},{9,10},{10,1... | collective-permute-start | bytes 18440 | tf_op jit(solution)/shard_map/ppermute | solution.py:25
  50.0 24.1 %collective-permute-start.9 = (bf16[8,1,384]{2,0,1:T(8,128)(2,1)S(1)}, bf16[8,1,384]{2,0,1:T(8,128)(2,1)S(1)}, u32[]{:S(2)}, u32[]{:S(2)}) collective-permute-start(bf16[8,1,384]{2,0,1:T(8,128)(2,1)S(1)} %get-tuple-element.36), channel_id=1, source_target_pairs={{1,0},{2,1},{3,2},{4,3},{5,4},{6,5},{7,6},{8,7},{9,8},{10,9},{11,1... | collective-permute-start | bytes 18440 | tf_op jit(solution)/shard_map/ppermute | solution.py:28
  67.1 8.2 %copy-start.3 = (bf16[512,227]{0,1:T(8,128)(2,1)}, bf16[512,227]{0,1:T(8,128)(2,1)S(1)}, u32[]{:S(2)}) copy-start(bf16[512,227]{0,1:T(8,128)(2,1)S(1)} %scatter.4) | copy-start | bytes 697348
  67.8 9.2 %collective-permute-start.4 = (bf16[320,512]{1,0:T(8,128)(2,1)S(1)}, bf16[320,512]{1,0:T(8,128)(2,1)S(1)}, u32[]{:S(2)}, u32[]{:S(2)}) collective-permute-start(bf16[320,512]{1,0:T(8,128)(2,1)S(1)} %fusion.8), channel_id=1, source_target_pairs={{0,1},{1,2},{2,3},{3,4},{4,5},{5,6},{6,7},{7,8},{8,9},{9,10},{10,1... | collective-permute-start | bytes 983048 | tf_op jit(solution)/shard_map/ppermute | solution.py:25
  69.7 9.0 %collective-permute-start.5 = (bf16[320,512]{1,0:T(8,128)(2,1)S(1)}, bf16[320,512]{1,0:T(8,128)(2,1)S(1)}, u32[]{:S(2)}, u32[]{:S(2)}) collective-permute-start(bf16[320,512]{1,0:T(8,128)(2,1)S(1)} %fusion.8), channel_id=1, source_target_pairs={{1,0},{2,1},{3,2},{4,3},{5,4},{6,5},{7,6},{8,7},{9,8},{10,9},{11,1... | collective-permute-start | bytes 983048 | tf_op jit(solution)/shard_map/ppermute | solution.py:28
  87.0 3.8 %copy-start.9 = (bf16[512,512]{1,0:T(8,128)(2,1)S(1)}, bf16[512,512]{1,0:T(8,128)(2,1)}, u32[]{:S(2)}) copy-start(bf16[512,512]{1,0:T(8,128)(2,1)} %param.38) | copy-start | bytes 1572868
  100.8 4.0 %copy-start.1 = (f32[2560,512]{1,0:T(8,128)S(1)}, f32[2560,512]{1,0:T(8,128)}, u32[]{:S(2)}) copy-start(f32[2560,512]{1,0:T(8,128)} %get-tuple-element.62) | copy-start | bytes 15728644
  100.8 4.0 %copy-start.6 = (f32[512]{0:T(512)S(1)}, f32[512]{0:T(512)}, u32[]{:S(2)}) copy-start(f32[512]{0:T(512)} %param.42) | copy-start | bytes 6148
  108.9 2.6 %copy-start.5 = (f32[512]{0:T(512)S(1)}, f32[512]{0:T(512)}, u32[]{:S(2)}) copy-start(f32[512]{0:T(512)} %param.43) | copy-start | bytes 6148
  108.9 4.8 %copy-start.7 = (pred[512]{0:T(512)(128)(4,1)S(1)}, pred[512]{0:T(512)(128)(4,1)}, u32[]{:S(2)}) copy-start(pred[512]{0:T(512)(128)(4,1)} %compare_and_fusion.1) | copy-start | bytes 1540
  115.1 0.7 copy-start.8
  115.8 22.4 %copy-start.2 = (f32[7,9,384]{2,0,1:T(8,128)S(1)}, f32[7,9,384]{2,0,1:T(8,128)}, u32[]{:S(2)}) copy-start(f32[7,9,384]{2,0,1:T(8,128)} %slice.515) | copy-start | bytes 290308
  117.5 9.7 %collective-permute-start.10 = (bf16[192]{0:T(256)(128)(2,1)S(1)}, bf16[192]{0:T(256)(128)(2,1)S(1)}, u32[]{:S(2)}, u32[]{:S(2)}) collective-permute-start(bf16[192]{0:T(256)(128)(2,1)S(1)} %and_select_fusion.3), channel_id=1, source_target_pairs={{14,0},{15,1},{0,2},{1,3},{2,4},{3,5},{4,6},{5,7},{6,8},{7,9},{8,1... | collective-permute-start | bytes 1160 | tf_op jit(solution)/shard_map/ppermute | solution.py:36
  119.2 8.6 %collective-permute-start.11 = (bf16[192]{0:T(256)(128)(2,1)S(1)}, bf16[192]{0:T(256)(128)(2,1)S(1)}, u32[]{:S(2)}, u32[]{:S(2)}) collective-permute-start(bf16[192]{0:T(256)(128)(2,1)S(1)} %and_select_fusion.2), channel_id=1, source_target_pairs={{15,0},{0,1},{1,2},{2,3},{3,4},{4,5},{5,6},{6,7},{7,8},{8,9},{9,10... | collective-permute-start | bytes 1160 | tf_op jit(solution)/shard_map/ppermute | solution.py:36
  120.9 7.6 %collective-permute-start.12 = (bf16[192]{0:T(256)(128)(2,1)S(1)}, bf16[192]{0:T(256)(128)(2,1)S(1)}, u32[]{:S(2)}, u32[]{:S(2)}) collective-permute-start(bf16[192]{0:T(256)(128)(2,1)S(1)} %and_select_fusion.1), channel_id=1, source_target_pairs={{0,0},{1,1},{2,2},{3,3},{4,4},{5,5},{6,6},{7,7},{8,8},{9,9},{10,10... | collective-permute-start | bytes 1160 | tf_op jit(solution)/shard_map/ppermute | solution.py:36
  122.5 12.6 %collective-permute-start.13 = (bf16[192]{0:T(256)(128)(2,1)S(1)}, bf16[192]{0:T(256)(128)(2,1)S(1)}, u32[]{:S(2)}, u32[]{:S(2)}) collective-permute-start(bf16[192]{0:T(256)(128)(2,1)S(1)} %and_select_fusion), channel_id=1, source_target_pairs={{1,0},{2,1},{3,2},{4,3},{5,4},{6,5},{7,6},{8,7},{9,8},{10,9},{11,1... | collective-permute-start | bytes 1160 | tf_op jit(solution)/shard_map/ppermute | solution.py:36
  138.3 5.8 %collective-permute-start.14 = (bf16[8,1,384]{2,0,1:T(8,128)(2,1)S(1)}, bf16[8,1,384]{2,0,1:T(8,128)(2,1)S(1)}, u32[]{:S(2)}, u32[]{:S(2)}) collective-permute-start(bf16[8,1,384]{2,0,1:T(8,128)(2,1)S(1)} %get-tuple-element.33), channel_id=1, source_target_pairs={{0,1},{1,2},{2,3},{3,4},{4,5},{5,6},{6,7},{7,8},{8,9},{9,10},{10,1... | collective-permute-start | bytes 18440 | tf_op jit(solution)/shard_map/ppermute | solution.py:25
  138.3 5.8 %collective-permute-start.15 = (bf16[8,1,384]{2,0,1:T(8,128)(2,1)S(1)}, bf16[8,1,384]{2,0,1:T(8,128)(2,1)S(1)}, u32[]{:S(2)}, u32[]{:S(2)}) collective-permute-start(bf16[8,1,384]{2,0,1:T(8,128)(2,1)S(1)} %get-tuple-element.34), channel_id=1, source_target_pairs={{1,0},{2,1},{3,2},{4,3},{5,4},{6,5},{7,6},{8,7},{9,8},{10,9},{11,1... | collective-permute-start | bytes 18440 | tf_op jit(solution)/shard_map/ppermute | solution.py:28
  144.5 5.8 %collective-permute-start.16 = (bf16[8,1,384]{2,0,1:T(8,128)(2,1)S(1)}, bf16[8,1,384]{2,0,1:T(8,128)(2,1)S(1)}, u32[]{:S(2)}, u32[]{:S(2)}) collective-permute-start(bf16[8,1,384]{2,0,1:T(8,128)(2,1)S(1)} %get-tuple-element.31), channel_id=1, source_target_pairs={{0,1},{1,2},{2,3},{3,4},{4,5},{5,6},{6,7},{7,8},{8,9},{9,10},{10,1... | collective-permute-start | bytes 18440 | tf_op jit(solution)/shard_map/ppermute | solution.py:25
  144.6 5.8 %collective-permute-start.17 = (bf16[8,1,384]{2,0,1:T(8,128)(2,1)S(1)}, bf16[8,1,384]{2,0,1:T(8,128)(2,1)S(1)}, u32[]{:S(2)}, u32[]{:S(2)}) collective-permute-start(bf16[8,1,384]{2,0,1:T(8,128)(2,1)S(1)} %get-tuple-element.32), channel_id=1, source_target_pairs={{1,0},{2,1},{3,2},{4,3},{5,4},{6,5},{7,6},{8,7},{9,8},{10,9},{11,1... | collective-permute-start | bytes 18440 | tf_op jit(solution)/shard_map/ppermute | solution.py:28
  150.8 5.8 %collective-permute-start.18 = (bf16[8,1,384]{2,0,1:T(8,128)(2,1)S(1)}, bf16[8,1,384]{2,0,1:T(8,128)(2,1)S(1)}, u32[]{:S(2)}, u32[]{:S(2)}) collective-permute-start(bf16[8,1,384]{2,0,1:T(8,128)(2,1)S(1)} %get-tuple-element.29), channel_id=1, source_target_pairs={{0,1},{1,2},{2,3},{3,4},{4,5},{5,6},{6,7},{7,8},{8,9},{9,10},{10,1... | collective-permute-start | bytes 18440 | tf_op jit(solution)/shard_map/ppermute | solution.py:25
  150.9 5.8 %collective-permute-start.19 = (bf16[8,1,384]{2,0,1:T(8,128)(2,1)S(1)}, bf16[8,1,384]{2,0,1:T(8,128)(2,1)S(1)}, u32[]{:S(2)}, u32[]{:S(2)}) collective-permute-start(bf16[8,1,384]{2,0,1:T(8,128)(2,1)S(1)} %get-tuple-element.30), channel_id=1, source_target_pairs={{1,0},{2,1},{3,2},{4,3},{5,4},{6,5},{7,6},{8,7},{9,8},{10,9},{11,1... | collective-permute-start | bytes 18440 | tf_op jit(solution)/shard_map/ppermute | solution.py:28
where the time goes:
time: 159 us; the launch traced here: 158 us
  other arithmetic  56.1 us (35%)
  starting transfers between devices  38.3 us (24%)
  local copies, waits for them, and re-layouts  28.5 us (18%)
  matrix products  18.1 us (11%)
  between operations  9.16 us (6%)
  waiting for transfers between devices  7.43 us (5%)
    ppermute x6, starting transfers between devices, padded(): lax.ppermute(lax.slice_in_dim(block, 0, width, axis=dim), axis, backward)  25.9 us
    ppermute x8, starting transfers between devices, from_behind(): return lax.ppermute(block, axis, route)  11.4 us
    dot_general x1, matrix products, body(): jnp.dot(edge_hidden, w_edge_out, preferred_element_type=jnp.float32)  9.92 us
    gather x1, local copies, waits for them, and re-layouts, body(): senders = jnp.take(latent_wide, sender_pos, axis=0)  8.21 us
    scatter-add x4, other arithmetic, body(): block_flux.at[block_labels]  7.87 us
    gather x4, local copies, waits for them, and re-layouts, body(): bundle_portion = jnp.take(flux_long, point_lists[shift_amount])  6.41 us
    scatter-add x1, other arithmetic, body(): jnp.zeros((points_here + 1,), jnp.float32).at[target_points].add(arrived[0])  5.85 us
    scatter-add x1, other arithmetic, body(): jnp.zeros((points_here + 1,), jnp.float32).at[target_points].add(arrived[1])  5.85 us
  transfers between devices with their start and end apart: 20, of which 7 were waited for; matrix products, arithmetic and copies ran while one was open for 31% of the time, Pallas kernels for 0%

commit v1 on v0

v1 whole, which is shorter than its diff:
```python
import functools

import jax
import jax.numpy as jnp
from jax import lax
from jax.experimental import pallas as pl
from jax.experimental.pallas import tpu as pltpu
from jax.sharding import PartitionSpec as P

K = 8
STEPS = 4
W = 4
EDGE = 4

COEFF_H = 0.15
COEFF_V = 0.1
COEFF_Q = 0.5
EPSILON = 1e-05

F32 = jnp.float32
BF16 = jnp.bfloat16
AXES = ("tile", "comp")


def shifted(block, distance):
    count = lax.axis_size(AXES)
    return lax.ppermute(block, AXES, [((i - distance) % count, i) for i in range(count)])


def dot(a, b):
    return jnp.dot(a, b, preferred_element_type=F32)


def dot_nt(a, b):
    return lax.dot_general(a, b, (((1,), (1,)), ((), ())), preferred_element_type=F32)


def silu(v):
    return 0.5 * v * (1.0 + jnp.tanh(0.5 * v))


def one_hot(test):
    return jnp.where(test, 1.0, 0.0).astype(BF16)


def iota(shape, dim):
    return lax.broadcasted_iota(jnp.int32, shape, dim)


def pack_kernel(counts, heat, east, north, mask, low_out, high_out, blocks_out):
    columns, rows = mask.shape
    wet = mask[...].astype(F32)
    top = heat[0] * wet
    triples = columns // 3

    def over_columns(x):
        return jnp.concatenate(
            [x[3 * t : 3 * t + 1] + x[3 * t + 1 : 3 * t + 2] + x[3 * t + 2 : 3 * t + 3] for t in range(triples)],
            axis=0,
        )

    sums = over_columns(top)
    first = sums.astype(BF16).astype(F32)
    second = (sums - first).astype(BF16).astype(F32)
    third = sums - first - second
    parts = jnp.concatenate(
        [first, second, third, over_columns(wet), jnp.zeros((16 - 4 * triples, rows), F32)], axis=0
    ).astype(BF16)
    pick = one_hot(iota((rows, rows // 3), 0) // 3 == iota((rows, rows // 3), 1))
    folded = dot(parts, pick)

    def flat(x):
        return jnp.concatenate([x[t : t + 1] for t in range(triples)], axis=1)

    t = triples
    total = flat(folded[:t] + folded[t : 2 * t] + folded[2 * t : 3 * t])
    number = flat(folded[3 * t : 4 * t])
    mean = total / jnp.maximum(number, 1.0)
    mean_high = mean.astype(BF16).astype(F32)
    flags = jnp.where(number > 0.5, 1.0, 0.0)
    lane = iota((1, rows), 1)
    held = jnp.zeros((1, rows), F32)
    for o in range(W):
        held = jnp.where(lane == o, counts[0, o].astype(F32), held)
    bundle = jnp.concatenate(
        [mean_high, mean - mean_high, flags, held, jnp.zeros((4, rows), F32)], axis=0
    )
    blank = jnp.zeros((4, rows), F32)
    for out, begin in ((low_out, 0), (high_out, columns - EDGE)):
        pieces = [source[:, c, :] for source in (heat, east, north) for c in range(begin, begin + EDGE)]
        pieces += [wet[begin : begin + EDGE], blank, bundle]
        out[...] = jnp.concatenate(pieces, axis=0).astype(BF16)
    blocks_out[...] = jnp.concatenate([bundle, jnp.zeros((8, rows), F32)], axis=0).astype(BF16)


def embed_kernel(geometry, w_geometry, w_in, latent_out, part_out, turned):
    edges = geometry.shape[1]
    nodes = edges // K
    flat = jnp.concatenate([geometry[...].astype(F32), jnp.zeros((4, edges), F32)], axis=0)
    turned[:, :8] = flat.T
    weights = w_in[...]
    features = w_geometry.shape[1]
    w_geo = jnp.concatenate([w_geometry[...].astype(F32), jnp.zeros((4, features), F32)], axis=0).astype(BF16)
    for k in range(K):
        points = turned[pl.ds(k, nodes, stride=K), :8].astype(BF16)
        value = silu(dot(points, w_geo)).astype(BF16)
        latent_out[k] = value
        part_out[k] = dot(value, weights).astype(BF16)


def rolled_points(points, starts):
    rows = 2 * points.shape[1]
    empty = jnp.full((1, rows - points.shape[1]), 1 << 20, jnp.int32)
    return [
        pltpu.roll(jnp.concatenate([points[o : o + 1, :], empty], axis=1), starts[o], 1) for o in range(W)
    ]


def before(bundle_rows, o):
    lane = iota((1, bundle_rows.shape[1]), 1)
    return jnp.sum(jnp.where(lane < o, bundle_rows[3:4], 0.0)).astype(jnp.int32)


def latent_kernel(
    counts, far, above, own, below, points, atmosphere, w_encode, grid_node, mesh_state,
    latent_out, coupled_out, placed_out,
):
    parts = [
        far[...].astype(F32)[:8],
        above[...].astype(F32)[-8:],
        own[...].astype(F32)[:8],
        below[...].astype(F32)[-8:],
    ]
    starts = [0, before(parts[1], 1), counts[0, 0] + counts[0, 1], before(parts[3], 3)]
    placed = jnp.concatenate(rolled_points(points, starts), axis=1)
    placed_out[...] = placed
    n_points = atmosphere.shape[0]
    values = jnp.concatenate(parts, axis=1).astype(BF16)
    match = one_hot(iota((n_points, placed.shape[1]), 0) == placed)
    sums = dot_nt(match, values)
    total = sums[:, 0:1] + sums[:, 1:2]
    number = sums[:, 2:3]
    state = atmosphere[...].astype(F32)
    surface = jnp.where(number > 0.5, total / jnp.maximum(number, 1.0), state[:, 0:1])
    coupled = jnp.where(iota(state.shape, 1) == 0, surface, state).astype(BF16)
    coupled_out[...] = coupled
    encoded = dot(coupled, w_encode[...]).astype(BF16)
    member = jnp.where(iota((mesh_state.shape[0], n_points), 0) == grid_node[...], 1.0, 0.0)
    population = jnp.sum(member, axis=1, keepdims=True)
    pooled = dot(member.astype(BF16), encoded)
    latent_out[...] = (mesh_state[...].astype(F32) + pooled / jnp.maximum(population, 1.0)).astype(BF16)


def slot_senders(neighbours, k):
    lane = iota(neighbours.shape, 1)
    return jnp.sum(jnp.where(lane == k, neighbours, 0.0), axis=1, keepdims=True).astype(jnp.int32)


def own_kernel(latent, w_in, part, edge_latent, neighbours, pre_out, base_out, sender):
    nodes, features = latent.shape
    value = latent[...]
    sender[...] = dot(value, w_in[features : 2 * features]).astype(BF16)
    receiver = dot(value, w_in[2 * features :])
    listed = neighbours[...].astype(F32)

    def step(k, base):
        at = slot_senders(listed, k)
        match = one_hot(iota((nodes, nodes), 1) + nodes == at)
        pre_out[k] = (part[k].astype(F32) + receiver + dot(match, sender[...])).astype(BF16)
        return base + jnp.where(at < 3 * nodes, edge_latent[k].astype(F32), 0.0)

    base_out[...] = lax.fori_loop(0, K, step, jnp.zeros((nodes, features), F32))


def normal(values):
    average = jnp.mean(values, axis=-1, keepdims=True)
    centred = values - average
    variance = jnp.mean(centred * centred, axis=-1, keepdims=True)
    return centred, lax.rsqrt(variance + EPSILON)


def mesh_kernel(
    low, high, latent, w_in, w_out, pre, base, neighbours, w_node_in, w_node_out, w_decode,
    gain_edge, gain_node, grid_node, coupled, placed, state_out, flux_out, sender, total,
):
    nodes, features = latent.shape
    w_sender = w_in[features : 2 * features]
    sender[:nodes] = dot(low[...], w_sender).astype(BF16)
    sender[nodes:] = dot(high[...], w_sender).astype(BF16)
    listed = neighbours[...].astype(F32)
    total[...] = jnp.zeros((nodes, features), F32)

    def step(k, carry):
        at = slot_senders(listed, k)
        place = jnp.where(at < nodes, at, jnp.where(at >= 2 * nodes, at - nodes, -1))
        match = one_hot(iota((nodes, 2 * nodes), 1) == place)
        hidden = silu(pre[k].astype(F32) + dot(match, sender[...])).astype(BF16)
        centred, scale = normal(dot(hidden, w_out[...]))
        total[...] += centred * jnp.where(at < 3 * nodes, scale, 0.0)
        return carry

    lax.fori_loop(0, K, step, 0)
    aggregate = (base[...] + total[...] * gain_edge[...]).astype(BF16)
    own = latent[...]
    hidden = silu(dot(own, w_node_in[:features]) + dot(aggregate, w_node_in[features:])).astype(BF16)
    centred, scale = normal(dot(hidden, w_node_out[...]))
    node_new = (own.astype(F32) + centred * scale * gain_node[...]).astype(BF16)
    n_points = coupled.shape[0]
    member = one_hot(iota((nodes, n_points), 0) == grid_node[...])
    picked = lax.dot_general(member, node_new, (((0,), (0,)), ((), ())), preferred_element_type=F32)
    state = (coupled[...].astype(F32) + dot(picked.astype(BF16), w_decode[...])).astype(BF16)
    state_out[...] = state
    channels = state.shape[1]
    flux = dot_nt(one_hot(iota((8, channels), 1) == 1), state).astype(BF16)
    match = one_hot(iota((n_points, placed.shape[1]), 0) == placed[...])
    spread = dot(flux, match)
    rows = placed.shape[1] // W
    out = jnp.zeros((8, rows), F32)
    for o in range(W):
        out = jnp.where(iota((8, rows), 0) == o, spread[:, o * rows : (o + 1) * rows], out)
    flux_out[...] = jnp.concatenate([out, jnp.zeros((8, rows), F32)], axis=0).astype(BF16)


def ready_kernel(heat, east, north, mask, low, high, field_out, wet_out, px_out, qx_out, py_out, qy_out, mix_out):
    columns, rows = mask.shape
    levels = heat.shape[0]
    below, above = low[...].astype(F32), high[...].astype(F32)
    own_wet = mask[...].astype(F32)

    def wide(source, at):
        left = [below[8 * (at * EDGE + c) : 8 * (at * EDGE + c) + 8] for c in range(EDGE)]
        right = [above[8 * (at * EDGE + c) : 8 * (at * EDGE + c) + 8] for c in range(EDGE)]
        return left + [source[:, c, :] for c in range(columns)] + right

    base = 3 * 8 * EDGE
    wet = [below[base + c : base + c + 1] for c in range(EDGE)]
    wet += [own_wet[c : c + 1] for c in range(columns)]
    wet += [above[base + c : base + c + 1] for c in range(EDGE)]
    wet = [jnp.broadcast_to(w, (levels, rows)) for w in wet]
    field, u, v = wide(heat, 0), wide(east, 1), wide(north, 2)
    lane = iota((levels, rows), 1)
    level = iota((levels, rows), 0)
    count = len(field)
    for c in range(count):
        field_out[c] = field[c]
        wet_out[c] = wet[c]
        mix_out[c] = jnp.where(level < levels - 1, COEFF_V * wet[c], 0.0)
        if c + 1 < count:
            opened = wet[c] * wet[c + 1]
            face = 0.25 * (u[c] + u[c + 1])
            px_out[c] = opened * (face + COEFF_H)
            qx_out[c] = opened * (face - COEFF_H)
        opened = jnp.where(lane < rows - 1, wet[c] * pltpu.roll(wet[c], rows - 1, 1), 0.0)
        face = 0.25 * (v[c] + pltpu.roll(v[c], rows - 1, 1))
        py_out[c] = opened * (face + COEFF_H)
        qy_out[c] = opened * (face - COEFF_H)


def ocean_kernel(f_m3, f_m2, f_m1, f_0, f_p1, f_p2, field_in, wet, px, qx, py, qy, mix, out):
    count, levels, rows = field_in.shape
    columns = count - 2 * EDGE
    triples = columns // 3
    span = rows // 3
    fluxes = [f[...].astype(F32) for f in (f_m3, f_m2, f_m1, f_0, f_p1, f_p2)]

    def gathered(begin):
        return sum(fluxes[begin + o][o : o + 1] for o in range(W))

    own = gathered(1)
    blocks = [gathered(0)[:, (triples - 1) * span :]]
    blocks += [own[:, t * span : (t + 1) * span] for t in range(triples)]
    blocks += [gathered(2)[:, :span]]
    blocks += [jnp.zeros((16 - len(blocks), span), F32)]
    expand = one_hot(iota((span, rows), 1) // 3 == iota((span, rows), 0))
    cells = COEFF_Q * dot(jnp.concatenate(blocks, axis=0).astype(BF16), expand)
    level = iota((levels, rows), 0)
    surface = [
        jnp.where(level == 0, jnp.broadcast_to(cells[t : t + 1], (levels, rows)), 0.0)
        for t in range(triples + 2)
    ]
    field = [field_in[c] for c in range(count)]
    for step in range(STEPS):
        begin, end = step + 1, count - step - 1
        across = {c: px[c] * field[c] + qx[c] * field[c + 1] for c in range(begin - 1, end)}
        later = [None] * count
        for c in range(begin, end):
            here = field[c]
            along = py[c] * here + qy[c] * pltpu.roll(here, rows - 1, 1)
            mixed = mix[c] * (pltpu.roll(here, levels - 1, 0) - here)
            group = (c - EDGE + 3) // 3
            change = (
                (across[c - 1] - across[c])
                + (pltpu.roll(along, 1, 1) - along)
                + (mixed - pltpu.roll(mixed, 1, 0))
            )
            later[c] = wet[c] * (here + change + surface[group])
        field = later
    for c in range(columns):
        out[:, c, :] = field[EDGE + c]


def call(kernel, outs, inputs, smem=0, scratch=(), flops=0, bytes_accessed=1 << 20, name=None):
    vmem = pl.BlockSpec(memory_space=pltpu.VMEM)
    specs = [pl.BlockSpec(memory_space=pltpu.SMEM)] * smem + [vmem] * (len(inputs) - smem)
    return pl.pallas_call(
        kernel,
        out_shape=[jax.ShapeDtypeStruct(s, t) for s, t in outs],
        in_specs=specs,
        out_specs=[vmem] * len(outs),
        scratch_shapes=list(scratch),
        compiler_params=pltpu.CompilerParams(vmem_limit_bytes=40 << 20),
        cost_estimate=pl.CostEstimate(flops=flops, bytes_accessed=bytes_accessed, transcendentals=0),
        name=name,
    )(*inputs)


def body(
    atmosphere,
    mesh_state,
    edge_geometry,
    neighbours,
    grid_node,
    ocean_heat_field,
    east_velocity,
    north_velocity,
    ocean_mask,
    intersection_points,
    intersection_counts,
    w_geometry,
    w_encode,
    w_edge_in,
    w_edge_out,
    w_node_in,
    w_node_out,
    w_decode,
    gain_edge,
    gain_node,
):
    levels, columns, rows = ocean_heat_field.shape
    nodes, features = mesh_state.shape
    n_points, channels = atmosphere.shape
    ends = (3 * levels * EDGE + 16, rows)
    few = (16, rows)
    low, high, blocks = call(
        pack_kernel,
        [(ends, BF16), (ends, BF16), (few, BF16)],
        [intersection_counts, ocean_heat_field, east_velocity, north_velocity, ocean_mask],
        smem=1,
        name="pack",
    )
    far = shifted(blocks, -2)
    above = shifted(low, -1)
    below = shifted(high, 1)
    edge_latent, part = call(
        embed_kernel,
        [((K, nodes, features), BF16), ((K, nodes, features), BF16)],
        [edge_geometry, w_geometry, w_edge_in[:features]],
        scratch=[pltpu.VMEM((K * nodes, 128), F32)],
        flops=2 * K * nodes * features * features,
        bytes_accessed=8 << 20,
        name="embed",
    )
    grid_row = grid_node.reshape(1, n_points)
    latent, coupled, placed = call(
        latent_kernel,
        [((nodes, features), BF16), ((n_points, channels), BF16), ((1, W * rows), jnp.int32)],
        [
            intersection_counts, far, above, blocks, below, intersection_points[0], atmosphere,
            w_encode, grid_row, mesh_state,
        ],
        smem=1,
        name="latents",
    )
    latent_low = shifted(latent, 1)
    latent_high = shifted(latent, -1)
    pre, base = call(
        own_kernel,
        [((K, nodes, features), BF16), ((nodes, features), F32)],
        [latent, w_edge_in, part, edge_latent, neighbours],
        scratch=[pltpu.VMEM((nodes, features), BF16)],
        flops=2 * K * nodes * nodes * features,
        bytes_accessed=10 << 20,
        name="own",
    )
    wide = (columns + 2 * EDGE, levels, rows)
    ready = call(
        ready_kernel,
        [(wide, F32)] * 7,
        [ocean_heat_field, east_velocity, north_velocity, ocean_mask, below, above],
        bytes_accessed=4 << 20,
        name="ready",
    )
    state, flux = call(
        mesh_kernel,
        [((n_points, channels), BF16), (few, BF16)],
        [
            latent_low, latent_high, latent, w_edge_in, w_edge_out, pre, base, neighbours,
            w_node_in, w_node_out, w_decode, gain_edge.reshape(1, features),
            gain_node.reshape(1, features), grid_row, coupled, placed,
        ],
        scratch=[pltpu.VMEM((2 * nodes, features), BF16), pltpu.VMEM((nodes, features), F32)],
        flops=2 * K * nodes * 3 * nodes * features,
        bytes_accessed=10 << 20,
        name="mesh",
    )
    arrived = [flux if d == 0 else shifted(flux, d) for d in (3, 2, 1, 0, -1, -2)]
    (ocean_new,) = call(
        ocean_kernel,
        [((levels, columns, rows), F32)],
        [*arrived, *ready],
        bytes_accessed=4 << 20,
        name="ocean",
    )
    return (state, ocean_new)


def solution(mesh):
    ranges = ("member", "tile", "comp")
    placed = (
        P(ranges, None),
        P(ranges, None),
        P(None, ranges),
        P(ranges, None),
        P(ranges),
        P(None, ranges, None),
        P(None, ranges, None),
        P(None, ranges, None),
        P(ranges, None),
        P(ranges, None, None),
        P(ranges, None),
        P(),
        P(),
        P(),
        P(),
        P(),
        P(),
        P(),
        P(),
        P(),
    )
    return jax.shard_map(
        body,
        mesh=mesh,
        in_specs=placed,
        out_specs=(P(ranges, None), P(None, ranges, None)),
        check_vma=False,
    )
```

time: 159 us -> 60.5 us (0.38)
  other arithmetic: 56.1 us -> 0 us
  Pallas kernels: 0 us -> 23.1 us
  starting transfers between devices: 38.3 us -> 17.5 us
  matrix products: 18.1 us -> 0 us
  local copies, waits for them, and re-layouts: 28.5 us -> 13.5 us
  between operations: 9.16 us -> 0.93 us
  waiting for transfers between devices: 7.43 us -> 5.05 us
    pallas_call x0 -> x7, Pallas kernels: none -> 23.1 us  [call(): pl.pallas_call(kernel, out_shape=[jax.ShapeDtypeStruct(s, t) for s, t in...]
    ppermute x20 -> x10, starting transfers between devices: 38.3 us -> 17.5 us  [shifted(): lax.ppermute(block, AXES, [((i - distance) % count, i) for i in range(cou...]
    scatter-add x6 -> x0, other arithmetic: 19.6 us -> none  [the longest x4 7.87 us: body(): block_flux.at[block_labels]]
    dot_general x5 -> x0, matrix products: 18.1 us -> none  [the longest x1 9.92 us: body(): jnp.dot(edge_hidden, w_edge_out, preferred_element_type=jnp.float32)]
    gather x6 -> x0, local copies, waits for them, and re-layouts: 16.6 us -> none  [the longest x1 8.21 us: body(): senders = jnp.take(latent_wide, sender_pos, axis=0)]
    select_n x22 -> x0, other arithmetic: 16 us -> none  [the longest x4 5.6 us: body(): block_flux.at[block_labels]]
    unnamed x27 -> x50, local copies, waits for them, and re-layouts: 2.31 us -> 13.5 us
    reduce_sum x6 -> x0, other arithmetic: 8.97 us -> none  [the longest x1 4.07 us: body(): jnp.sum(edge_new.reshape(node_count, K, features), axis=1)]
  transfers between devices with their start and end apart: 20 -> 10, of which waited for: 7 -> 3; matrix products, arithmetic and copies ran while one was open for 31% -> 6% of each run, Pallas kernels for 0% -> 13%
where the time goes in v1:
time: 60.5 us; the launch traced here: 60.1 us
  Pallas kernels  23.1 us (38%)
  starting transfers between devices  17.5 us (29%)
  local copies, waits for them, and re-layouts  13.5 us (22%)
  waiting for transfers between devices  5.05 us (8%)
  between operations  0.93 us (2%)
    pallas_call x7, Pallas kernels, call(): pl.pallas_call(kernel, out_shape=[jax.ShapeDtypeStruct(s, t) for s, t in...  23.1 us
    ppermute x10, starting transfers between devices, shifted(): lax.ppermute(block, AXES, [((i - distance) % count, i) for i in range(cou...  17.5 us
    unnamed x50, local copies, waits for them, and re-layouts  13.5 us
    ppermute x10, waiting for transfers between devices, shifted(): lax.ppermute(block, AXES, [((i - distance) % count, i) for i in range(cou...  5.05 us
  transfers between devices with their start and end apart: 10, of which 3 were waited for; matrix products, arithmetic and copies ran while one was open for 6% of the time, Pallas kernels for 13%

profile of v1, /device:TPU:0, one launch (start us, length us, event | category | flops | bytes accessed | tf_op | source)
XLA Modules:
  0.0 60.1 jit_solution(4815408628202266438)
XLA Ops:
  0.6 1.0 %copy.22.heat = f32[8,9,384]{2,1,0:T(8,128)S(1)} copy(f32[8,9,384]{2,0,1:T(8,128)} %param.25) | data formatting | bytes 221184 | tf_op args[5]
  1.7 0.9 %copy.23.east = f32[8,9,384]{2,1,0:T(8,128)S(1)} copy(f32[8,9,384]{2,0,1:T(8,128)} %param.26) | data formatting | bytes 221184 | tf_op args[6]
  2.6 0.9 %copy.24.north = f32[8,9,384]{2,1,0:T(8,128)S(1)} copy(f32[8,9,384]{2,0,1:T(8,128)} %param.27) | data formatting | bytes 221184 | tf_op args[7]
  3.6 0.7 %copy-done.4 = s32[9,384]{1,0:T(8,128)S(1)} copy-done((s32[9,384]{1,0:T(8,128)S(1)}, s32[9,384]{1,0:T(8,128)}, u32[]{:S(2)}) %copy-start.4) | copy-done | bytes 13848
  4.3 0.7 %copy-done.7 = s32[1,4]{1,0:T(1,128)S(1)} copy-done((s32[1,4]{1,0:T(1,128)S(1)}, s32[1,4]{1,0:T(1,128)}, u32[]{:S(2)}) %copy-start.7) | copy-done | bytes 40
  5.0 0.7 %pack.1 = (bf16[112,384]{1,0:T(8,128)(2,1)S(1)}, bf16[112,384]{1,0:T(8,128)(2,1)S(1)}, bf16[16,384]{1,0:T(8,128)(2,1)S(1)}) custom-call(s32[1,4]{1,0:T(1,128)S(1)} %copy-done.7, f32[8,9,384]{2,1,0:T(8,128)S(1)} %copy.22.heat, f32[8,9,384]{2,1,0:T(8,128)S(1)} %copy.23.east, f32[8,9,384]{2,1,0:T(8,128)S(1)} %copy.24.north, s32[9,384]{1,0:T(8,128)S(1)} %copy-done.4), custom_call_target="tpu_custom_call" | custom-call | bytes 1048576 | tf_op jit(solution)/shard_map/pack/pallas_call | solution.py:305
  5.7 5.5 %collective-permute-start.1 = (bf16[112,384]{1,0:T(8,128)(2,1)S(1)}, bf16[112,384]{1,0:T(8,128)(2,1)S(1)}, u32[]{:S(2)}, u32[]{:S(2)}) collective-permute-start(bf16[112,384]{1,0:T(8,128)(2,1)S(1)} %get-tuple-element.22), channel_id=1, source_target_pairs={{1,0},{2,1},{3,2},{4,3},{5,4},{6,5},{7,6},{8,7},{9,8},{10,9},{11,1... | collective-permute-start | bytes 258056 | tf_op jit(solution)/shard_map/ppermute | solution.py:27
  11.2 1.1 %collective-permute-start = (bf16[16,384]{1,0:T(8,128)(2,1)S(1)}, bf16[16,384]{1,0:T(8,128)(2,1)S(1)}, u32[]{:S(2)}, u32[]{:S(2)}) collective-permute-start(bf16[16,384]{1,0:T(8,128)(2,1)S(1)} %get-tuple-element.21.own), channel_id=1, source_target_pairs={{2,0},{3,1},{4,2},{5,3},{6,4},{7,5},{8,6},{9,7},{10,8},{11,9},{12,... | collective-permute-start | bytes 36872 | tf_op jit(solution)/shard_map/ppermute | solution.py:27
  12.2 1.1 %copy.25.atmosphere = bf16[512,227]{1,0:T(8,128)(2,1)S(1)} copy(bf16[512,227]{0,1:T(8,128)(2,1)} %param.20) | data formatting | bytes 464896 | tf_op args[0]
  13.3 1.5 %collective-permute-done.far = bf16[16,384]{1,0:T(8,128)(2,1)S(1)} collective-permute-done((bf16[16,384]{1,0:T(8,128)(2,1)S(1)}, bf16[16,384]{1,0:T(8,128)(2,1)S(1)}, u32[]{:S(2)}, u32[]{:S(2)}) %collective-permute-start) | collective-permute-done | bytes 12320 | tf_op jit(solution)/shard_map/ppermute | solution.py:27
  14.9 2.9 %collective-permute-done.2.below.low = bf16[112,384]{1,0:T(8,128)(2,1)S(1)} collective-permute-done((bf16[112,384]{1,0:T(8,128)(2,1)S(1)}, bf16[112,384]{1,0:T(8,128)(2,1)S(1)}, u32[]{:S(2)}, u32[]{:S(2)}) %collective-permute-start.2) | collective-permute-done | bytes 86048 | tf_op jit(solution)/shard_map/ppermute | solution.py:27
  17.8 1.0 %copy-done.1 = bf16[320,512]{1,0:T(8,128)(2,1)S(1)} copy-done((bf16[320,512]{1,0:T(8,128)(2,1)S(1)}, bf16[320,512]{1,0:T(8,128)(2,1)}, u32[]{:S(2)}) %copy-start.1) | copy-done | bytes 327704
  18.8 0.9 %copy-done.3 = bf16[227,512]{1,0:T(8,128)(2,1)S(1)} copy-done((bf16[227,512]{1,0:T(8,128)(2,1)S(1)}, bf16[227,512]{1,0:T(8,128)(2,1)}, u32[]{:S(2)}) %copy-start.3) | copy-done | bytes 232472
  19.7 0.7 %copy-done.6 = s32[1,4,192]{2,1,0:T(4,128)S(1)} copy-done((s32[1,4,192]{2,1,0:T(4,128)S(1)}, s32[1,4,192]{2,1,0:T(4,128)}, u32[]{:S(2)}) %copy-start.6) | copy-done | bytes 3096
  20.4 0.7 %copy-done.8 = s32[1,4]{1,0:T(1,128)S(1)} copy-done((s32[1,4]{1,0:T(1,128)S(1)}, s32[1,4]{1,0:T(1,128)}, u32[]{:S(2)}) %copy-start.8) | copy-done | bytes 40
  21.0 0.7 %copy-done.9 = s32[512]{0:T(512)S(1)} copy-done((s32[512]{0:T(512)S(1)}, s32[512]{0:T(512)}, u32[]{:S(2)}) %copy-start.9) | copy-done | bytes 2072
  21.7 2.4 %latents.1 = (bf16[320,512]{1,0:T(8,128)(2,1)S(1)}, bf16[512,227]{1,0:T(8,128)(2,1)S(1)}, s32[1,1536]{1,0:T(1,128)S(1)}) custom-call(s32[1,4]{1,0:T(1,128)S(1)} %copy-done.8, bf16[16,384]{1,0:T(8,128)(2,1)S(1)} %collective-permute-done.far, bf16[112,384]{1,0:T(8,128)(2,1)S(1)} %collective-permute-done.1.above.high, ...), custom_call_target="tpu_custom_call" | custom-call | bytes 1048576 | tf_op jit(solution)/shard_map/latents/pallas_call | solution.py:305
  24.2 0.7 %copy-done.14 = bf16[512,227]{1,0:T(8,128)(2,1)} copy-done((bf16[512,227]{1,0:T(8,128)(2,1)}, bf16[512,227]{1,0:T(8,128)(2,1)S(1)}, u32[]{:S(2)}) %copy-start.14) | copy-done | bytes 232472
  24.9 4.4 %collective-permute-start.4 = (bf16[320,512]{1,0:T(8,128)(2,1)S(1)}, bf16[320,512]{1,0:T(8,128)(2,1)}, u32[]{:S(2)}, u32[]{:S(2)}) collective-permute-start(bf16[320,512]{1,0:T(8,128)(2,1)S(1)} %get-tuple-element.24.latent), channel_id=1, source_target_pairs={{1,0},{2,1},{3,2},{4,3},{5,4},{6,5},{7,6},{8,7},{9,8},{10,9},{11,1... | collective-permute-start | bytes 983048 | tf_op jit(solution)/shard_map/ppermute | solution.py:27
  29.4 0.1 copy.26.neighbours
  29.5 1.8 %copy.28.w_decode = bf16[512,227]{1,0:T(8,128)(2,1)} copy(bf16[512,227]{0,1:T(8,128)(2,1)} %param.37) | data formatting | bytes 464896 | tf_op args[17]
  31.3 3.2 %embed.1 = (bf16[8,320,512]{2,1,0:T(8,128)(2,1)S(1)}, bf16[8,320,512]{2,1,0:T(8,128)(2,1)S(1)}) custom-call(bf16[4,2560]{1,0:T(4,128)(2,1)S(1)} %copy-done.16, bf16[4,512]{1,0:T(4,128)(2,1)S(1)} %copy-done.17, bf16[512,512]{1,0:T(8,128)(2,1)S(1)} %slice.3.w_in), custom_call_target="tpu_custom_call" | custom-call | flops 1342177280 | bytes 8388608 | tf_op jit(solution)/shard_map/embed/pallas_call | solution.py:305
  34.6 4.4 %own.1 = (bf16[8,320,512]{2,1,0:T(8,128)(2,1)S(1)}, f32[320,512]{1,0:T(8,128)S(1)}) custom-call(bf16[320,512]{1,0:T(8,128)(2,1)S(1)} %get-tuple-element.24.latent, bf16[1536,512]{1,0:T(8,128)(2,1)S(1)} %copy-done, bf16[8,320,512]{2,1,0:T(8,128)(2,1)S(1)} %get-tuple-element.25.part, bf16[8,320,512]{2,1,0:T(8,128)(2,1)S(1)} %get-tuple-element.26.edge_latent, ...), custom_call_target="tpu_custom_call" | custom-call | flops 838860800 | bytes 10485760 | tf_op jit(solution)/shard_map/own/pallas_call | solution.py:305
  39.1 11.3 %mesh.1 = (bf16[512,227]{1,0:T(8,128)(2,1)S(1)}, bf16[16,384]{1,0:T(8,128)(2,1)S(1)}) custom-call(bf16[320,512]{1,0:T(8,128)(2,1)} %collective-permute-done.3.low, bf16[320,512]{1,0:T(8,128)(2,1)} %collective-permute-done.4.high, bf16[320,512]{1,0:T(8,128)(2,1)S(1)} %get-tuple-element.24.latent, bf16[1536,512]{1,0:T(8,128)(2,1)S(1)} %copy-done, ...), custom_call_target="tpu_custom_call" | custom-call | flops 2516582400 | bytes 10485760 | tf_op jit(solution)/shard_map/mesh/pallas_call | solution.py:305
  50.5 0.1 collective-permute-start.7
  50.5 4.4 %collective-permute-start.8 = (bf16[16,384]{1,0:T(8,128)(2,1)S(1)}, bf16[16,384]{1,0:T(8,128)(2,1)S(1)}, u32[]{:S(2)}, u32[]{:S(2)}) collective-permute-start(bf16[16,384]{1,0:T(8,128)(2,1)S(1)} %get-tuple-element.32.f_0), channel_id=1, source_target_pairs={{1,0},{2,1},{3,2},{4,3},{5,4},{6,5},{7,6},{8,7},{9,8},{10,9},{11,1... | collective-permute-start | bytes 36872 | tf_op jit(solution)/shard_map/ppermute | solution.py:27
  55.0 2.0 %collective-permute-start.9 = (bf16[16,384]{1,0:T(8,128)(2,1)S(1)}, bf16[16,384]{1,0:T(8,128)(2,1)S(1)}, u32[]{:S(2)}, u32[]{:S(2)}) collective-permute-start(bf16[16,384]{1,0:T(8,128)(2,1)S(1)} %get-tuple-element.32.f_0), channel_id=1, source_target_pairs={{2,0},{3,1},{4,2},{5,3},{6,4},{7,5},{8,6},{9,7},{10,8},{11,9},{12,... | collective-permute-start | bytes 36872 | tf_op jit(solution)/shard_map/ppermute | solution.py:27
  56.9 0.3 ready.1
  57.2 0.8 %copy.32 = bf16[512,227]{0,1:T(8,128)(2,1)} copy(bf16[512,227]{1,0:T(8,128)(2,1)S(1)} %get-tuple-element.40) | data formatting | bytes 464896
  58.1 0.6 collective-permute-done.9.f_p2
  58.6 0.7 %ocean.1 = f32[8,9,384]{2,1,0:T(8,128)S(1)} custom-call(bf16[16,384]{1,0:T(8,128)(2,1)S(1)} %collective-permute-done.5.f_m3, bf16[16,384]{1,0:T(8,128)(2,1)S(1)} %collective-permute-done.6.f_m2, bf16[16,384]{1,0:T(8,128)(2,1)S(1)} %collective-permute-done.7.f_m1, bf16[16,384]{1,0:T(8,128)(2,1)S(1)} %get-tuple-element.32.f_0, ...), custom_call_target="tpu_custom_call" | custom-call | bytes 4194304 | tf_op jit(solution)/shard_map/ocean/pallas_call | solution.py:305
  59.4 0.7 %copy.33 = f32[8,9,384]{2,0,1:T(8,128)} copy(f32[8,9,384]{2,1,0:T(8,128)S(1)} %ocean.1) | data formatting | bytes 221184
  (46 shorter events, 0.2 us)
Async XLA Ops:
  0.6 28.7 %copy-start = (bf16[1536,512]{1,0:T(8,128)(2,1)S(1)}, bf16[1536,512]{1,0:T(8,128)(2,1)}, u32[]{:S(2)}) copy-start(bf16[1536,512]{1,0:T(8,128)(2,1)} %w_in.3) | copy-start | bytes 4718596
  3.6 0.7 %copy-start.4 = (s32[9,384]{1,0:T(8,128)S(1)}, s32[9,384]{1,0:T(8,128)}, u32[]{:S(2)}) copy-start(s32[9,384]{1,0:T(8,128)} %mask.3) | copy-start | bytes 41476
  4.3 0.7 %copy-start.7 = (s32[1,4]{1,0:T(1,128)S(1)}, s32[1,4]{1,0:T(1,128)}, u32[]{:S(2)}) copy-start(s32[1,4]{1,0:T(1,128)} %counts.3) | copy-start | bytes 52
  5.0 24.4 %copy-start.20 = (s32[320,8]{0,1:T(8,128)S(1)}, s32[320,8]{0,1:T(8,128)}, u32[]{:S(2)}) copy-start(s32[320,8]{0,1:T(8,128)} %param.23) | copy-start | bytes 30724
  5.0 26.3 %copy-start.16 = (bf16[4,2560]{1,0:T(4,128)(2,1)S(1)}, bf16[4,2560]{1,0:T(4,128)(2,1)}, u32[]{:S(2)}) copy-start(bf16[4,2560]{1,0:T(4,128)(2,1)} %geometry.1) | copy-start | bytes 61444
  5.0 26.3 %copy-start.17 = (bf16[4,512]{1,0:T(4,128)(2,1)S(1)}, bf16[4,512]{1,0:T(4,128)(2,1)}, u32[]{:S(2)}) copy-start(bf16[4,512]{1,0:T(4,128)(2,1)} %w_geometry.1) | copy-start | bytes 12292
  5.7 9.2 %collective-permute-start.1 = (bf16[112,384]{1,0:T(8,128)(2,1)S(1)}, bf16[112,384]{1,0:T(8,128)(2,1)S(1)}, u32[]{:S(2)}, u32[]{:S(2)}) collective-permute-start(bf16[112,384]{1,0:T(8,128)(2,1)S(1)} %get-tuple-element.22), channel_id=1, source_target_pairs={{1,0},{2,1},{3,2},{4,3},{5,4},{6,5},{7,6},{8,7},{9,8},{10,9},{11,1... | collective-permute-start | bytes 258056 | tf_op jit(solution)/shard_map/ppermute | solution.py:27
  11.2 6.6 %collective-permute-start.2 = (bf16[112,384]{1,0:T(8,128)(2,1)S(1)}, bf16[112,384]{1,0:T(8,128)(2,1)S(1)}, u32[]{:S(2)}, u32[]{:S(2)}) collective-permute-start(bf16[112,384]{1,0:T(8,128)(2,1)S(1)} %get-tuple-element.23), channel_id=1, source_target_pairs={{15,0},{0,1},{1,2},{2,3},{3,4},{4,5},{5,6},{6,7},{7,8},{8,9},{9,10... | collective-permute-start | bytes 258056 | tf_op jit(solution)/shard_map/ppermute | solution.py:27
  11.2 3.7 %collective-permute-start = (bf16[16,384]{1,0:T(8,128)(2,1)S(1)}, bf16[16,384]{1,0:T(8,128)(2,1)S(1)}, u32[]{:S(2)}, u32[]{:S(2)}) collective-permute-start(bf16[16,384]{1,0:T(8,128)(2,1)S(1)} %get-tuple-element.21.own), channel_id=1, source_target_pairs={{2,0},{3,1},{4,2},{5,3},{6,4},{7,5},{8,6},{9,7},{10,8},{11,9},{12,... | collective-permute-start | bytes 36872 | tf_op jit(solution)/shard_map/ppermute | solution.py:27
  17.8 1.0 %copy-start.1 = (bf16[320,512]{1,0:T(8,128)(2,1)S(1)}, bf16[320,512]{1,0:T(8,128)(2,1)}, u32[]{:S(2)}) copy-start(bf16[320,512]{1,0:T(8,128)(2,1)} %mesh_state.1) | copy-start | bytes 983044
  18.7 0.9 %copy-start.3 = (bf16[227,512]{1,0:T(8,128)(2,1)S(1)}, bf16[227,512]{1,0:T(8,128)(2,1)}, u32[]{:S(2)}) copy-start(bf16[227,512]{1,0:T(8,128)(2,1)} %w_encode.1) | copy-start | bytes 697348
  19.7 0.7 %copy-start.6 = (s32[1,4,192]{2,1,0:T(4,128)S(1)}, s32[1,4,192]{2,1,0:T(4,128)}, u32[]{:S(2)}) copy-start(s32[1,4,192]{2,1,0:T(4,128)} %param.29) | copy-start | bytes 9220
  20.4 0.7 %copy-start.8 = (s32[1,4]{1,0:T(1,128)S(1)}, s32[1,4]{1,0:T(1,128)}, u32[]{:S(2)}) copy-start(s32[1,4]{1,0:T(1,128)} %counts.3) | copy-start | bytes 52
  21.0 0.7 %copy-start.9 = (s32[512]{0:T(512)S(1)}, s32[512]{0:T(512)}, u32[]{:S(2)}) copy-start(s32[512]{0:T(512)} %param.24) | copy-start | bytes 6148
  24.2 0.7 %copy-start.14 = (bf16[512,227]{1,0:T(8,128)(2,1)}, bf16[512,227]{1,0:T(8,128)(2,1)S(1)}, u32[]{:S(2)}) copy-start(bf16[512,227]{1,0:T(8,128)(2,1)S(1)} %get-tuple-element.29.coupled) | copy-start | bytes 697348
  24.9 14.1 %collective-permute-start.3 = (bf16[320,512]{1,0:T(8,128)(2,1)S(1)}, bf16[320,512]{1,0:T(8,128)(2,1)}, u32[]{:S(2)}, u32[]{:S(2)}) collective-permute-start(bf16[320,512]{1,0:T(8,128)(2,1)S(1)} %get-tuple-element.24.latent), channel_id=1, source_target_pairs={{15,0},{0,1},{1,2},{2,3},{3,4},{4,5},{5,6},{6,7},{7,8},{8,9},{9,10... | collective-permute-start | bytes 983048 | tf_op jit(solution)/shard_map/ppermute | solution.py:27
  24.9 14.1 %collective-permute-start.4 = (bf16[320,512]{1,0:T(8,128)(2,1)S(1)}, bf16[320,512]{1,0:T(8,128)(2,1)}, u32[]{:S(2)}, u32[]{:S(2)}) collective-permute-start(bf16[320,512]{1,0:T(8,128)(2,1)S(1)} %get-tuple-element.24.latent), channel_id=1, source_target_pairs={{1,0},{2,1},{3,2},{4,3},{5,4},{6,5},{7,6},{8,7},{9,8},{10,9},{11,1... | collective-permute-start | bytes 983048 | tf_op jit(solution)/shard_map/ppermute | solution.py:27
  34.5 4.5 %copy-start.2 = (bf16[512,227]{1,0:T(8,128)(2,1)S(1)}, bf16[512,227]{1,0:T(8,128)(2,1)}, u32[]{:S(2)}) copy-start(bf16[512,227]{1,0:T(8,128)(2,1)} %copy.28.w_decode) | copy-start | bytes 697348
  34.5 4.5 %copy-start.10 = (s32[512]{0:T(512)S(1)}, s32[512]{0:T(512)}, u32[]{:S(2)}) copy-start(s32[512]{0:T(512)} %param.24) | copy-start | bytes 6148
  34.6 4.5 %copy-start.11 = (bf16[1024,512]{1,0:T(8,128)(2,1)S(1)}, bf16[1024,512]{1,0:T(8,128)(2,1)}, u32[]{:S(2)}) copy-start(bf16[1024,512]{1,0:T(8,128)(2,1)} %w_node_in.1) | copy-start | bytes 3145732
  34.6 4.5 %copy-start.12 = (bf16[512,512]{1,0:T(8,128)(2,1)S(1)}, bf16[512,512]{1,0:T(8,128)(2,1)}, u32[]{:S(2)}) copy-start(bf16[512,512]{1,0:T(8,128)(2,1)} %w_out.1) | copy-start | bytes 1572868
  34.6 4.5 %copy-start.13 = (bf16[512,512]{1,0:T(8,128)(2,1)S(1)}, bf16[512,512]{1,0:T(8,128)(2,1)}, u32[]{:S(2)}) copy-start(bf16[512,512]{1,0:T(8,128)(2,1)} %w_node_out.1) | copy-start | bytes 1572868
  34.6 4.5 %copy-start.15 = (bf16[512,227]{1,0:T(8,128)(2,1)S(1)}, bf16[512,227]{1,0:T(8,128)(2,1)}, u32[]{:S(2)}) copy-start(bf16[512,227]{1,0:T(8,128)(2,1)} %copy-done.14) | copy-start | bytes 697348
  34.6 4.5 %copy-start.18 = (f32[512]{0:T(512)S(1)}, f32[512]{0:T(512)}, u32[]{:S(2)}) copy-start(f32[512]{0:T(512)} %param.38) | copy-start | bytes 6148
  34.6 4.5 %copy-start.19 = (f32[512]{0:T(512)S(1)}, f32[512]{0:T(512)}, u32[]{:S(2)}) copy-start(f32[512]{0:T(512)} %param.39) | copy-start | bytes 6148
  39.1 17.8 %copy-start.5 = (s32[9,384]{1,0:T(8,128)S(1)}, s32[9,384]{1,0:T(8,128)}, u32[]{:S(2)}) copy-start(s32[9,384]{1,0:T(8,128)} %mask.3) | copy-start | bytes 41476
  50.4 7.6 %collective-permute-start.5 = (bf16[16,384]{1,0:T(8,128)(2,1)S(1)}, bf16[16,384]{1,0:T(8,128)(2,1)S(1)}, u32[]{:S(2)}, u32[]{:S(2)}) collective-permute-start(bf16[16,384]{1,0:T(8,128)(2,1)S(1)} %get-tuple-element.32.f_0), channel_id=1, source_target_pairs={{13,0},{14,1},{15,2},{0,3},{1,4},{2,5},{3,6},{4,7},{5,8},{6,9},{7,... | collective-permute-start | bytes 36872 | tf_op jit(solution)/shard_map/ppermute | solution.py:27
  50.4 7.6 %collective-permute-start.6 = (bf16[16,384]{1,0:T(8,128)(2,1)S(1)}, bf16[16,384]{1,0:T(8,128)(2,1)S(1)}, u32[]{:S(2)}, u32[]{:S(2)}) collective-permute-start(bf16[16,384]{1,0:T(8,128)(2,1)S(1)} %get-tuple-element.32.f_0), channel_id=1, source_target_pairs={{14,0},{15,1},{0,2},{1,3},{2,4},{3,5},{4,6},{5,7},{6,8},{7,9},{8,1... | collective-permute-start | bytes 36872 | tf_op jit(solution)/shard_map/ppermute | solution.py:27
  50.5 7.6 %collective-permute-start.7 = (bf16[16,384]{1,0:T(8,128)(2,1)S(1)}, bf16[16,384]{1,0:T(8,128)(2,1)S(1)}, u32[]{:S(2)}, u32[]{:S(2)}) collective-permute-start(bf16[16,384]{1,0:T(8,128)(2,1)S(1)} %get-tuple-element.32.f_0), channel_id=1, source_target_pairs={{15,0},{0,1},{1,2},{2,3},{3,4},{4,5},{5,6},{6,7},{7,8},{8,9},{9,10... | collective-permute-start | bytes 36872 | tf_op jit(solution)/shard_map/ppermute | solution.py:27
  50.5 7.5 %collective-permute-start.8 = (bf16[16,384]{1,0:T(8,128)(2,1)S(1)}, bf16[16,384]{1,0:T(8,128)(2,1)S(1)}, u32[]{:S(2)}, u32[]{:S(2)}) collective-permute-start(bf16[16,384]{1,0:T(8,128)(2,1)S(1)} %get-tuple-element.32.f_0), channel_id=1, source_target_pairs={{1,0},{2,1},{3,2},{4,3},{5,4},{6,5},{7,6},{8,7},{9,8},{10,9},{11,1... | collective-permute-start | bytes 36872 | tf_op jit(solution)/shard_map/ppermute | solution.py:27
  55.0 3.7 %collective-permute-start.9 = (bf16[16,384]{1,0:T(8,128)(2,1)S(1)}, bf16[16,384]{1,0:T(8,128)(2,1)S(1)}, u32[]{:S(2)}, u32[]{:S(2)}) collective-permute-start(bf16[16,384]{1,0:T(8,128)(2,1)S(1)} %get-tuple-element.32.f_0), channel_id=1, source_target_pairs={{2,0},{3,1},{4,2},{5,3},{6,4},{7,5},{8,6},{9,7},{10,8},{11,9},{12,... | collective-permute-start | bytes 36872 | tf_op jit(solution)/shard_map/ppermute | solution.py:27

commit v2 on v1

--- a/solution.py
+++ b/solution.py
@@ -1,5 +1,3 @@
-import functools
-
 import jax
 import jax.numpy as jnp
 from jax import lax
@@ -47,24 +45,36 @@
     return lax.broadcasted_iota(jnp.int32, shape, dim)
 
 
-def pack_kernel(counts, heat, east, north, mask, low_out, high_out, blocks_out):
+def started(pairs, sems):
+    copies = [pltpu.make_async_copy(a, b, sems.at[i]) for i, (a, b) in enumerate(pairs)]
+    for copy in copies:
+        copy.start()
+    return copies
+
+
+def pack_kernel(
+    counts_in, heat_in, east_in, north_in, mask_in, low_out, high_out, blocks_out,
+    counts, heat, east, north, mask, sems,
+):
+    copies = started(
+        ((counts_in, counts), (heat_in, heat), (mask_in, mask), (east_in, east), (north_in, north)), sems
+    )
+    for copy in copies:
+        copy.wait()
     columns, rows = mask.shape
     wet = mask[...].astype(F32)
-    top = heat[0] * wet
     triples = columns // 3
 
     def over_columns(x):
-        return jnp.concatenate(
-            [x[3 * t : 3 * t + 1] + x[3 * t + 1 : 3 * t + 2] + x[3 * t + 2 : 3 * t + 3] for t in range(triples)],
-            axis=0,
-        )
-
-    sums = over_columns(top)
+        return jnp.concatenate([x[3 * t] + x[3 * t + 1] + x[3 * t + 2] for t in range(triples)], axis=0)
+
+    wet_rows = [wet[c : c + 1] for c in range(columns)]
+    sums = over_columns([heat[c, 0:1] * wet_rows[c] for c in range(columns)])
     first = sums.astype(BF16).astype(F32)
     second = (sums - first).astype(BF16).astype(F32)
     third = sums - first - second
     parts = jnp.concatenate(
-        [first, second, third, over_columns(wet), jnp.zeros((16 - 4 * triples, rows), F32)], axis=0
+        [first, second, third, over_columns(wet_rows), jnp.zeros((16 - 4 * triples, rows), F32)], axis=0
     ).astype(BF16)
     pick = one_hot(iota((rows, rows // 3), 0) // 3 == iota((rows, rows // 3), 1))
     folded = dot(parts, pick)
@@ -87,25 +97,56 @@
     )
     blank = jnp.zeros((4, rows), F32)
     for out, begin in ((low_out, 0), (high_out, columns - EDGE)):
-        pieces = [source[:, c, :] for source in (heat, east, north) for c in range(begin, begin + EDGE)]
+        pieces = [source[c] for source in (heat, east, north) for c in range(begin, begin + EDGE)]
         pieces += [wet[begin : begin + EDGE], blank, bundle]
         out[...] = jnp.concatenate(pieces, axis=0).astype(BF16)
     blocks_out[...] = jnp.concatenate([bundle, jnp.zeros((8, rows), F32)], axis=0).astype(BF16)
 
 
-def embed_kernel(geometry, w_geometry, w_in, latent_out, part_out, turned):
+def members(nodes, grid_row):
+    return one_hot(iota((nodes, grid_row.shape[1]), 0) == grid_row)
+
+
+def embed_kernel(
+    geometry_in, w_geometry_in, w_in_in, atmosphere_in, w_encode_in, grid_row_in, mesh_state_in,
+    latent_out, part_out, plain_out,
+    turned, geometry, w_geometry, weights, atmosphere, w_encode, grid_row, mesh_state, sems,
+):
+    first = w_in_in.at[pl.ds(0, weights.shape[0])]
+    copies = started(
+        (
+            (geometry_in, geometry),
+            (w_geometry_in, w_geometry),
+            (grid_row_in, grid_row),
+            (atmosphere_in, atmosphere),
+            (w_encode_in, w_encode),
+            (mesh_state_in, mesh_state),
+            (first, weights),
+        ),
+        sems,
+    )
+    for copy in copies:
+        copy.wait()
     edges = geometry.shape[1]
     nodes = edges // K
+    features = w_geometry.shape[1]
     flat = jnp.concatenate([geometry[...].astype(F32), jnp.zeros((4, edges), F32)], axis=0)
     turned[:, :8] = flat.T
-    weights = w_in[...]
-    features = w_geometry.shape[1]
+    member = members(nodes, grid_row[...])
+    population = jnp.sum(member.astype(F32), axis=1, keepdims=True)
+    state = atmosphere[...]
+    state = jnp.where(iota(state.shape, 0) == 0, 0.0, state.astype(F32)).astype(BF16)
+    pooled = dot_nt(member, state) / jnp.maximum(population, 1.0)
+    pooled_high = pooled.astype(BF16)
+    pooled_low = (pooled - pooled_high.astype(F32)).astype(BF16)
+    encode = w_encode[...]
+    plain_out[...] = mesh_state[...].astype(F32) + dot(pooled_high, encode) + dot(pooled_low, encode)
     w_geo = jnp.concatenate([w_geometry[...].astype(F32), jnp.zeros((4, features), F32)], axis=0).astype(BF16)
     for k in range(K):
         points = turned[pl.ds(k, nodes, stride=K), :8].astype(BF16)
         value = silu(dot(points, w_geo)).astype(BF16)
         latent_out[k] = value
-        part_out[k] = dot(value, weights).astype(BF16)
+        part_out[k] = dot(value, weights[...]).astype(BF16)
 
 
 def rolled_points(points, starts):
@@ -122,8 +163,8 @@
 
 
 def latent_kernel(
-    counts, far, above, own, below, points, atmosphere, w_encode, grid_node, mesh_state,
-    latent_out, coupled_out, placed_out,
+    far, above, own, below, points, atmosphere, w_encode, grid_row, plain,
+    latent_out, surface_out, placed_out,
 ):
     parts = [
         far[...].astype(F32)[:8],
@@ -131,29 +172,32 @@
         own[...].astype(F32)[:8],
         below[...].astype(F32)[-8:],
     ]
-    starts = [0, before(parts[1], 1), counts[0, 0] + counts[0, 1], before(parts[3], 3)]
+    starts = [0, before(parts[1], 1), before(parts[2], 2), before(parts[3], 3)]
     placed = jnp.concatenate(rolled_points(points, starts), axis=1)
     placed_out[...] = placed
-    n_points = atmosphere.shape[0]
+    n_points = grid_row.shape[1]
     values = jnp.concatenate(parts, axis=1).astype(BF16)
     match = one_hot(iota((n_points, placed.shape[1]), 0) == placed)
-    sums = dot_nt(match, values)
-    total = sums[:, 0:1] + sums[:, 1:2]
-    number = sums[:, 2:3]
-    state = atmosphere[...].astype(F32)
-    surface = jnp.where(number > 0.5, total / jnp.maximum(number, 1.0), state[:, 0:1])
-    coupled = jnp.where(iota(state.shape, 1) == 0, surface, state).astype(BF16)
-    coupled_out[...] = coupled
-    encoded = dot(coupled, w_encode[...]).astype(BF16)
-    member = jnp.where(iota((mesh_state.shape[0], n_points), 0) == grid_node[...], 1.0, 0.0)
-    population = jnp.sum(member, axis=1, keepdims=True)
-    pooled = dot(member.astype(BF16), encoded)
-    latent_out[...] = (mesh_state[...].astype(F32) + pooled / jnp.maximum(population, 1.0)).astype(BF16)
-
-
-def slot_senders(neighbours, k):
-    lane = iota(neighbours.shape, 1)
-    return jnp.sum(jnp.where(lane == k, neighbours, 0.0), axis=1, keepdims=True).astype(jnp.int32)
+    sums = dot_nt(values, match)
+    total = sums[0:1] + sums[1:2]
+    number = sums[2:3]
+    surface = jnp.where(
+        number > 0.5, total / jnp.maximum(number, 1.0), atmosphere[0:16].astype(F32)[0:1]
+    )
+    surface_out[...] = surface
+    pair = jnp.concatenate([surface, jnp.ones((7, n_points), F32)], axis=0).astype(BF16)
+    pooled = dot_nt(members(plain.shape[0], grid_row[...]), pair)
+    share = pooled[:, 0:1] / jnp.maximum(pooled[:, 1:2], 1.0)
+    latent_out[...] = (plain[...] + share * w_encode[0:16].astype(F32)[0:1]).astype(BF16)
+
+
+def listed_slots(neighbours):
+    return neighbours[...].astype(F32).T
+
+
+def slot_senders(listed, k):
+    lane = iota(listed.shape, 1)
+    return jnp.sum(jnp.where(lane == k, listed, 0.0), axis=1, keepdims=True).astype(jnp.int32)
 
 
 def own_kernel(latent, w_in, part, edge_latent, neighbours, pre_out, base_out, sender):
@@ -161,7 +205,7 @@
     value = latent[...]
     sender[...] = dot(value, w_in[features : 2 * features]).astype(BF16)
     receiver = dot(value, w_in[2 * features :])
-    listed = neighbours[...].astype(F32)
+    listed = listed_slots(neighbours)
 
     def step(k, base):
         at = slot_senders(listed, k)
@@ -181,13 +225,13 @@
 
 def mesh_kernel(
     low, high, latent, w_in, w_out, pre, base, neighbours, w_node_in, w_node_out, w_decode,
-    gain_edge, gain_node, grid_node, coupled, placed, state_out, flux_out, sender, total,
+    gain_edge, gain_node, grid_row, atmosphere, surface, placed, state_out, flux_out, sender, total,
 ):
     nodes, features = latent.shape
     w_sender = w_in[features : 2 * features]
     sender[:nodes] = dot(low[...], w_sender).astype(BF16)
     sender[nodes:] = dot(high[...], w_sender).astype(BF16)
-    listed = neighbours[...].astype(F32)
+    listed = listed_slots(neighbours)
     total[...] = jnp.zeros((nodes, features), F32)
 
     def step(k, carry):
@@ -205,13 +249,16 @@
     hidden = silu(dot(own, w_node_in[:features]) + dot(aggregate, w_node_in[features:])).astype(BF16)
     centred, scale = normal(dot(hidden, w_node_out[...]))
     node_new = (own.astype(F32) + centred * scale * gain_node[...]).astype(BF16)
-    n_points = coupled.shape[0]
-    member = one_hot(iota((nodes, n_points), 0) == grid_node[...])
-    picked = lax.dot_general(member, node_new, (((0,), (0,)), ((), ())), preferred_element_type=F32)
-    state = (coupled[...].astype(F32) + dot(picked.astype(BF16), w_decode[...])).astype(BF16)
-    state_out[...] = state
-    channels = state.shape[1]
-    flux = dot_nt(one_hot(iota((8, channels), 1) == 1), state).astype(BF16)
+    change = dot_nt(w_decode[...], node_new)
+    change_high = change.astype(BF16)
+    change_low = (change - change_high.astype(F32)).astype(BF16)
+    member = members(nodes, grid_row[...])
+    state = atmosphere[...].astype(F32)
+    state = jnp.where(iota(state.shape, 0) == 0, surface[...].astype(BF16).astype(F32), state)
+    state = state + dot(change_high, member) + dot(change_low, member)
+    state_out[...] = state.astype(BF16)
+    n_points = state.shape[1]
+    flux = jnp.broadcast_to(state[1:2], (8, n_points)).astype(BF16)
     match = one_hot(iota((n_points, placed.shape[1]), 0) == placed[...])
     spread = dot(flux, match)
     rows = placed.shape[1] // W
@@ -223,14 +270,14 @@
 
 def ready_kernel(heat, east, north, mask, low, high, field_out, wet_out, px_out, qx_out, py_out, qy_out, mix_out):
     columns, rows = mask.shape
-    levels = heat.shape[0]
+    levels = heat.shape[1]
     below, above = low[...].astype(F32), high[...].astype(F32)
     own_wet = mask[...].astype(F32)
 
     def wide(source, at):
         left = [below[8 * (at * EDGE + c) : 8 * (at * EDGE + c) + 8] for c in range(EDGE)]
         right = [above[8 * (at * EDGE + c) : 8 * (at * EDGE + c) + 8] for c in range(EDGE)]
-        return left + [source[:, c, :] for c in range(columns)] + right
+        return left + [source[c] for c in range(columns)] + right
 
     base = 3 * 8 * EDGE
     wet = [below[base + c : base + c + 1] for c in range(EDGE)]
@@ -296,17 +343,21 @@
             later[c] = wet[c] * (here + change + surface[group])
         field = later
     for c in range(columns):
-        out[:, c, :] = field[EDGE + c]
-
-
-def call(kernel, outs, inputs, smem=0, scratch=(), flops=0, bytes_accessed=1 << 20, name=None):
-    vmem = pl.BlockSpec(memory_space=pltpu.VMEM)
-    specs = [pl.BlockSpec(memory_space=pltpu.SMEM)] * smem + [vmem] * (len(inputs) - smem)
+        out[c] = field[EDGE + c]
+
+
+VMEM = pl.BlockSpec(memory_space=pltpu.VMEM)
+HBM = pl.BlockSpec(memory_space=pltpu.HBM)
+
+
+def call(kernel, outs, inputs, spec=VMEM, scratch=(), flops=0, bytes_accessed=1 << 20, name=None):
+    if spec is HBM:
+        inputs = [pltpu.with_memory_space_constraint(x, pltpu.HBM) for x in inputs]
     return pl.pallas_call(
         kernel,
         out_shape=[jax.ShapeDtypeStruct(s, t) for s, t in outs],
-        in_specs=specs,
-        out_specs=[vmem] * len(outs),
+        in_specs=[spec] * len(inputs),
+        out_specs=[VMEM] * len(outs),
         scratch_shapes=list(scratch),
         compiler_params=pltpu.CompilerParams(vmem_limit_bytes=40 << 20),
         cost_estimate=pl.CostEstimate(flops=flops, bytes_accessed=bytes_accessed, transcendentals=0),
@@ -339,36 +390,57 @@
     levels, columns, rows = ocean_heat_field.shape
     nodes, features = mesh_state.shape
     n_points, channels = atmosphere.shape
+    heat, east, north = (
+        x.transpose(1, 0, 2) for x in (ocean_heat_field, east_velocity, north_velocity)
+    )
+    atmosphere_t = atmosphere.T
+    slots = neighbours.T
+    grid_row = grid_node.reshape(1, n_points)
     ends = (3 * levels * EDGE + 16, rows)
     few = (16, rows)
+    own_ocean = (columns, levels, rows)
     low, high, blocks = call(
         pack_kernel,
         [(ends, BF16), (ends, BF16), (few, BF16)],
-        [intersection_counts, ocean_heat_field, east_velocity, north_velocity, ocean_mask],
-        smem=1,
+        [intersection_counts, heat, east, north, ocean_mask],
+        spec=HBM,
+        scratch=[
+            pltpu.SMEM((1, W), jnp.int32),
+            pltpu.VMEM(own_ocean, F32),
+            pltpu.VMEM(own_ocean, F32),
+            pltpu.VMEM(own_ocean, F32),
+            pltpu.VMEM((columns, rows), jnp.int32),
+            pltpu.SemaphoreType.DMA((5,)),
+        ],
         name="pack",
     )
     far = shifted(blocks, -2)
     above = shifted(low, -1)
     below = shifted(high, 1)
-    edge_latent, part = call(
+    edge_latent, part, plain = call(
         embed_kernel,
-        [((K, nodes, features), BF16), ((K, nodes, features), BF16)],
-        [edge_geometry, w_geometry, w_edge_in[:features]],
-        scratch=[pltpu.VMEM((K * nodes, 128), F32)],
+        [((K, nodes, features), BF16), ((K, nodes, features), BF16), ((nodes, features), F32)],
+        [edge_geometry, w_geometry, w_edge_in, atmosphere_t, w_encode, grid_row, mesh_state],
+        spec=HBM,
+        scratch=[
+            pltpu.VMEM((K * nodes, 128), F32),
+            pltpu.VMEM(edge_geometry.shape, BF16),
+            pltpu.VMEM(w_geometry.shape, BF16),
+            pltpu.VMEM((features, features), BF16),
+            pltpu.VMEM((channels, n_points), BF16),
+            pltpu.VMEM(w_encode.shape, BF16),
+            pltpu.VMEM((1, n_points), jnp.int32),
+            pltpu.VMEM((nodes, features), BF16),
+            pltpu.SemaphoreType.DMA((7,)),
+        ],
         flops=2 * K * nodes * features * features,
         bytes_accessed=8 << 20,
         name="embed",
     )
-    grid_row = grid_node.reshape(1, n_points)
-    latent, coupled, placed = call(
+    latent, surface, placed = call(
         latent_kernel,
-        [((nodes, features), BF16), ((n_points, channels), BF16), ((1, W * rows), jnp.int32)],
-        [
-            intersection_counts, far, above, blocks, below, intersection_points[0], atmosphere,
-            w_encode, grid_row, mesh_state,
-        ],
-        smem=1,
+        [((nodes, features), BF16), ((1, n_points), F32), ((1, W * rows), jnp.int32)],
+        [far, above, blocks, below, intersection_points[0], atmosphere_t, w_encode, grid_row, plain],
         name="latents",
     )
     latent_low = shifted(latent, 1)
@@ -376,7 +448,7 @@
     pre, base = call(
         own_kernel,
         [((K, nodes, features), BF16), ((nodes, features), F32)],
-        [latent, w_edge_in, part, edge_latent, neighbours],
+        [latent, w_edge_in, part, edge_latent, slots],
         scratch=[pltpu.VMEM((nodes, features), BF16)],
         flops=2 * K * nodes * nodes * features,
         bytes_accessed=10 << 20,
@@ -386,17 +458,17 @@
     ready = call(
         ready_kernel,
         [(wide, F32)] * 7,
-        [ocean_heat_field, east_velocity, north_velocity, ocean_mask, below, above],
+        [heat, east, north, ocean_mask, below, above],
         bytes_accessed=4 << 20,
         name="ready",
     )
     state, flux = call(
         mesh_kernel,
-        [((n_points, channels), BF16), (few, BF16)],
+        [((channels, n_points), BF16), (few, BF16)],
         [
-            latent_low, latent_high, latent, w_edge_in, w_edge_out, pre, base, neighbours,
-            w_node_in, w_node_out, w_decode, gain_edge.reshape(1, features),
-            gain_node.reshape(1, features), grid_row, coupled, placed,
+            latent_low, latent_high, latent, w_edge_in, w_edge_out, pre, base, slots,
+            w_node_in, w_node_out, w_decode.T, gain_edge.reshape(1, features),
+            gain_node.reshape(1, features), grid_row, atmosphere_t, surface, placed,
         ],
         scratch=[pltpu.VMEM((2 * nodes, features), BF16), pltpu.VMEM((nodes, features), F32)],
         flops=2 * K * nodes * 3 * nodes * features,
@@ -406,12 +478,12 @@
     arrived = [flux if d == 0 else shifted(flux, d) for d in (3, 2, 1, 0, -1, -2)]
     (ocean_new,) = call(
         ocean_kernel,
-        [((levels, columns, rows), F32)],
+        [(own_ocean, F32)],
         [*arrived, *ready],
         bytes_accessed=4 << 20,
         name="ocean",
     )
-    return (state, ocean_new)
+    return (state.T, ocean_new.transpose(1, 0, 2))
 
 
 def solution(mesh):

time: 60.5 us -> 47.7 us (0.79)
  local copies, waits for them, and re-layouts: 13.5 us -> 0.09 us
  starting transfers between devices: 17.5 us -> 20.4 us
  waiting for transfers between devices: 5.05 us -> 2.32 us
  Pallas kernels: 23.1 us -> 23.9 us
    unnamed x50 -> x32, local copies, waits for them, and re-layouts: 13.5 us -> 0.09 us
    ppermute x10, starting transfers between devices: 17.5 us -> 20.4 us  [shifted(): lax.ppermute(block, AXES, [((i - distance) % count, i) for i in range(cou...]
    ppermute x10, waiting for transfers between devices: 5.05 us -> 2.32 us  [shifted(): lax.ppermute(block, AXES, [((i - distance) % count, i) for i in range(cou...]
    pallas_call x7, Pallas kernels: 23.1 us -> 23.9 us  [call(): pl.pallas_call(kernel, out_shape=[jax.ShapeDtypeStruct(s, t) for s, t in...]
  transfers between devices with their start and end apart: 10 -> 10, of which waited for: 3 -> 3; matrix products, arithmetic and copies ran while one was open for 6% -> 0% of each run, Pallas kernels for 13% -> 20%
where the time goes in v2:
time: 47.7 us; the launch traced here: 47.5 us
  Pallas kernels  23.9 us (50%)
  starting transfers between devices  20.4 us (43%)
  waiting for transfers between devices  2.32 us (5%)
  between operations  0.87 us (2%)
    pallas_call x7, Pallas kernels, call(): pl.pallas_call(kernel, out_shape=[jax.ShapeDtypeStruct(s, t) for s, t in...  23.9 us
    ppermute x10, starting transfers between devices, shifted(): lax.ppermute(block, AXES, [((i - distance) % count, i) for i in range(cou...  20.4 us
    ppermute x10, waiting for transfers between devices, shifted(): lax.ppermute(block, AXES, [((i - distance) % count, i) for i in range(cou...  2.32 us
  transfers between devices with their start and end apart: 10, of which 3 were waited for; matrix products, arithmetic and copies ran while one was open for 0% of the time, Pallas kernels for 20%

profile of v2, /device:TPU:0, one launch (start us, length us, event | category | flops | bytes accessed | tf_op | source)
XLA Modules:
  0.0 47.5 jit_solution(4941377570368790156)
XLA Ops:
  0.6 0.0 copy-start.4
  0.6 0.0 copy-start.5
  0.7 0.0 copy-start.9
  0.7 1.3 %pack.1 = (bf16[112,384]{1,0:T(8,128)(2,1)S(1)}, bf16[112,384]{1,0:T(8,128)(2,1)S(1)}, bf16[16,384]{1,0:T(8,128)(2,1)S(1)}) custom-call(s32[1,4]{1,0:T(1,128)} %counts_in.1, f32[9,8,384]{2,1,0:T(8,128)} %bitcast.12, f32[9,8,384]{2,1,0:T(8,128)} %bitcast.14, f32[9,8,384]{2,1,0:T(8,128)} %bitcast.16, s32[9,384]{1,0:T(8,128)} %mask.1), custom_call_target="tpu_custom_call" | custom-call | bytes 1048576 | tf_op jit(solution)/shard_map/pack/pallas_call | solution.py:356
  2.0 5.5 %collective-permute-start.1 = (bf16[112,384]{1,0:T(8,128)(2,1)S(1)}, bf16[112,384]{1,0:T(8,128)(2,1)S(1)}, u32[]{:S(2)}, u32[]{:S(2)}) collective-permute-start(bf16[112,384]{1,0:T(8,128)(2,1)S(1)} %get-tuple-element.23), channel_id=1, source_target_pairs={{1,0},{2,1},{3,2},{4,3},{5,4},{6,5},{7,6},{8,7},{9,8},{10,9},{11,1... | collective-permute-start | bytes 258056 | tf_op jit(solution)/shard_map/ppermute | solution.py:25
  7.5 0.0 collective-permute-start.2
  7.5 1.1 %collective-permute-start = (bf16[16,384]{1,0:T(8,128)(2,1)S(1)}, bf16[16,384]{1,0:T(8,128)(2,1)S(1)}, u32[]{:S(2)}, u32[]{:S(2)}) collective-permute-start(bf16[16,384]{1,0:T(8,128)(2,1)S(1)} %get-tuple-element.22.own), channel_id=1, source_target_pairs={{2,0},{3,1},{4,2},{5,3},{6,4},{7,5},{8,6},{9,7},{10,8},{11,9},{12,... | collective-permute-start | bytes 36872 | tf_op jit(solution)/shard_map/ppermute | solution.py:25
  8.6 5.0 %embed.1 = (bf16[8,320,512]{2,1,0:T(8,128)(2,1)S(1)}, bf16[8,320,512]{2,1,0:T(8,128)(2,1)S(1)}, f32[320,512]{1,0:T(8,128)S(1)}) custom-call(bf16[4,2560]{1,0:T(4,128)(2,1)} %geometry_in.1, bf16[4,512]{1,0:T(4,128)(2,1)} %w_geometry_in.1, bf16[1536,512]{1,0:T(8,128)(2,1)} %w_in.3, bf16[227,512]{1,0:T(8,128)(2,1)} %bitcast.18, bf16[227,512]{1,0:T(8,128)(2,1)} %w_encode.1, ...), custom_call_target="tpu_custom_call" | custom-call | flops 1342177280 | bytes 8388608 | tf_op jit(solution)/shard_map/embed/pallas_call | solution.py:356
  13.6 0.0 collective-permute-done.far
  13.6 0.5 collective-permute-done.2.below.low
  14.1 1.0 %latents.1 = (bf16[320,512]{1,0:T(8,128)(2,1)S(1)}, f32[1,512]{1,0:T(1,128)S(1)}, s32[1,1536]{1,0:T(1,128)S(1)}) custom-call(bf16[16,384]{1,0:T(8,128)(2,1)S(1)} %collective-permute-done.far, bf16[112,384]{1,0:T(8,128)(2,1)S(1)} %collective-permute-done.1.above.high, bf16[16,384]{1,0:T(8,128)(2,1)S(1)} %get-tuple-element.22.own, ...), custom_call_target="tpu_custom_call" | custom-call | bytes 1048576 | tf_op jit(solution)/shard_map/latents/pallas_call | solution.py:356
  15.2 3.1 %collective-permute-start.3 = (bf16[320,512]{1,0:T(8,128)(2,1)S(1)}, bf16[320,512]{1,0:T(8,128)(2,1)S(1)}, u32[]{:S(2)}, u32[]{:S(2)}) collective-permute-start(bf16[320,512]{1,0:T(8,128)(2,1)S(1)} %get-tuple-element.26.latent), channel_id=1, source_target_pairs={{15,0},{0,1},{1,2},{2,3},{3,4},{4,5},{5,6},{6,7},{7,8},{8,9},{9,10... | collective-permute-start | bytes 983048 | tf_op jit(solution)/shard_map/ppermute | solution.py:25
  18.3 1.4 %collective-permute-start.4 = (bf16[320,512]{1,0:T(8,128)(2,1)S(1)}, bf16[320,512]{1,0:T(8,128)(2,1)S(1)}, u32[]{:S(2)}, u32[]{:S(2)}) collective-permute-start(bf16[320,512]{1,0:T(8,128)(2,1)S(1)} %get-tuple-element.26.latent), channel_id=1, source_target_pairs={{1,0},{2,1},{3,2},{4,3},{5,4},{6,5},{7,6},{8,7},{9,8},{10,9},{11,1... | collective-permute-start | bytes 983048 | tf_op jit(solution)/shard_map/ppermute | solution.py:25
  19.7 0.0 copy-start.12
  19.7 0.0 copy-start.13
  19.7 0.0 copy-start.14
  19.7 0.0 copy-start.15
  19.7 4.5 %own.1 = (bf16[8,320,512]{2,1,0:T(8,128)(2,1)S(1)}, f32[320,512]{1,0:T(8,128)S(1)}) custom-call(bf16[320,512]{1,0:T(8,128)(2,1)S(1)} %get-tuple-element.26.latent, bf16[1536,512]{1,0:T(8,128)(2,1)S(1)} %copy-done, bf16[8,320,512]{2,1,0:T(8,128)(2,1)S(1)} %get-tuple-element.27.part, bf16[8,320,512]{2,1,0:T(8,128)(2,1)S(1)} %get-tuple-element.28.edge_latent, ...), custom_call_target="tpu_custom_call" | custom-call | flops 838860800 | bytes 10485760 | tf_op jit(solution)/shard_map/own/pallas_call | solution.py:356
  24.2 0.3 collective-permute-done.3.low
  24.5 0.0 collective-permute-done.4.high
  24.6 0.0 copy-start.1
  24.6 0.0 copy-start.2
  24.6 0.0 copy-start.3
  24.6 0.0 copy-start.6
  24.6 10.5 %mesh.1 = (bf16[227,512]{1,0:T(8,128)(2,1)}, bf16[16,384]{1,0:T(8,128)(2,1)S(1)}) custom-call(bf16[320,512]{1,0:T(8,128)(2,1)S(1)} %collective-permute-done.3.low, bf16[320,512]{1,0:T(8,128)(2,1)S(1)} %collective-permute-done.4.high, bf16[320,512]{1,0:T(8,128)(2,1)S(1)} %get-tuple-element.26.latent, bf16[1536,512]{1,0:T(8,128)(2,1)S(1)} %copy-done, ...), custom_call_target="tpu_custom_call" | custom-call | flops 2516582400 | bytes 10485760 | tf_op jit(solution)/shard_map/mesh/pallas_call | solution.py:356
  35.1 2.9 %collective-permute-start.6 = (bf16[16,384]{1,0:T(8,128)(2,1)S(1)}, bf16[16,384]{1,0:T(8,128)(2,1)S(1)}, u32[]{:S(2)}, u32[]{:S(2)}) collective-permute-start(bf16[16,384]{1,0:T(8,128)(2,1)S(1)} %get-tuple-element.34.f_0), channel_id=1, source_target_pairs={{14,0},{15,1},{0,2},{1,3},{2,4},{3,5},{4,6},{5,7},{6,8},{7,9},{8,1... | collective-permute-start | bytes 36872 | tf_op jit(solution)/shard_map/ppermute | solution.py:25
  38.1 0.3 collective-permute-start.7
  38.3 4.2 %collective-permute-start.8 = (bf16[16,384]{1,0:T(8,128)(2,1)S(1)}, bf16[16,384]{1,0:T(8,128)(2,1)S(1)}, u32[]{:S(2)}, u32[]{:S(2)}) collective-permute-start(bf16[16,384]{1,0:T(8,128)(2,1)S(1)} %get-tuple-element.34.f_0), channel_id=1, source_target_pairs={{1,0},{2,1},{3,2},{4,3},{5,4},{6,5},{7,6},{8,7},{9,8},{10,9},{11,1... | collective-permute-start | bytes 36872 | tf_op jit(solution)/shard_map/ppermute | solution.py:25
  42.5 1.9 %collective-permute-start.9 = (bf16[16,384]{1,0:T(8,128)(2,1)S(1)}, bf16[16,384]{1,0:T(8,128)(2,1)S(1)}, u32[]{:S(2)}, u32[]{:S(2)}) collective-permute-start(bf16[16,384]{1,0:T(8,128)(2,1)S(1)} %get-tuple-element.34.f_0), channel_id=1, source_target_pairs={{2,0},{3,1},{4,2},{5,3},{6,4},{7,5},{8,6},{9,7},{10,8},{11,9},{12,... | collective-permute-start | bytes 36872 | tf_op jit(solution)/shard_map/ppermute | solution.py:25
  44.5 0.2 ready.1
  44.7 1.5 %collective-permute-done.9.f_p2 = bf16[16,384]{1,0:T(8,128)(2,1)S(1)} collective-permute-done((bf16[16,384]{1,0:T(8,128)(2,1)S(1)}, bf16[16,384]{1,0:T(8,128)(2,1)S(1)}, u32[]{:S(2)}, u32[]{:S(2)}) %collective-permute-start.9) | collective-permute-done | bytes 12320 | tf_op jit(solution)/shard_map/ppermute | solution.py:25
  46.2 1.3 %ocean.1 = f32[9,8,384]{2,1,0:T(8,128)} custom-call(bf16[16,384]{1,0:T(8,128)(2,1)S(1)} %collective-permute-done.5.f_m3, bf16[16,384]{1,0:T(8,128)(2,1)S(1)} %collective-permute-done.6.f_m2, bf16[16,384]{1,0:T(8,128)(2,1)S(1)} %collective-permute-done.7.f_m1, bf16[16,384]{1,0:T(8,128)(2,1)S(1)} %get-tuple-element.34.f_0, ...), custom_call_target="tpu_custom_call" | custom-call | bytes 4194304 | tf_op jit(solution)/shard_map/ocean/pallas_call | solution.py:356
  (27 shorter events, 0.1 us)
Async XLA Ops:
  0.6 13.5 %copy-start.4 = (bf16[227,512]{1,0:T(8,128)(2,1)S(1)}, bf16[227,512]{1,0:T(8,128)(2,1)}, u32[]{:S(2)}) copy-start(bf16[227,512]{1,0:T(8,128)(2,1)} %w_encode.1) | copy-start | bytes 697348
  0.6 13.5 %copy-start.5 = (bf16[512,227]{0,1:T(8,128)(2,1)S(1)}, bf16[512,227]{0,1:T(8,128)(2,1)}, u32[]{:S(2)}) copy-start(bf16[512,227]{0,1:T(8,128)(2,1)} %param.20) | copy-start | bytes 697348
  0.7 13.4 %copy-start.8 = (s32[1,4,192]{2,1,0:T(4,128)S(1)}, s32[1,4,192]{2,1,0:T(4,128)}, u32[]{:S(2)}) copy-start(s32[1,4,192]{2,1,0:T(4,128)} %param.29) | copy-start | bytes 9220
  0.7 13.4 %copy-start.9 = (s32[512]{0:T(512)S(1)}, s32[512]{0:T(512)}, u32[]{:S(2)}) copy-start(s32[512]{0:T(512)} %param.24) | copy-start | bytes 6148
  2.0 11.6 %collective-permute-start.1 = (bf16[112,384]{1,0:T(8,128)(2,1)S(1)}, bf16[112,384]{1,0:T(8,128)(2,1)S(1)}, u32[]{:S(2)}, u32[]{:S(2)}) collective-permute-start(bf16[112,384]{1,0:T(8,128)(2,1)S(1)} %get-tuple-element.23), channel_id=1, source_target_pairs={{1,0},{2,1},{3,2},{4,3},{5,4},{6,5},{7,6},{8,7},{9,8},{10,9},{11,1... | collective-permute-start | bytes 258056 | tf_op jit(solution)/shard_map/ppermute | solution.py:25
  7.5 6.6 %collective-permute-start.2 = (bf16[112,384]{1,0:T(8,128)(2,1)S(1)}, bf16[112,384]{1,0:T(8,128)(2,1)S(1)}, u32[]{:S(2)}, u32[]{:S(2)}) collective-permute-start(bf16[112,384]{1,0:T(8,128)(2,1)S(1)} %get-tuple-element.24), channel_id=1, source_target_pairs={{15,0},{0,1},{1,2},{2,3},{3,4},{4,5},{5,6},{6,7},{7,8},{8,9},{9,10... | collective-permute-start | bytes 258056 | tf_op jit(solution)/shard_map/ppermute | solution.py:25
  7.5 6.1 %collective-permute-start = (bf16[16,384]{1,0:T(8,128)(2,1)S(1)}, bf16[16,384]{1,0:T(8,128)(2,1)S(1)}, u32[]{:S(2)}, u32[]{:S(2)}) collective-permute-start(bf16[16,384]{1,0:T(8,128)(2,1)S(1)} %get-tuple-element.22.own), channel_id=1, source_target_pairs={{2,0},{3,1},{4,2},{5,3},{6,4},{7,5},{8,6},{9,7},{10,8},{11,9},{12,... | collective-permute-start | bytes 36872 | tf_op jit(solution)/shard_map/ppermute | solution.py:25
  8.6 11.1 %copy-start = (bf16[1536,512]{1,0:T(8,128)(2,1)S(1)}, bf16[1536,512]{1,0:T(8,128)(2,1)}, u32[]{:S(2)}) copy-start(bf16[1536,512]{1,0:T(8,128)(2,1)} %w_in.3) | copy-start | bytes 4718596
  8.6 11.1 %copy-start.7 = (s32[320,8]{0,1:T(8,128)S(1)}, s32[320,8]{0,1:T(8,128)}, u32[]{:S(2)}) copy-start(s32[320,8]{0,1:T(8,128)} %param.23) | copy-start | bytes 30724
  15.2 9.4 %collective-permute-start.3 = (bf16[320,512]{1,0:T(8,128)(2,1)S(1)}, bf16[320,512]{1,0:T(8,128)(2,1)S(1)}, u32[]{:S(2)}, u32[]{:S(2)}) collective-permute-start(bf16[320,512]{1,0:T(8,128)(2,1)S(1)} %get-tuple-element.26.latent), channel_id=1, source_target_pairs={{15,0},{0,1},{1,2},{2,3},{3,4},{4,5},{5,6},{6,7},{7,8},{8,9},{9,10... | collective-permute-start | bytes 983048 | tf_op jit(solution)/shard_map/ppermute | solution.py:25
  18.3 6.3 %collective-permute-start.4 = (bf16[320,512]{1,0:T(8,128)(2,1)S(1)}, bf16[320,512]{1,0:T(8,128)(2,1)S(1)}, u32[]{:S(2)}, u32[]{:S(2)}) collective-permute-start(bf16[320,512]{1,0:T(8,128)(2,1)S(1)} %get-tuple-element.26.latent), channel_id=1, source_target_pairs={{1,0},{2,1},{3,2},{4,3},{5,4},{6,5},{7,6},{8,7},{9,8},{10,9},{11,1... | collective-permute-start | bytes 983048 | tf_op jit(solution)/shard_map/ppermute | solution.py:25
  19.7 4.9 %copy-start.10 = (bf16[1024,512]{1,0:T(8,128)(2,1)S(1)}, bf16[1024,512]{1,0:T(8,128)(2,1)}, u32[]{:S(2)}) copy-start(bf16[1024,512]{1,0:T(8,128)(2,1)} %w_node_in.1) | copy-start | bytes 3145732
  19.7 4.9 %copy-start.11 = (bf16[512,512]{1,0:T(8,128)(2,1)S(1)}, bf16[512,512]{1,0:T(8,128)(2,1)}, u32[]{:S(2)}) copy-start(bf16[512,512]{1,0:T(8,128)(2,1)} %w_out.1) | copy-start | bytes 1572868
  19.7 4.9 %copy-start.12 = (bf16[512,512]{1,0:T(8,128)(2,1)S(1)}, bf16[512,512]{1,0:T(8,128)(2,1)}, u32[]{:S(2)}) copy-start(bf16[512,512]{1,0:T(8,128)(2,1)} %w_node_out.1) | copy-start | bytes 1572868
  19.7 4.9 %copy-start.13 = (bf16[512,227]{0,1:T(8,128)(2,1)S(1)}, bf16[512,227]{0,1:T(8,128)(2,1)}, u32[]{:S(2)}) copy-start(bf16[512,227]{0,1:T(8,128)(2,1)} %param.37) | copy-start | bytes 697348
  19.7 4.9 %copy-start.14 = (f32[512]{0:T(512)S(1)}, f32[512]{0:T(512)}, u32[]{:S(2)}) copy-start(f32[512]{0:T(512)} %param.38) | copy-start | bytes 6148
  19.7 4.8 %copy-start.15 = (f32[512]{0:T(512)S(1)}, f32[512]{0:T(512)}, u32[]{:S(2)}) copy-start(f32[512]{0:T(512)} %param.39) | copy-start | bytes 6148
  24.6 19.9 %copy-start.1 = (f32[8,9,384]{2,0,1:T(8,128)S(1)}, f32[8,9,384]{2,0,1:T(8,128)}, u32[]{:S(2)}) copy-start(f32[8,9,384]{2,0,1:T(8,128)} %param.25) | copy-start | bytes 331780
  24.6 19.9 %copy-start.2 = (f32[8,9,384]{2,0,1:T(8,128)S(1)}, f32[8,9,384]{2,0,1:T(8,128)}, u32[]{:S(2)}) copy-start(f32[8,9,384]{2,0,1:T(8,128)} %param.26) | copy-start | bytes 331780
  24.6 19.9 %copy-start.3 = (f32[8,9,384]{2,0,1:T(8,128)S(1)}, f32[8,9,384]{2,0,1:T(8,128)}, u32[]{:S(2)}) copy-start(f32[8,9,384]{2,0,1:T(8,128)} %param.27) | copy-start | bytes 331780
  24.6 19.9 %copy-start.6 = (s32[9,384]{1,0:T(8,128)S(1)}, s32[9,384]{1,0:T(8,128)}, u32[]{:S(2)}) copy-start(s32[9,384]{1,0:T(8,128)} %mask.1) | copy-start | bytes 41476
  35.1 9.5 %collective-permute-start.5 = (bf16[16,384]{1,0:T(8,128)(2,1)S(1)}, bf16[16,384]{1,0:T(8,128)(2,1)S(1)}, u32[]{:S(2)}, u32[]{:S(2)}) collective-permute-start(bf16[16,384]{1,0:T(8,128)(2,1)S(1)} %get-tuple-element.34.f_0), channel_id=1, source_target_pairs={{13,0},{14,1},{15,2},{0,3},{1,4},{2,5},{3,6},{4,7},{5,8},{6,9},{7,... | collective-permute-start | bytes 36872 | tf_op jit(solution)/shard_map/ppermute | solution.py:25
  35.1 9.5 %collective-permute-start.6 = (bf16[16,384]{1,0:T(8,128)(2,1)S(1)}, bf16[16,384]{1,0:T(8,128)(2,1)S(1)}, u32[]{:S(2)}, u32[]{:S(2)}) collective-permute-start(bf16[16,384]{1,0:T(8,128)(2,1)S(1)} %get-tuple-element.34.f_0), channel_id=1, source_target_pairs={{14,0},{15,1},{0,2},{1,3},{2,4},{3,5},{4,6},{5,7},{6,8},{7,9},{8,1... | collective-permute-start | bytes 36872 | tf_op jit(solution)/shard_map/ppermute | solution.py:25
  38.1 6.6 %collective-permute-start.7 = (bf16[16,384]{1,0:T(8,128)(2,1)S(1)}, bf16[16,384]{1,0:T(8,128)(2,1)S(1)}, u32[]{:S(2)}, u32[]{:S(2)}) collective-permute-start(bf16[16,384]{1,0:T(8,128)(2,1)S(1)} %get-tuple-element.34.f_0), channel_id=1, source_target_pairs={{15,0},{0,1},{1,2},{2,3},{3,4},{4,5},{5,6},{6,7},{7,8},{8,9},{9,10... | collective-permute-start | bytes 36872 | tf_op jit(solution)/shard_map/ppermute | solution.py:25
  38.3 6.3 %collective-permute-start.8 = (bf16[16,384]{1,0:T(8,128)(2,1)S(1)}, bf16[16,384]{1,0:T(8,128)(2,1)S(1)}, u32[]{:S(2)}, u32[]{:S(2)}) collective-permute-start(bf16[16,384]{1,0:T(8,128)(2,1)S(1)} %get-tuple-element.34.f_0), channel_id=1, source_target_pairs={{1,0},{2,1},{3,2},{4,3},{5,4},{6,5},{7,6},{8,7},{9,8},{10,9},{11,1... | collective-permute-start | bytes 36872 | tf_op jit(solution)/shard_map/ppermute | solution.py:25
  42.5 3.7 %collective-permute-start.9 = (bf16[16,384]{1,0:T(8,128)(2,1)S(1)}, bf16[16,384]{1,0:T(8,128)(2,1)S(1)}, u32[]{:S(2)}, u32[]{:S(2)}) collective-permute-start(bf16[16,384]{1,0:T(8,128)(2,1)S(1)} %get-tuple-element.34.f_0), channel_id=1, source_target_pairs={{2,0},{3,1},{4,2},{5,3},{6,4},{7,5},{8,6},{9,7},{10,8},{11,9},{12,... | collective-permute-start | bytes 36872 | tf_op jit(solution)/shard_map/ppermute | solution.py:25

commit v3 on v2

--- a/solution.py
+++ b/solution.py
@@ -108,11 +108,10 @@
 
 
 def embed_kernel(
-    geometry_in, w_geometry_in, w_in_in, atmosphere_in, w_encode_in, grid_row_in, mesh_state_in,
-    latent_out, part_out, plain_out,
-    turned, geometry, w_geometry, weights, atmosphere, w_encode, grid_row, mesh_state, sems,
+    geometry_in, w_geometry_in, atmosphere_in, w_encode_in, grid_row_in, mesh_state_in,
+    latent_out, plain_out,
+    turned, geometry, w_geometry, atmosphere, w_encode, grid_row, mesh_state, sems,
 ):
-    first = w_in_in.at[pl.ds(0, weights.shape[0])]
     copies = started(
         (
             (geometry_in, geometry),
@@ -121,7 +120,6 @@
             (atmosphere_in, atmosphere),
             (w_encode_in, w_encode),
             (mesh_state_in, mesh_state),
-            (first, weights),
         ),
         sems,
     )
@@ -144,9 +142,7 @@
     w_geo = jnp.concatenate([w_geometry[...].astype(F32), jnp.zeros((4, features), F32)], axis=0).astype(BF16)
     for k in range(K):
         points = turned[pl.ds(k, nodes, stride=K), :8].astype(BF16)
-        value = silu(dot(points, w_geo)).astype(BF16)
-        latent_out[k] = value
-        part_out[k] = dot(value, weights[...]).astype(BF16)
+        latent_out[k] = silu(dot(points, w_geo)).astype(BF16)
 
 
 def rolled_points(points, starts):
@@ -200,20 +196,23 @@
     return jnp.sum(jnp.where(lane == k, listed, 0.0), axis=1, keepdims=True).astype(jnp.int32)
 
 
-def own_kernel(latent, w_in, part, edge_latent, neighbours, pre_out, base_out, sender):
+def own_kernel(latent, w_in, edge_latent, neighbours, w_node_in, pre_out, base_out, node_out, sender):
     nodes, features = latent.shape
     value = latent[...]
     sender[...] = dot(value, w_in[features : 2 * features]).astype(BF16)
     receiver = dot(value, w_in[2 * features :])
+    node_out[...] = dot(value, w_node_in[:features])
     listed = listed_slots(neighbours)
 
     def step(k, base):
         at = slot_senders(listed, k)
+        edge = edge_latent[k]
         match = one_hot(iota((nodes, nodes), 1) + nodes == at)
-        pre_out[k] = (part[k].astype(F32) + receiver + dot(match, sender[...])).astype(BF16)
-        return base + jnp.where(at < 3 * nodes, edge_latent[k].astype(F32), 0.0)
-
-    base_out[...] = lax.fori_loop(0, K, step, jnp.zeros((nodes, features), F32))
+        joined = dot(edge, w_in[:features]) + dot(match, sender[...])
+        pre_out[k] = (joined + receiver).astype(BF16)
+        return base + jnp.where(at < 3 * nodes, edge.astype(F32), 0.0)
+
+    base_out[...] = lax.fori_loop(0, K, step, jnp.zeros((nodes, features), F32), unroll=True)
 
 
 def normal(values):
@@ -224,8 +223,8 @@
 
 
 def mesh_kernel(
-    low, high, latent, w_in, w_out, pre, base, neighbours, w_node_in, w_node_out, w_decode,
-    gain_edge, gain_node, grid_row, atmosphere, surface, placed, state_out, flux_out, sender, total,
+    low, high, latent, w_in, w_out, pre, base, node_part, neighbours, w_node_in, w_node_out, w_decode,
+    gain_edge, gain_node, grid_row, atmosphere, placed, node_out, flux_out, sender, total,
 ):
     nodes, features = latent.shape
     w_sender = w_in[features : 2 * features]
@@ -243,29 +242,38 @@
         total[...] += centred * jnp.where(at < 3 * nodes, scale, 0.0)
         return carry
 
-    lax.fori_loop(0, K, step, 0)
+    lax.fori_loop(0, K, step, 0, unroll=True)
     aggregate = (base[...] + total[...] * gain_edge[...]).astype(BF16)
-    own = latent[...]
-    hidden = silu(dot(own, w_node_in[:features]) + dot(aggregate, w_node_in[features:])).astype(BF16)
+    hidden = silu(node_part[...] + dot(aggregate, w_node_in[features:])).astype(BF16)
     centred, scale = normal(dot(hidden, w_node_out[...]))
-    node_new = (own.astype(F32) + centred * scale * gain_node[...]).astype(BF16)
-    change = dot_nt(w_decode[...], node_new)
-    change_high = change.astype(BF16)
-    change_low = (change - change_high.astype(F32)).astype(BF16)
-    member = members(nodes, grid_row[...])
-    state = atmosphere[...].astype(F32)
-    state = jnp.where(iota(state.shape, 0) == 0, surface[...].astype(BF16).astype(F32), state)
-    state = state + dot(change_high, member) + dot(change_low, member)
-    state_out[...] = state.astype(BF16)
-    n_points = state.shape[1]
-    flux = jnp.broadcast_to(state[1:2], (8, n_points)).astype(BF16)
+    node_new = (latent[...].astype(F32) + centred * scale * gain_node[...]).astype(BF16)
+    node_out[...] = node_new
+    flux = two_parts(dot_nt(w_decode[0:16], node_new)[1:2])
+    flux = dot(flux, members(nodes, grid_row[...]))
+    flux = atmosphere[0:16].astype(F32)[1:2] + flux[0:1] + flux[1:2]
+    n_points = flux.shape[1]
     match = one_hot(iota((n_points, placed.shape[1]), 0) == placed[...])
-    spread = dot(flux, match)
+    spread = dot(jnp.broadcast_to(flux, (8, n_points)).astype(BF16), match)
     rows = placed.shape[1] // W
     out = jnp.zeros((8, rows), F32)
     for o in range(W):
         out = jnp.where(iota((8, rows), 0) == o, spread[:, o * rows : (o + 1) * rows], out)
     flux_out[...] = jnp.concatenate([out, jnp.zeros((8, rows), F32)], axis=0).astype(BF16)
+
+
+def two_parts(row):
+    high = row.astype(BF16).astype(F32)
+    return jnp.concatenate([high, row - high, jnp.zeros((6, row.shape[1]), F32)], axis=0).astype(BF16)
+
+
+def decode_kernel(node_new, w_decode, grid_row, atmosphere, surface, state_out):
+    change = dot_nt(w_decode[...], node_new[...])
+    change_high = change.astype(BF16)
+    change_low = (change - change_high.astype(F32)).astype(BF16)
+    member = members(node_new.shape[0], grid_row[...])
+    state = atmosphere[...].astype(F32)
+    state = jnp.where(iota(state.shape, 0) == 0, surface[...].astype(BF16).astype(F32), state)
+    state_out[...] = (state + dot(change_high, member) + dot(change_low, member)).astype(BF16)
 
 
 def ready_kernel(heat, east, north, mask, low, high, field_out, wet_out, px_out, qx_out, py_out, qy_out, mix_out):
@@ -303,7 +311,7 @@
         qy_out[c] = opened * (face - COEFF_H)
 
 
-def ocean_kernel(f_m3, f_m2, f_m1, f_0, f_p1, f_p2, field_in, wet, px, qx, py, qy, mix, out):
+def ocean_kernel(f_p1, f_p2, f_m3, f_m2, f_m1, f_0, field_in, wet, px, qx, py, qy, mix, out):
     count, levels, rows = field_in.shape
     columns = count - 2 * EDGE
     triples = columns // 3
@@ -396,6 +404,7 @@
     atmosphere_t = atmosphere.T
     slots = neighbours.T
     grid_row = grid_node.reshape(1, n_points)
+    decode_t = w_decode.T
     ends = (3 * levels * EDGE + 16, rows)
     few = (16, rows)
     own_ocean = (columns, levels, rows)
@@ -417,21 +426,20 @@
     far = shifted(blocks, -2)
     above = shifted(low, -1)
     below = shifted(high, 1)
-    edge_latent, part, plain = call(
+    edge_latent, plain = call(
         embed_kernel,
-        [((K, nodes, features), BF16), ((K, nodes, features), BF16), ((nodes, features), F32)],
-        [edge_geometry, w_geometry, w_edge_in, atmosphere_t, w_encode, grid_row, mesh_state],
+        [((K, nodes, features), BF16), ((nodes, features), F32)],
+        [edge_geometry, w_geometry, atmosphere_t, w_encode, grid_row, mesh_state],
         spec=HBM,
         scratch=[
             pltpu.VMEM((K * nodes, 128), F32),
             pltpu.VMEM(edge_geometry.shape, BF16),
             pltpu.VMEM(w_geometry.shape, BF16),
-            pltpu.VMEM((features, features), BF16),
             pltpu.VMEM((channels, n_points), BF16),
             pltpu.VMEM(w_encode.shape, BF16),
             pltpu.VMEM((1, n_points), jnp.int32),
             pltpu.VMEM((nodes, features), BF16),
-            pltpu.SemaphoreType.DMA((7,)),
+            pltpu.SemaphoreType.DMA((6,)),
         ],
         flops=2 * K * nodes * features * features,
         bytes_accessed=8 << 20,
@@ -445,12 +453,12 @@
     )
     latent_low = shifted(latent, 1)
     latent_high = shifted(latent, -1)
-    pre, base = call(
+    pre, base, node_part = call(
         own_kernel,
-        [((K, nodes, features), BF16), ((nodes, features), F32)],
-        [latent, w_edge_in, part, edge_latent, slots],
+        [((K, nodes, features), BF16), ((nodes, features), F32), ((nodes, features), F32)],
+        [latent, w_edge_in, edge_latent, slots, w_node_in],
         scratch=[pltpu.VMEM((nodes, features), BF16)],
-        flops=2 * K * nodes * nodes * features,
+        flops=2 * K * nodes * (nodes + features) * features,
         bytes_accessed=10 << 20,
         name="own",
     )
@@ -462,20 +470,29 @@
         bytes_accessed=4 << 20,
         name="ready",
     )
-    state, flux = call(
+    node_new, flux = call(
         mesh_kernel,
-        [((channels, n_points), BF16), (few, BF16)],
+        [((nodes, features), BF16), (few, BF16)],
         [
-            latent_low, latent_high, latent, w_edge_in, w_edge_out, pre, base, slots,
-            w_node_in, w_node_out, w_decode.T, gain_edge.reshape(1, features),
-            gain_node.reshape(1, features), grid_row, atmosphere_t, surface, placed,
+            latent_low, latent_high, latent, w_edge_in, w_edge_out, pre, base, node_part, slots,
+            w_node_in, w_node_out, decode_t, gain_edge.reshape(1, features),
+            gain_node.reshape(1, features), grid_row, atmosphere_t, placed,
         ],
         scratch=[pltpu.VMEM((2 * nodes, features), BF16), pltpu.VMEM((nodes, features), F32)],
         flops=2 * K * nodes * 3 * nodes * features,
         bytes_accessed=10 << 20,
         name="mesh",
     )
-    arrived = [flux if d == 0 else shifted(flux, d) for d in (3, 2, 1, 0, -1, -2)]
+    sent = {d: shifted(flux, d) for d in (1, 2, 3, -1, -2)}
+    sent[0] = flux
+    arrived = [sent[d] for d in (-1, -2, 3, 2, 1, 0)]
+    (state,) = call(
+        decode_kernel,
+        [((channels, n_points), BF16)],
+        [node_new, decode_t, grid_row, atmosphere_t, surface],
+        flops=6 * nodes * channels * n_points,
+        name="decode",
+    )
     (ocean_new,) = call(
         ocean_kernel,
         [(own_ocean, F32)],

time: 47.7 us -> 45.1 us (0.945)
  waiting for transfers between devices: 2.32 us -> 7.86 us
  Pallas kernels: 23.9 us -> 18.7 us
  starting transfers between devices: 20.4 us -> 17.4 us
    ppermute x10, waiting for transfers between devices: 2.32 us -> 7.86 us  [shifted(): lax.ppermute(block, AXES, [((i - distance) % count, i) for i in range(cou...]
    pallas_call x7 -> x8, Pallas kernels: 23.9 us -> 18.7 us  [call(): pl.pallas_call(kernel, out_shape=[jax.ShapeDtypeStruct(s, t) for s, t in...]
    ppermute x10, starting transfers between devices: 20.4 us -> 17.4 us  [shifted(): lax.ppermute(block, AXES, [((i - distance) % count, i) for i in range(cou...]
  transfers between devices with their start and end apart: 10 -> 10, of which waited for: 3 -> 6; matrix products, arithmetic and copies ran while one was open for 0% -> 0% of each run, Pallas kernels for 20% -> 18%
where the time goes in v3:
time: 45.1 us; the launch traced here: 44.9 us
  Pallas kernels  18.7 us (41%)
  starting transfers between devices  17.4 us (39%)
  waiting for transfers between devices  7.86 us (17%)
  between operations  0.86 us (2%)
    pallas_call x8, Pallas kernels, call(): pl.pallas_call(kernel, out_shape=[jax.ShapeDtypeStruct(s, t) for s, t in...  18.7 us
    ppermute x10, starting transfers between devices, shifted(): lax.ppermute(block, AXES, [((i - distance) % count, i) for i in range(cou...  17.4 us
    ppermute x10, waiting for transfers between devices, shifted(): lax.ppermute(block, AXES, [((i - distance) % count, i) for i in range(cou...  7.86 us
  transfers between devices with their start and end apart: 10, of which 6 were waited for; matrix products, arithmetic and copies ran while one was open for 0% of the time, Pallas kernels for 18%

profile of v3, /device:TPU:0, one launch (start us, length us, event | category | flops | bytes accessed | tf_op | source)
XLA Modules:
  0.0 44.9 jit_solution(15251392465077820592)
XLA Ops:
  0.6 0.0 copy-start
  0.6 0.0 copy-start.4
  0.7 0.0 copy-start.7
  0.7 1.3 %pack.1 = (bf16[112,384]{1,0:T(8,128)(2,1)S(1)}, bf16[112,384]{1,0:T(8,128)(2,1)S(1)}, bf16[16,384]{1,0:T(8,128)(2,1)S(1)}) custom-call(s32[1,4]{1,0:T(1,128)} %counts_in.1, f32[9,8,384]{2,1,0:T(8,128)} %bitcast.16, f32[9,8,384]{2,1,0:T(8,128)} %bitcast.18, f32[9,8,384]{2,1,0:T(8,128)} %bitcast.20, s32[9,384]{1,0:T(8,128)} %mask.1), custom_call_target="tpu_custom_call" | custom-call | bytes 1048576 | tf_op jit(solution)/shard_map/pack/pallas_call | solution.py:364
  2.0 5.5 %collective-permute-start.1 = (bf16[112,384]{1,0:T(8,128)(2,1)S(1)}, bf16[112,384]{1,0:T(8,128)(2,1)S(1)}, u32[]{:S(2)}, u32[]{:S(2)}) collective-permute-start(bf16[112,384]{1,0:T(8,128)(2,1)S(1)} %get-tuple-element.23), channel_id=1, source_target_pairs={{1,0},{2,1},{3,2},{4,3},{5,4},{6,5},{7,6},{8,7},{9,8},{10,9},{11,1... | collective-permute-start | bytes 258056 | tf_op jit(solution)/shard_map/ppermute | solution.py:25
  7.5 1.1 %collective-permute-start = (bf16[16,384]{1,0:T(8,128)(2,1)S(1)}, bf16[16,384]{1,0:T(8,128)(2,1)S(1)}, u32[]{:S(2)}, u32[]{:S(2)}) collective-permute-start(bf16[16,384]{1,0:T(8,128)(2,1)S(1)} %get-tuple-element.22.own), channel_id=1, source_target_pairs={{2,0},{3,1},{4,2},{5,3},{6,4},{7,5},{8,6},{9,7},{10,8},{11,9},{12,... | collective-permute-start | bytes 36872 | tf_op jit(solution)/shard_map/ppermute | solution.py:25
  8.6 0.0 copy-start.9
  8.6 0.0 copy-start.10
  8.6 0.0 copy-start.13
  8.6 3.0 %embed.1 = (bf16[8,320,512]{2,1,0:T(8,128)(2,1)S(1)}, f32[320,512]{1,0:T(8,128)S(1)}) custom-call(bf16[4,2560]{1,0:T(4,128)(2,1)} %geometry_in.1, bf16[4,512]{1,0:T(4,128)(2,1)} %w_geometry_in.1, bf16[227,512]{1,0:T(8,128)(2,1)} %bitcast.12, bf16[227,512]{1,0:T(8,128)(2,1)} %w_encode.1, s32[1,512]{1,0:T(1,128)} %bitcast.24, bf16[320,512]{1,0:T(8,128)(2,1)} %mesh_state_in.1), custom_call_target="tpu_custom_call" | custom-call | flops 1342177280 | bytes 8388608 | tf_op jit(solution)/shard_map/embed/pallas_call | solution.py:364
  11.6 0.0 collective-permute-done.1.above.high
  11.6 2.5 %collective-permute-done.2.below.low = bf16[112,384]{1,0:T(8,128)(2,1)S(1)} collective-permute-done((bf16[112,384]{1,0:T(8,128)(2,1)S(1)}, bf16[112,384]{1,0:T(8,128)(2,1)S(1)}, u32[]{:S(2)}, u32[]{:S(2)}) %collective-permute-start.2) | collective-permute-done | bytes 86048 | tf_op jit(solution)/shard_map/ppermute | solution.py:25
  14.1 1.0 %latents.1 = (bf16[320,512]{1,0:T(8,128)(2,1)S(1)}, f32[1,512]{1,0:T(1,128)S(1)}, s32[1,1536]{1,0:T(1,128)S(1)}) custom-call(bf16[16,384]{1,0:T(8,128)(2,1)S(1)} %collective-permute-done.far, bf16[112,384]{1,0:T(8,128)(2,1)S(1)} %collective-permute-done.1.above.high, bf16[16,384]{1,0:T(8,128)(2,1)S(1)} %get-tuple-element.22.own, ...), custom_call_target="tpu_custom_call" | custom-call | bytes 1048576 | tf_op jit(solution)/shard_map/latents/pallas_call | solution.py:364
  15.2 1.1 %collective-permute-start.3 = (bf16[320,512]{1,0:T(8,128)(2,1)S(1)}, bf16[320,512]{1,0:T(8,128)(2,1)S(1)}, u32[]{:S(2)}, u32[]{:S(2)}) collective-permute-start(bf16[320,512]{1,0:T(8,128)(2,1)S(1)} %get-tuple-element.26.latent), channel_id=1, source_target_pairs={{15,0},{0,1},{1,2},{2,3},{3,4},{4,5},{5,6},{6,7},{7,8},{8,9},{9,10... | collective-permute-start | bytes 983048 | tf_op jit(solution)/shard_map/ppermute | solution.py:25
  16.3 3.4 %collective-permute-start.4 = (bf16[320,512]{1,0:T(8,128)(2,1)S(1)}, bf16[320,512]{1,0:T(8,128)(2,1)S(1)}, u32[]{:S(2)}, u32[]{:S(2)}) collective-permute-start(bf16[320,512]{1,0:T(8,128)(2,1)S(1)} %get-tuple-element.26.latent), channel_id=1, source_target_pairs={{1,0},{2,1},{3,2},{4,3},{5,4},{6,5},{7,6},{8,7},{9,8},{10,9},{11,1... | collective-permute-start | bytes 983048 | tf_op jit(solution)/shard_map/ppermute | solution.py:25
  19.7 0.2 ready.1
  19.9 0.0 copy-start.5
  19.9 0.0 copy-start.11
  19.9 0.0 copy-start.12
  19.9 0.0 copy-start.14
  19.9 0.0 copy-start.15
  19.9 3.6 %own.1 = (bf16[8,320,512]{2,1,0:T(8,128)(2,1)S(1)}, f32[320,512]{1,0:T(8,128)S(1)}, f32[320,512]{1,0:T(8,128)S(1)}) custom-call(bf16[320,512]{1,0:T(8,128)(2,1)S(1)} %get-tuple-element.26.latent, bf16[1536,512]{1,0:T(8,128)(2,1)S(1)} %copy-done.9, bf16[8,320,512]{2,1,0:T(8,128)(2,1)S(1)} %get-tuple-element.27.edge_latent, s32[8,320]{1,0:T(8,128)S(1)} %bitcast.29, ...), custom_call_target="tpu_custom_call" | custom-call | flops 2181038080 | bytes 10485760 | tf_op jit(solution)/shard_map/own/pallas_call | solution.py:364
  23.6 1.0 %collective-permute-done.3.low = bf16[320,512]{1,0:T(8,128)(2,1)S(1)} collective-permute-done((bf16[320,512]{1,0:T(8,128)(2,1)S(1)}, bf16[320,512]{1,0:T(8,128)(2,1)S(1)}, u32[]{:S(2)}, u32[]{:S(2)}) %collective-permute-start.3) | collective-permute-done | bytes 327712 | tf_op jit(solution)/shard_map/ppermute | solution.py:25
  24.6 6.9 %mesh.1 = (bf16[320,512]{1,0:T(8,128)(2,1)S(1)}, bf16[16,384]{1,0:T(8,128)(2,1)S(1)}) custom-call(bf16[320,512]{1,0:T(8,128)(2,1)S(1)} %collective-permute-done.3.low, bf16[320,512]{1,0:T(8,128)(2,1)S(1)} %collective-permute-done.4.high, bf16[320,512]{1,0:T(8,128)(2,1)S(1)} %get-tuple-element.26.latent, bf16[1536,512]{1,0:T(8,128)(2,1)S(1)} %copy-done.9, ...), custom_call_target="tpu_custom_call" | custom-call | flops 2516582400 | bytes 10485760 | tf_op jit(solution)/shard_map/mesh/pallas_call | solution.py:364
  31.4 4.3 %collective-permute-start.5 = (bf16[16,384]{1,0:T(8,128)(2,1)S(1)}, bf16[16,384]{1,0:T(8,128)(2,1)S(1)}, u32[]{:S(2)}, u32[]{:S(2)}) collective-permute-start(bf16[16,384]{1,0:T(8,128)(2,1)S(1)} %get-tuple-element.34.f_0), channel_id=1, source_target_pairs={{1,0},{2,1},{3,2},{4,3},{5,4},{6,5},{7,6},{8,7},{9,8},{10,9},{11,1... | collective-permute-start | bytes 36872 | tf_op jit(solution)/shard_map/ppermute | solution.py:25
  35.8 2.0 %collective-permute-start.8 = (bf16[16,384]{1,0:T(8,128)(2,1)S(1)}, bf16[16,384]{1,0:T(8,128)(2,1)S(1)}, u32[]{:S(2)}, u32[]{:S(2)}) collective-permute-start(bf16[16,384]{1,0:T(8,128)(2,1)S(1)} %get-tuple-element.34.f_0), channel_id=1, source_target_pairs={{14,0},{15,1},{0,2},{1,3},{2,4},{3,5},{4,6},{5,7},{6,8},{7,9},{8,1... | collective-permute-start | bytes 36872 | tf_op jit(solution)/shard_map/ppermute | solution.py:25
  37.8 1.4 %decode.1 = bf16[227,512]{1,0:T(8,128)(2,1)} custom-call(bf16[320,512]{1,0:T(8,128)(2,1)S(1)} %get-tuple-element.32.node_new, bf16[227,512]{1,0:T(8,128)(2,1)S(1)} %bitcast.23, s32[1,512]{1,0:T(1,128)S(1)} %bitcast.27, bf16[227,512]{1,0:T(8,128)(2,1)S(1)} %bitcast.15, f32[1,512]{1,0:T(1,128)S(1)} %get-tuple-element.33.surface), custom_call_target="tpu_custom_call" | custom-call | flops 223150080 | bytes 1048576 | tf_op jit(solution)/shard_map/decode/pallas_call | solution.py:364
  39.2 0.3 collective-permute-done.6.f_p2
  39.4 1.2 %collective-permute-done.7.f_m3 = bf16[16,384]{1,0:T(8,128)(2,1)S(1)} collective-permute-done((bf16[16,384]{1,0:T(8,128)(2,1)S(1)}, bf16[16,384]{1,0:T(8,128)(2,1)S(1)}, u32[]{:S(2)}, u32[]{:S(2)}) %collective-permute-start.7) | collective-permute-done | bytes 12320 | tf_op jit(solution)/shard_map/ppermute | solution.py:25
  40.7 1.6 %collective-permute-done.8.f_m2 = bf16[16,384]{1,0:T(8,128)(2,1)S(1)} collective-permute-done((bf16[16,384]{1,0:T(8,128)(2,1)S(1)}, bf16[16,384]{1,0:T(8,128)(2,1)S(1)}, u32[]{:S(2)}, u32[]{:S(2)}) %collective-permute-start.8) | collective-permute-done | bytes 12320 | tf_op jit(solution)/shard_map/ppermute | solution.py:25
  42.3 1.3 %collective-permute-done.9.f_m1 = bf16[16,384]{1,0:T(8,128)(2,1)S(1)} collective-permute-done((bf16[16,384]{1,0:T(8,128)(2,1)S(1)}, bf16[16,384]{1,0:T(8,128)(2,1)S(1)}, u32[]{:S(2)}, u32[]{:S(2)}) %collective-permute-start.9) | collective-permute-done | bytes 12320 | tf_op jit(solution)/shard_map/ppermute | solution.py:25
  43.6 1.3 %ocean.1 = f32[9,8,384]{2,1,0:T(8,128)} custom-call(bf16[16,384]{1,0:T(8,128)(2,1)S(1)} %collective-permute-done.5.f_p1, bf16[16,384]{1,0:T(8,128)(2,1)S(1)} %collective-permute-done.6.f_p2, bf16[16,384]{1,0:T(8,128)(2,1)S(1)} %collective-permute-done.7.f_m3, bf16[16,384]{1,0:T(8,128)(2,1)S(1)} %collective-permute-done.8.f_m2, ...), custom_call_target="tpu_custom_call" | custom-call | bytes 4194304 | tf_op jit(solution)/shard_map/ocean/pallas_call | solution.py:364
  (28 shorter events, 0.1 us)
Async XLA Ops:
  0.6 13.5 %copy-start = (bf16[512,227]{0,1:T(8,128)(2,1)S(1)}, bf16[512,227]{0,1:T(8,128)(2,1)}, u32[]{:S(2)}) copy-start(bf16[512,227]{0,1:T(8,128)(2,1)} %param.20) | copy-start | bytes 697348
  0.6 13.5 %copy-start.4 = (bf16[227,512]{1,0:T(8,128)(2,1)S(1)}, bf16[227,512]{1,0:T(8,128)(2,1)}, u32[]{:S(2)}) copy-start(bf16[227,512]{1,0:T(8,128)(2,1)} %w_encode.1) | copy-start | bytes 697348
  0.7 13.4 %copy-start.7 = (s32[512]{0:T(512)S(1)}, s32[512]{0:T(512)}, u32[]{:S(2)}) copy-start(s32[512]{0:T(512)} %param.24) | copy-start | bytes 6148
  0.7 13.4 %copy-start.8 = (s32[1,4,192]{2,1,0:T(4,128)S(1)}, s32[1,4,192]{2,1,0:T(4,128)}, u32[]{:S(2)}) copy-start(s32[1,4,192]{2,1,0:T(4,128)} %param.29) | copy-start | bytes 9220
  2.0 9.6 %collective-permute-start.1 = (bf16[112,384]{1,0:T(8,128)(2,1)S(1)}, bf16[112,384]{1,0:T(8,128)(2,1)S(1)}, u32[]{:S(2)}, u32[]{:S(2)}) collective-permute-start(bf16[112,384]{1,0:T(8,128)(2,1)S(1)} %get-tuple-element.23), channel_id=1, source_target_pairs={{1,0},{2,1},{3,2},{4,3},{5,4},{6,5},{7,6},{8,7},{9,8},{10,9},{11,1... | collective-permute-start | bytes 258056 | tf_op jit(solution)/shard_map/ppermute | solution.py:25
  7.5 6.6 %collective-permute-start.2 = (bf16[112,384]{1,0:T(8,128)(2,1)S(1)}, bf16[112,384]{1,0:T(8,128)(2,1)S(1)}, u32[]{:S(2)}, u32[]{:S(2)}) collective-permute-start(bf16[112,384]{1,0:T(8,128)(2,1)S(1)} %get-tuple-element.24), channel_id=1, source_target_pairs={{15,0},{0,1},{1,2},{2,3},{3,4},{4,5},{5,6},{6,7},{7,8},{8,9},{9,10... | collective-permute-start | bytes 258056 | tf_op jit(solution)/shard_map/ppermute | solution.py:25
  7.5 4.1 %collective-permute-start = (bf16[16,384]{1,0:T(8,128)(2,1)S(1)}, bf16[16,384]{1,0:T(8,128)(2,1)S(1)}, u32[]{:S(2)}, u32[]{:S(2)}) collective-permute-start(bf16[16,384]{1,0:T(8,128)(2,1)S(1)} %get-tuple-element.22.own), channel_id=1, source_target_pairs={{2,0},{3,1},{4,2},{5,3},{6,4},{7,5},{8,6},{9,7},{10,8},{11,9},{12,... | collective-permute-start | bytes 36872 | tf_op jit(solution)/shard_map/ppermute | solution.py:25
  8.6 11.1 %copy-start.1 = (f32[8,9,384]{2,0,1:T(8,128)S(1)}, f32[8,9,384]{2,0,1:T(8,128)}, u32[]{:S(2)}) copy-start(f32[8,9,384]{2,0,1:T(8,128)} %param.25) | copy-start | bytes 331780
  8.6 11.1 %copy-start.2 = (f32[8,9,384]{2,0,1:T(8,128)S(1)}, f32[8,9,384]{2,0,1:T(8,128)}, u32[]{:S(2)}) copy-start(f32[8,9,384]{2,0,1:T(8,128)} %param.26) | copy-start | bytes 331780
  8.6 11.1 %copy-start.3 = (f32[8,9,384]{2,0,1:T(8,128)S(1)}, f32[8,9,384]{2,0,1:T(8,128)}, u32[]{:S(2)}) copy-start(f32[8,9,384]{2,0,1:T(8,128)} %param.27) | copy-start | bytes 331780
  8.6 11.1 %copy-start.6 = (s32[9,384]{1,0:T(8,128)S(1)}, s32[9,384]{1,0:T(8,128)}, u32[]{:S(2)}) copy-start(s32[9,384]{1,0:T(8,128)} %mask.1) | copy-start | bytes 41476
  8.6 11.3 %copy-start.9 = (bf16[1536,512]{1,0:T(8,128)(2,1)S(1)}, bf16[1536,512]{1,0:T(8,128)(2,1)}, u32[]{:S(2)}) copy-start(bf16[1536,512]{1,0:T(8,128)(2,1)} %w_in.3) | copy-start | bytes 4718596
  8.6 11.3 %copy-start.10 = (bf16[1024,512]{1,0:T(8,128)(2,1)S(1)}, bf16[1024,512]{1,0:T(8,128)(2,1)}, u32[]{:S(2)}) copy-start(bf16[1024,512]{1,0:T(8,128)(2,1)} %w_node_in.3) | copy-start | bytes 3145732
  8.6 11.3 %copy-start.13 = (s32[320,8]{0,1:T(8,128)S(1)}, s32[320,8]{0,1:T(8,128)}, u32[]{:S(2)}) copy-start(s32[320,8]{0,1:T(8,128)} %param.23) | copy-start | bytes 30724
  15.2 9.4 %collective-permute-start.3 = (bf16[320,512]{1,0:T(8,128)(2,1)S(1)}, bf16[320,512]{1,0:T(8,128)(2,1)S(1)}, u32[]{:S(2)}, u32[]{:S(2)}) collective-permute-start(bf16[320,512]{1,0:T(8,128)(2,1)S(1)} %get-tuple-element.26.latent), channel_id=1, source_target_pairs={{15,0},{0,1},{1,2},{2,3},{3,4},{4,5},{5,6},{6,7},{7,8},{8,9},{9,10... | collective-permute-start | bytes 983048 | tf_op jit(solution)/shard_map/ppermute | solution.py:25
  16.3 8.3 %collective-permute-start.4 = (bf16[320,512]{1,0:T(8,128)(2,1)S(1)}, bf16[320,512]{1,0:T(8,128)(2,1)S(1)}, u32[]{:S(2)}, u32[]{:S(2)}) collective-permute-start(bf16[320,512]{1,0:T(8,128)(2,1)S(1)} %get-tuple-element.26.latent), channel_id=1, source_target_pairs={{1,0},{2,1},{3,2},{4,3},{5,4},{6,5},{7,6},{8,7},{9,8},{10,9},{11,1... | collective-permute-start | bytes 983048 | tf_op jit(solution)/shard_map/ppermute | solution.py:25
  19.9 4.6 %copy-start.5 = (bf16[512,227]{0,1:T(8,128)(2,1)S(1)}, bf16[512,227]{0,1:T(8,128)(2,1)}, u32[]{:S(2)}) copy-start(bf16[512,227]{0,1:T(8,128)(2,1)} %param.37) | copy-start | bytes 697348
  19.9 4.6 %copy-start.11 = (bf16[512,512]{1,0:T(8,128)(2,1)S(1)}, bf16[512,512]{1,0:T(8,128)(2,1)}, u32[]{:S(2)}) copy-start(bf16[512,512]{1,0:T(8,128)(2,1)} %w_out.1) | copy-start | bytes 1572868
  19.9 4.6 %copy-start.12 = (bf16[512,512]{1,0:T(8,128)(2,1)S(1)}, bf16[512,512]{1,0:T(8,128)(2,1)}, u32[]{:S(2)}) copy-start(bf16[512,512]{1,0:T(8,128)(2,1)} %w_node_out.1) | copy-start | bytes 1572868
  19.9 4.6 %copy-start.14 = (f32[512]{0:T(512)S(1)}, f32[512]{0:T(512)}, u32[]{:S(2)}) copy-start(f32[512]{0:T(512)} %param.38) | copy-start | bytes 6148
  19.9 4.6 %copy-start.15 = (f32[512]{0:T(512)S(1)}, f32[512]{0:T(512)}, u32[]{:S(2)}) copy-start(f32[512]{0:T(512)} %param.39) | copy-start | bytes 6148
  31.4 7.7 %collective-permute-start.5 = (bf16[16,384]{1,0:T(8,128)(2,1)S(1)}, bf16[16,384]{1,0:T(8,128)(2,1)S(1)}, u32[]{:S(2)}, u32[]{:S(2)}) collective-permute-start(bf16[16,384]{1,0:T(8,128)(2,1)S(1)} %get-tuple-element.34.f_0), channel_id=1, source_target_pairs={{1,0},{2,1},{3,2},{4,3},{5,4},{6,5},{7,6},{8,7},{9,8},{10,9},{11,1... | collective-permute-start | bytes 36872 | tf_op jit(solution)/shard_map/ppermute | solution.py:25
  35.8 3.7 %collective-permute-start.6 = (bf16[16,384]{1,0:T(8,128)(2,1)S(1)}, bf16[16,384]{1,0:T(8,128)(2,1)S(1)}, u32[]{:S(2)}, u32[]{:S(2)}) collective-permute-start(bf16[16,384]{1,0:T(8,128)(2,1)S(1)} %get-tuple-element.34.f_0), channel_id=1, source_target_pairs={{2,0},{3,1},{4,2},{5,3},{6,4},{7,5},{8,6},{9,7},{10,8},{11,9},{12,... | collective-permute-start | bytes 36872 | tf_op jit(solution)/shard_map/ppermute | solution.py:25
  35.8 4.9 %collective-permute-start.7 = (bf16[16,384]{1,0:T(8,128)(2,1)S(1)}, bf16[16,384]{1,0:T(8,128)(2,1)S(1)}, u32[]{:S(2)}, u32[]{:S(2)}) collective-permute-start(bf16[16,384]{1,0:T(8,128)(2,1)S(1)} %get-tuple-element.34.f_0), channel_id=1, source_target_pairs={{13,0},{14,1},{15,2},{0,3},{1,4},{2,5},{3,6},{4,7},{5,8},{6,9},{7,... | collective-permute-start | bytes 36872 | tf_op jit(solution)/shard_map/ppermute | solution.py:25
  35.8 6.5 %collective-permute-start.8 = (bf16[16,384]{1,0:T(8,128)(2,1)S(1)}, bf16[16,384]{1,0:T(8,128)(2,1)S(1)}, u32[]{:S(2)}, u32[]{:S(2)}) collective-permute-start(bf16[16,384]{1,0:T(8,128)(2,1)S(1)} %get-tuple-element.34.f_0), channel_id=1, source_target_pairs={{14,0},{15,1},{0,2},{1,3},{2,4},{3,5},{4,6},{5,7},{6,8},{7,9},{8,1... | collective-permute-start | bytes 36872 | tf_op jit(solution)/shard_map/ppermute | solution.py:25
  37.8 5.8 %collective-permute-start.9 = (bf16[16,384]{1,0:T(8,128)(2,1)S(1)}, bf16[16,384]{1,0:T(8,128)(2,1)S(1)}, u32[]{:S(2)}, u32[]{:S(2)}) collective-permute-start(bf16[16,384]{1,0:T(8,128)(2,1)S(1)} %get-tuple-element.34.f_0), channel_id=1, source_target_pairs={{15,0},{0,1},{1,2},{2,3},{3,4},{4,5},{5,6},{6,7},{7,8},{8,9},{9,10... | collective-permute-start | bytes 36872 | tf_op jit(solution)/shard_map/ppermute | solution.py:25

commit v4 on v3

--- a/solution.py
+++ b/solution.py
@@ -107,15 +107,12 @@
     return one_hot(iota((nodes, grid_row.shape[1]), 0) == grid_row)
 
 
-def embed_kernel(
-    geometry_in, w_geometry_in, atmosphere_in, w_encode_in, grid_row_in, mesh_state_in,
-    latent_out, plain_out,
-    turned, geometry, w_geometry, atmosphere, w_encode, grid_row, mesh_state, sems,
+def plain_kernel(
+    atmosphere_in, w_encode_in, grid_row_in, mesh_state_in, plain_out,
+    atmosphere, w_encode, grid_row, mesh_state, sems,
 ):
     copies = started(
         (
-            (geometry_in, geometry),
-            (w_geometry_in, w_geometry),
             (grid_row_in, grid_row),
             (atmosphere_in, atmosphere),
             (w_encode_in, w_encode),
@@ -125,12 +122,7 @@
     )
     for copy in copies:
         copy.wait()
-    edges = geometry.shape[1]
-    nodes = edges // K
-    features = w_geometry.shape[1]
-    flat = jnp.concatenate([geometry[...].astype(F32), jnp.zeros((4, edges), F32)], axis=0)
-    turned[:, :8] = flat.T
-    member = members(nodes, grid_row[...])
+    member = members(mesh_state.shape[0], grid_row[...])
     population = jnp.sum(member.astype(F32), axis=1, keepdims=True)
     state = atmosphere[...]
     state = jnp.where(iota(state.shape, 0) == 0, 0.0, state.astype(F32)).astype(BF16)
@@ -139,10 +131,6 @@
     pooled_low = (pooled - pooled_high.astype(F32)).astype(BF16)
     encode = w_encode[...]
     plain_out[...] = mesh_state[...].astype(F32) + dot(pooled_high, encode) + dot(pooled_low, encode)
-    w_geo = jnp.concatenate([w_geometry[...].astype(F32), jnp.zeros((4, features), F32)], axis=0).astype(BF16)
-    for k in range(K):
-        points = turned[pl.ds(k, nodes, stride=K), :8].astype(BF16)
-        latent_out[k] = silu(dot(points, w_geo)).astype(BF16)
 
 
 def rolled_points(points, starts):
@@ -159,7 +147,7 @@
 
 
 def latent_kernel(
-    far, above, own, below, points, atmosphere, w_encode, grid_row, plain,
+    below, above, far, own, points, atmosphere, w_encode, grid_row, plain,
     latent_out, surface_out, placed_out,
 ):
     parts = [
@@ -196,23 +184,28 @@
     return jnp.sum(jnp.where(lane == k, listed, 0.0), axis=1, keepdims=True).astype(jnp.int32)
 
 
-def own_kernel(latent, w_in, edge_latent, neighbours, w_node_in, pre_out, base_out, node_out, sender):
+def own_kernel(
+    latent, w_in, geometry, w_geometry, neighbours, w_node_in, pre_out, base_out, node_out, sender, turned,
+):
     nodes, features = latent.shape
     value = latent[...]
     sender[...] = dot(value, w_in[features : 2 * features]).astype(BF16)
     receiver = dot(value, w_in[2 * features :])
     node_out[...] = dot(value, w_node_in[:features])
     listed = listed_slots(neighbours)
-
-    def step(k, base):
+    blank = jnp.zeros((4, geometry.shape[1]), F32)
+    turned[:, :8] = jnp.concatenate([geometry[...].astype(F32), blank], axis=0).T
+    blank = jnp.zeros((4, features), F32)
+    w_geo = jnp.concatenate([w_geometry[...].astype(F32), blank], axis=0).astype(BF16)
+    base = jnp.zeros((nodes, features), F32)
+    for k in range(K):
         at = slot_senders(listed, k)
-        edge = edge_latent[k]
+        edge = silu(dot(turned[pl.ds(k, nodes, stride=K), :8].astype(BF16), w_geo)).astype(BF16)
         match = one_hot(iota((nodes, nodes), 1) + nodes == at)
         joined = dot(edge, w_in[:features]) + dot(match, sender[...])
         pre_out[k] = (joined + receiver).astype(BF16)
-        return base + jnp.where(at < 3 * nodes, edge.astype(F32), 0.0)
-
-    base_out[...] = lax.fori_loop(0, K, step, jnp.zeros((nodes, features), F32), unroll=True)
+        base = base + jnp.where(at < 3 * nodes, edge.astype(F32), 0.0)
+    base_out[...] = base
 
 
 def normal(values):
@@ -311,7 +304,7 @@
         qy_out[c] = opened * (face - COEFF_H)
 
 
-def ocean_kernel(f_p1, f_p2, f_m3, f_m2, f_m1, f_0, field_in, wet, px, qx, py, qy, mix, out):
+def ocean_kernel(f_m1, f_m2, f_m3, f_p2, f_p1, f_0, field_in, wet, px, qx, py, qy, mix, out):
     count, levels, rows = field_in.shape
     columns = count - 2 * EDGE
     triples = columns // 3
@@ -423,32 +416,29 @@
         ],
         name="pack",
     )
+    below = shifted(high, 1)
+    above = shifted(low, -1)
     far = shifted(blocks, -2)
-    above = shifted(low, -1)
-    below = shifted(high, 1)
-    edge_latent, plain = call(
-        embed_kernel,
-        [((K, nodes, features), BF16), ((nodes, features), F32)],
-        [edge_geometry, w_geometry, atmosphere_t, w_encode, grid_row, mesh_state],
+    (plain,) = call(
+        plain_kernel,
+        [((nodes, features), F32)],
+        [atmosphere_t, w_encode, grid_row, mesh_state],
         spec=HBM,
         scratch=[
-            pltpu.VMEM((K * nodes, 128), F32),
-            pltpu.VMEM(edge_geometry.shape, BF16),
-            pltpu.VMEM(w_geometry.shape, BF16),
             pltpu.VMEM((channels, n_points), BF16),
             pltpu.VMEM(w_encode.shape, BF16),
             pltpu.VMEM((1, n_points), jnp.int32),
             pltpu.VMEM((nodes, features), BF16),
-            pltpu.SemaphoreType.DMA((6,)),
+            pltpu.SemaphoreType.DMA((4,)),
         ],
-        flops=2 * K * nodes * features * features,
-        bytes_accessed=8 << 20,
-        name="embed",
+        flops=6 * nodes * channels * n_points,
+        bytes_accessed=2 << 20,
+        name="plain",
     )
     latent, surface, placed = call(
         latent_kernel,
         [((nodes, features), BF16), ((1, n_points), F32), ((1, W * rows), jnp.int32)],
-        [far, above, blocks, below, intersection_points[0], atmosphere_t, w_encode, grid_row, plain],
+        [below, above, far, blocks, intersection_points[0], atmosphere_t, w_encode, grid_row, plain],
         name="latents",
     )
     latent_low = shifted(latent, 1)
@@ -456,8 +446,8 @@
     pre, base, node_part = call(
         own_kernel,
         [((K, nodes, features), BF16), ((nodes, features), F32), ((nodes, features), F32)],
-        [latent, w_edge_in, edge_latent, slots, w_node_in],
-        scratch=[pltpu.VMEM((nodes, features), BF16)],
+        [latent, w_edge_in, edge_geometry, w_geometry, slots, w_node_in],
+        scratch=[pltpu.VMEM((nodes, features), BF16), pltpu.VMEM((K * nodes, 128), F32)],
         flops=2 * K * nodes * (nodes + features) * features,
         bytes_accessed=10 << 20,
         name="own",
@@ -485,7 +475,7 @@
     )
     sent = {d: shifted(flux, d) for d in (1, 2, 3, -1, -2)}
     sent[0] = flux
-    arrived = [sent[d] for d in (-1, -2, 3, 2, 1, 0)]
+    arrived = [sent[d] for d in (1, 2, 3, -2, -1, 0)]
     (state,) = call(
         decode_kernel,
         [((channels, n_points), BF16)],

time: 45.1 us -> 42.9 us (0.951)
  waiting for transfers between devices: 7.86 us -> 0.03 us
  local copies, waits for them, and re-layouts: 0.09 us -> 4.72 us
  starting transfers between devices: 17.4 us -> 18.2 us
    ppermute x10, waiting for transfers between devices: 7.86 us -> 0.03 us  [shifted(): lax.ppermute(block, AXES, [((i - distance) % count, i) for i in range(cou...]
    unnamed x32 -> x42, local copies, waits for them, and re-layouts: 0.09 us -> 4.72 us
    ppermute x10, starting transfers between devices: 17.4 us -> 18.2 us  [shifted(): lax.ppermute(block, AXES, [((i - distance) % count, i) for i in range(cou...]
  transfers between devices with their start and end apart: 10 -> 10, of which waited for: 6 -> 0; matrix products, arithmetic and copies ran while one was open for 0% -> 0% of each run, Pallas kernels for 18% -> 19%
where the time goes in v4:
time: 42.9 us; the launch traced here: 42.6 us
  Pallas kernels  18.8 us (44%)
  starting transfers between devices  18.2 us (42%)
  local copies, waits for them, and re-layouts  4.72 us (11%)
  between operations  0.97 us (2%)
    pallas_call x8, Pallas kernels, call(): pl.pallas_call(kernel, out_shape=[jax.ShapeDtypeStruct(s, t) for s, t in...  18.8 us
    ppermute x10, starting transfers between devices, shifted(): lax.ppermute(block, AXES, [((i - distance) % count, i) for i in range(cou...  18.2 us
    unnamed x42, local copies, waits for them, and re-layouts  4.72 us
  transfers between devices with their start and end apart: 10, of which 0 were waited for; matrix products, arithmetic and copies ran while one was open for 0% of the time, Pallas kernels for 19%

profile of v4, /device:TPU:0, one launch (start us, length us, event | category | flops | bytes accessed | tf_op | source)
XLA Modules:
  0.0 42.6 jit_solution(16478160888876312534)
XLA Ops:
  0.7 1.4 %pack.1 = (bf16[112,384]{1,0:T(8,128)(2,1)S(1)}, bf16[112,384]{1,0:T(8,128)(2,1)S(1)}, bf16[16,384]{1,0:T(8,128)(2,1)S(1)}) custom-call(s32[1,4]{1,0:T(1,128)} %counts_in.1, f32[9,8,384]{2,1,0:T(8,128)} %bitcast.16, f32[9,8,384]{2,1,0:T(8,128)} %bitcast.18, f32[9,8,384]{2,1,0:T(8,128)} %bitcast.20, s32[9,384]{1,0:T(8,128)} %mask.1), custom_call_target="tpu_custom_call" | custom-call | bytes 1048576 | tf_op jit(solution)/shard_map/pack/pallas_call | solution.py:357
  2.1 0.5 %collective-permute-start = (bf16[112,384]{1,0:T(8,128)(2,1)S(1)}, bf16[112,384]{1,0:T(8,128)(2,1)S(1)}, u32[]{:S(2)}, u32[]{:S(2)}) collective-permute-start(bf16[112,384]{1,0:T(8,128)(2,1)S(1)} %get-tuple-element.20), channel_id=1, source_target_pairs={{15,0},{0,1},{1,2},{2,3},{3,4},{4,5},{5,6},{6,7},{7,8},{8,9},{9,10... | collective-permute-start | bytes 258056 | tf_op jit(solution)/shard_map/ppermute | solution.py:25
  2.6 5.0 %collective-permute-start.1 = (bf16[112,384]{1,0:T(8,128)(2,1)S(1)}, bf16[112,384]{1,0:T(8,128)(2,1)S(1)}, u32[]{:S(2)}, u32[]{:S(2)}) collective-permute-start(bf16[112,384]{1,0:T(8,128)(2,1)S(1)} %get-tuple-element.21), channel_id=1, source_target_pairs={{1,0},{2,1},{3,2},{4,3},{5,4},{6,5},{7,6},{8,7},{9,8},{10,9},{11,1... | collective-permute-start | bytes 258056 | tf_op jit(solution)/shard_map/ppermute | solution.py:25
  7.7 2.2 %collective-permute-start.2 = (bf16[16,384]{1,0:T(8,128)(2,1)S(1)}, bf16[16,384]{1,0:T(8,128)(2,1)S(1)}, u32[]{:S(2)}, u32[]{:S(2)}) collective-permute-start(bf16[16,384]{1,0:T(8,128)(2,1)S(1)} %get-tuple-element.22.own), channel_id=1, source_target_pairs={{2,0},{3,1},{4,2},{5,3},{6,4},{7,5},{8,6},{9,7},{10,8},{11,9},{12,... | collective-permute-start | bytes 36872 | tf_op jit(solution)/shard_map/ppermute | solution.py:25
  9.9 2.0 %plain.1 = f32[320,512]{1,0:T(8,128)S(1)} custom-call(bf16[227,512]{1,0:T(8,128)(2,1)} %bitcast.12, bf16[227,512]{1,0:T(8,128)(2,1)} %w_encode.1, s32[1,512]{1,0:T(1,128)} %bitcast.24, bf16[320,512]{1,0:T(8,128)(2,1)} %mesh_state_in.1), custom_call_target="tpu_custom_call" | custom-call | flops 223150080 | bytes 2097152 | tf_op jit(solution)/shard_map/plain/pallas_call | solution.py:357
  11.9 0.0 collective-permute-done.2.far
  11.9 0.0 collective-permute-done.below.low
  11.9 0.0 copy-start
  11.9 0.9 %copy-done = bf16[512,227]{0,1:T(8,128)(2,1)S(1)} copy-done((bf16[512,227]{0,1:T(8,128)(2,1)S(1)}, bf16[512,227]{0,1:T(8,128)(2,1)}, u32[]{:S(2)}) %copy-start) | copy-done | bytes 232472
  12.8 0.9 %copy-done.2 = bf16[227,512]{1,0:T(8,128)(2,1)S(1)} copy-done((bf16[227,512]{1,0:T(8,128)(2,1)S(1)}, bf16[227,512]{1,0:T(8,128)(2,1)}, u32[]{:S(2)}) %copy-start.2) | copy-done | bytes 232472
  13.8 0.7 %copy-done.8 = s32[512]{0:T(512)S(1)} copy-done((s32[512]{0:T(512)S(1)}, s32[512]{0:T(512)}, u32[]{:S(2)}) %copy-start.8) | copy-done | bytes 2072
  14.5 0.7 %copy-done.10 = s32[1,4,192]{2,1,0:T(4,128)S(1)} copy-done((s32[1,4,192]{2,1,0:T(4,128)S(1)}, s32[1,4,192]{2,1,0:T(4,128)}, u32[]{:S(2)}) %copy-start.10) | copy-done | bytes 3096
  15.2 1.0 %latents.1 = (bf16[320,512]{1,0:T(8,128)(2,1)S(1)}, f32[1,512]{1,0:T(1,128)S(1)}, s32[1,1536]{1,0:T(1,128)S(1)}) custom-call(bf16[112,384]{1,0:T(8,128)(2,1)S(1)} %collective-permute-done.below.low, bf16[112,384]{1,0:T(8,128)(2,1)S(1)} %collective-permute-done.1.above.high, bf16[16,384]{1,0:T(8,128)(2,1)S(1)} %collective-permute-done.2.far, ...), custom_call_target="tpu_custom_call" | custom-call | bytes 1048576 | tf_op jit(solution)/shard_map/latents/pallas_call | solution.py:357
  16.2 0.1 collective-permute-start.3
  16.3 4.4 %collective-permute-start.4 = (bf16[320,512]{1,0:T(8,128)(2,1)S(1)}, bf16[320,512]{1,0:T(8,128)(2,1)S(1)}, u32[]{:S(2)}, u32[]{:S(2)}) collective-permute-start(bf16[320,512]{1,0:T(8,128)(2,1)S(1)} %get-tuple-element.23.latent), channel_id=1, source_target_pairs={{1,0},{2,1},{3,2},{4,3},{5,4},{6,5},{7,6},{8,7},{9,8},{10,9},{11,1... | collective-permute-start | bytes 983048 | tf_op jit(solution)/shard_map/ppermute | solution.py:25
  20.7 0.2 ready.1
  20.9 0.0 copy-start.11
  20.9 1.4 %copy-done.11 = bf16[1536,512]{1,0:T(8,128)(2,1)S(1)} copy-done((bf16[1536,512]{1,0:T(8,128)(2,1)S(1)}, bf16[1536,512]{1,0:T(8,128)(2,1)}, u32[]{:S(2)}) %copy-start.11) | copy-done | bytes 1572888
  22.4 0.0 copy-start.14
  22.4 0.0 copy-start.15
  22.4 0.0 copy-start.19
  22.4 0.0 copy-start.20
  22.4 4.6 %own.1 = (bf16[8,320,512]{2,1,0:T(8,128)(2,1)S(1)}, f32[320,512]{1,0:T(8,128)S(1)}, f32[320,512]{1,0:T(8,128)S(1)}) custom-call(bf16[320,512]{1,0:T(8,128)(2,1)S(1)} %get-tuple-element.23.latent, bf16[1536,512]{1,0:T(8,128)(2,1)S(1)} %copy-done.11, bf16[4,2560]{1,0:T(4,128)(2,1)S(1)} %copy-done.16, bf16[4,512]{1,0:T(4,128)(2,1)S(1)} %copy-done.18, ...), custom_call_target="tpu_custom_call" | custom-call | flops 2181038080 | bytes 10485760 | tf_op jit(solution)/shard_map/own/pallas_call | solution.py:357
  27.0 0.0 collective-permute-done.4.high
  27.1 6.9 %mesh.1 = (bf16[320,512]{1,0:T(8,128)(2,1)S(1)}, bf16[16,384]{1,0:T(8,128)(2,1)S(1)}) custom-call(bf16[320,512]{1,0:T(8,128)(2,1)S(1)} %collective-permute-done.3.low, bf16[320,512]{1,0:T(8,128)(2,1)S(1)} %collective-permute-done.4.high, bf16[320,512]{1,0:T(8,128)(2,1)S(1)} %get-tuple-element.23.latent, bf16[1536,512]{1,0:T(8,128)(2,1)S(1)} %copy-done.12, ...), custom_call_target="tpu_custom_call" | custom-call | flops 2516582400 | bytes 10485760 | tf_op jit(solution)/shard_map/mesh/pallas_call | solution.py:357
  34.0 0.0 collective-permute-start.6
  34.0 1.7 %collective-permute-start.7 = (bf16[16,384]{1,0:T(8,128)(2,1)S(1)}, bf16[16,384]{1,0:T(8,128)(2,1)S(1)}, u32[]{:S(2)}, u32[]{:S(2)}) collective-permute-start(bf16[16,384]{1,0:T(8,128)(2,1)S(1)} %get-tuple-element.30.f_0), channel_id=1, source_target_pairs={{13,0},{14,1},{15,2},{0,3},{1,4},{2,5},{3,6},{4,7},{5,8},{6,9},{7,... | collective-permute-start | bytes 36872 | tf_op jit(solution)/shard_map/ppermute | solution.py:25
  35.7 3.1 %collective-permute-start.8 = (bf16[16,384]{1,0:T(8,128)(2,1)S(1)}, bf16[16,384]{1,0:T(8,128)(2,1)S(1)}, u32[]{:S(2)}, u32[]{:S(2)}) collective-permute-start(bf16[16,384]{1,0:T(8,128)(2,1)S(1)} %get-tuple-element.30.f_0), channel_id=1, source_target_pairs={{2,0},{3,1},{4,2},{5,3},{6,4},{7,5},{8,6},{9,7},{10,8},{11,9},{12,... | collective-permute-start | bytes 36872 | tf_op jit(solution)/shard_map/ppermute | solution.py:25
  38.8 1.2 %collective-permute-start.9 = (bf16[16,384]{1,0:T(8,128)(2,1)S(1)}, bf16[16,384]{1,0:T(8,128)(2,1)S(1)}, u32[]{:S(2)}, u32[]{:S(2)}) collective-permute-start(bf16[16,384]{1,0:T(8,128)(2,1)S(1)} %get-tuple-element.30.f_0), channel_id=1, source_target_pairs={{1,0},{2,1},{3,2},{4,3},{5,4},{6,5},{7,6},{8,7},{9,8},{10,9},{11,1... | collective-permute-start | bytes 36872 | tf_op jit(solution)/shard_map/ppermute | solution.py:25
  39.9 1.4 %decode.1 = bf16[227,512]{1,0:T(8,128)(2,1)} custom-call(bf16[320,512]{1,0:T(8,128)(2,1)S(1)} %get-tuple-element.28.node_new, bf16[227,512]{1,0:T(8,128)(2,1)S(1)} %bitcast.23, s32[1,512]{1,0:T(1,128)S(1)} %bitcast.27, bf16[227,512]{1,0:T(8,128)(2,1)S(1)} %bitcast.15, f32[1,512]{1,0:T(1,128)S(1)} %get-tuple-element.29.surface), custom_call_target="tpu_custom_call" | custom-call | flops 223150080 | bytes 1048576 | tf_op jit(solution)/shard_map/decode/pallas_call | solution.py:357
  41.3 0.0 collective-permute-done.9.f_p1
  41.3 1.3 %ocean.1 = f32[9,8,384]{2,1,0:T(8,128)} custom-call(bf16[16,384]{1,0:T(8,128)(2,1)S(1)} %collective-permute-done.5.f_m1, bf16[16,384]{1,0:T(8,128)(2,1)S(1)} %collective-permute-done.6.f_m2, bf16[16,384]{1,0:T(8,128)(2,1)S(1)} %collective-permute-done.7.f_m3, bf16[16,384]{1,0:T(8,128)(2,1)S(1)} %collective-permute-done.8.f_p2, ...), custom_call_target="tpu_custom_call" | custom-call | bytes 4194304 | tf_op jit(solution)/shard_map/ocean/pallas_call | solution.py:357
  (38 shorter events, 0.1 us)
Async XLA Ops:
  0.6 20.1 %copy-start.3 = (f32[8,9,384]{2,0,1:T(8,128)S(1)}, f32[8,9,384]{2,0,1:T(8,128)}, u32[]{:S(2)}) copy-start(f32[8,9,384]{2,0,1:T(8,128)} %param.25) | copy-start | bytes 331780
  0.6 20.1 %copy-start.4 = (f32[8,9,384]{2,0,1:T(8,128)S(1)}, f32[8,9,384]{2,0,1:T(8,128)}, u32[]{:S(2)}) copy-start(f32[8,9,384]{2,0,1:T(8,128)} %param.26) | copy-start | bytes 331780
  0.7 20.0 %copy-start.5 = (f32[8,9,384]{2,0,1:T(8,128)S(1)}, f32[8,9,384]{2,0,1:T(8,128)}, u32[]{:S(2)}) copy-start(f32[8,9,384]{2,0,1:T(8,128)} %param.27) | copy-start | bytes 331780
  0.7 20.0 %copy-start.7 = (s32[9,384]{1,0:T(8,128)S(1)}, s32[9,384]{1,0:T(8,128)}, u32[]{:S(2)}) copy-start(s32[9,384]{1,0:T(8,128)} %mask.1) | copy-start | bytes 41476
  0.7 20.2 %copy-start.17 = (s32[320,8]{0,1:T(8,128)S(1)}, s32[320,8]{0,1:T(8,128)}, u32[]{:S(2)}) copy-start(s32[320,8]{0,1:T(8,128)} %param.23) | copy-start | bytes 30724
  0.7 20.2 %copy-start.16 = (bf16[4,2560]{1,0:T(4,128)(2,1)S(1)}, bf16[4,2560]{1,0:T(4,128)(2,1)}, u32[]{:S(2)}) copy-start(bf16[4,2560]{1,0:T(4,128)(2,1)} %geometry.1) | copy-start | bytes 61444
  0.7 20.2 %copy-start.18 = (bf16[4,512]{1,0:T(4,128)(2,1)S(1)}, bf16[4,512]{1,0:T(4,128)(2,1)}, u32[]{:S(2)}) copy-start(bf16[4,512]{1,0:T(4,128)(2,1)} %w_geometry.1) | copy-start | bytes 12292
  0.7 20.2 %copy-start.13 = (bf16[1024,512]{1,0:T(8,128)(2,1)S(1)}, bf16[1024,512]{1,0:T(8,128)(2,1)}, u32[]{:S(2)}) copy-start(bf16[1024,512]{1,0:T(8,128)(2,1)} %w_node_in.3) | copy-start | bytes 3145732
  2.1 9.8 %collective-permute-start = (bf16[112,384]{1,0:T(8,128)(2,1)S(1)}, bf16[112,384]{1,0:T(8,128)(2,1)S(1)}, u32[]{:S(2)}, u32[]{:S(2)}) collective-permute-start(bf16[112,384]{1,0:T(8,128)(2,1)S(1)} %get-tuple-element.20), channel_id=1, source_target_pairs={{15,0},{0,1},{1,2},{2,3},{3,4},{4,5},{5,6},{6,7},{7,8},{8,9},{9,10... | collective-permute-start | bytes 258056 | tf_op jit(solution)/shard_map/ppermute | solution.py:25
  2.6 9.3 %collective-permute-start.1 = (bf16[112,384]{1,0:T(8,128)(2,1)S(1)}, bf16[112,384]{1,0:T(8,128)(2,1)S(1)}, u32[]{:S(2)}, u32[]{:S(2)}) collective-permute-start(bf16[112,384]{1,0:T(8,128)(2,1)S(1)} %get-tuple-element.21), channel_id=1, source_target_pairs={{1,0},{2,1},{3,2},{4,3},{5,4},{6,5},{7,6},{8,7},{9,8},{10,9},{11,1... | collective-permute-start | bytes 258056 | tf_op jit(solution)/shard_map/ppermute | solution.py:25
  7.7 4.2 %collective-permute-start.2 = (bf16[16,384]{1,0:T(8,128)(2,1)S(1)}, bf16[16,384]{1,0:T(8,128)(2,1)S(1)}, u32[]{:S(2)}, u32[]{:S(2)}) collective-permute-start(bf16[16,384]{1,0:T(8,128)(2,1)S(1)} %get-tuple-element.22.own), channel_id=1, source_target_pairs={{2,0},{3,1},{4,2},{5,3},{6,4},{7,5},{8,6},{9,7},{10,8},{11,9},{12,... | collective-permute-start | bytes 36872 | tf_op jit(solution)/shard_map/ppermute | solution.py:25
  11.9 0.9 %copy-start = (bf16[512,227]{0,1:T(8,128)(2,1)S(1)}, bf16[512,227]{0,1:T(8,128)(2,1)}, u32[]{:S(2)}) copy-start(bf16[512,227]{0,1:T(8,128)(2,1)} %param.20) | copy-start | bytes 697348
  12.8 0.9 %copy-start.2 = (bf16[227,512]{1,0:T(8,128)(2,1)S(1)}, bf16[227,512]{1,0:T(8,128)(2,1)}, u32[]{:S(2)}) copy-start(bf16[227,512]{1,0:T(8,128)(2,1)} %w_encode.1) | copy-start | bytes 697348
  13.8 0.7 %copy-start.8 = (s32[512]{0:T(512)S(1)}, s32[512]{0:T(512)}, u32[]{:S(2)}) copy-start(s32[512]{0:T(512)} %param.24) | copy-start | bytes 6148
  14.5 0.7 %copy-start.10 = (s32[1,4,192]{2,1,0:T(4,128)S(1)}, s32[1,4,192]{2,1,0:T(4,128)}, u32[]{:S(2)}) copy-start(s32[1,4,192]{2,1,0:T(4,128)} %param.29) | copy-start | bytes 9220
  16.2 10.8 %collective-permute-start.3 = (bf16[320,512]{1,0:T(8,128)(2,1)S(1)}, bf16[320,512]{1,0:T(8,128)(2,1)S(1)}, u32[]{:S(2)}, u32[]{:S(2)}) collective-permute-start(bf16[320,512]{1,0:T(8,128)(2,1)S(1)} %get-tuple-element.23.latent), channel_id=1, source_target_pairs={{15,0},{0,1},{1,2},{2,3},{3,4},{4,5},{5,6},{6,7},{7,8},{8,9},{9,10... | collective-permute-start | bytes 983048 | tf_op jit(solution)/shard_map/ppermute | solution.py:25
  16.3 10.8 %collective-permute-start.4 = (bf16[320,512]{1,0:T(8,128)(2,1)S(1)}, bf16[320,512]{1,0:T(8,128)(2,1)S(1)}, u32[]{:S(2)}, u32[]{:S(2)}) collective-permute-start(bf16[320,512]{1,0:T(8,128)(2,1)S(1)} %get-tuple-element.23.latent), channel_id=1, source_target_pairs={{1,0},{2,1},{3,2},{4,3},{5,4},{6,5},{7,6},{8,7},{9,8},{10,9},{11,1... | collective-permute-start | bytes 983048 | tf_op jit(solution)/shard_map/ppermute | solution.py:25
  20.9 1.4 %copy-start.11 = (bf16[1536,512]{1,0:T(8,128)(2,1)S(1)}, bf16[1536,512]{1,0:T(8,128)(2,1)}, u32[]{:S(2)}) copy-start(bf16[1536,512]{1,0:T(8,128)(2,1)} %w_in.3) | copy-start | bytes 4718596
  22.3 4.7 %copy-start.1 = (bf16[512,227]{0,1:T(8,128)(2,1)S(1)}, bf16[512,227]{0,1:T(8,128)(2,1)}, u32[]{:S(2)}) copy-start(bf16[512,227]{0,1:T(8,128)(2,1)} %param.20) | copy-start | bytes 697348
  22.4 4.7 %copy-start.6 = (bf16[512,227]{0,1:T(8,128)(2,1)S(1)}, bf16[512,227]{0,1:T(8,128)(2,1)}, u32[]{:S(2)}) copy-start(bf16[512,227]{0,1:T(8,128)(2,1)} %param.37) | copy-start | bytes 697348
  22.4 4.7 %copy-start.9 = (s32[512]{0:T(512)S(1)}, s32[512]{0:T(512)}, u32[]{:S(2)}) copy-start(s32[512]{0:T(512)} %param.24) | copy-start | bytes 6148
  22.4 4.7 %copy-start.12 = (bf16[1536,512]{1,0:T(8,128)(2,1)S(1)}, bf16[1536,512]{1,0:T(8,128)(2,1)}, u32[]{:S(2)}) copy-start(bf16[1536,512]{1,0:T(8,128)(2,1)} %w_in.3) | copy-start | bytes 4718596
  22.4 4.7 %copy-start.14 = (bf16[512,512]{1,0:T(8,128)(2,1)S(1)}, bf16[512,512]{1,0:T(8,128)(2,1)}, u32[]{:S(2)}) copy-start(bf16[512,512]{1,0:T(8,128)(2,1)} %w_out.1) | copy-start | bytes 1572868
  22.4 4.7 %copy-start.15 = (bf16[512,512]{1,0:T(8,128)(2,1)S(1)}, bf16[512,512]{1,0:T(8,128)(2,1)}, u32[]{:S(2)}) copy-start(bf16[512,512]{1,0:T(8,128)(2,1)} %w_node_out.1) | copy-start | bytes 1572868
  22.4 4.7 %copy-start.19 = (f32[512]{0:T(512)S(1)}, f32[512]{0:T(512)}, u32[]{:S(2)}) copy-start(f32[512]{0:T(512)} %param.38) | copy-start | bytes 6148
  22.4 4.7 %copy-start.20 = (f32[512]{0:T(512)S(1)}, f32[512]{0:T(512)}, u32[]{:S(2)}) copy-start(f32[512]{0:T(512)} %param.39) | copy-start | bytes 6148
  34.0 7.3 %collective-permute-start.5 = (bf16[16,384]{1,0:T(8,128)(2,1)S(1)}, bf16[16,384]{1,0:T(8,128)(2,1)S(1)}, u32[]{:S(2)}, u32[]{:S(2)}) collective-permute-start(bf16[16,384]{1,0:T(8,128)(2,1)S(1)} %get-tuple-element.30.f_0), channel_id=1, source_target_pairs={{15,0},{0,1},{1,2},{2,3},{3,4},{4,5},{5,6},{6,7},{7,8},{8,9},{9,10... | collective-permute-start | bytes 36872 | tf_op jit(solution)/shard_map/ppermute | solution.py:25
  34.0 7.3 %collective-permute-start.6 = (bf16[16,384]{1,0:T(8,128)(2,1)S(1)}, bf16[16,384]{1,0:T(8,128)(2,1)S(1)}, u32[]{:S(2)}, u32[]{:S(2)}) collective-permute-start(bf16[16,384]{1,0:T(8,128)(2,1)S(1)} %get-tuple-element.30.f_0), channel_id=1, source_target_pairs={{14,0},{15,1},{0,2},{1,3},{2,4},{3,5},{4,6},{5,7},{6,8},{7,9},{8,1... | collective-permute-start | bytes 36872 | tf_op jit(solution)/shard_map/ppermute | solution.py:25
  34.0 7.3 %collective-permute-start.7 = (bf16[16,384]{1,0:T(8,128)(2,1)S(1)}, bf16[16,384]{1,0:T(8,128)(2,1)S(1)}, u32[]{:S(2)}, u32[]{:S(2)}) collective-permute-start(bf16[16,384]{1,0:T(8,128)(2,1)S(1)} %get-tuple-element.30.f_0), channel_id=1, source_target_pairs={{13,0},{14,1},{15,2},{0,3},{1,4},{2,5},{3,6},{4,7},{5,8},{6,9},{7,... | collective-permute-start | bytes 36872 | tf_op jit(solution)/shard_map/ppermute | solution.py:25
  35.7 5.6 %collective-permute-start.8 = (bf16[16,384]{1,0:T(8,128)(2,1)S(1)}, bf16[16,384]{1,0:T(8,128)(2,1)S(1)}, u32[]{:S(2)}, u32[]{:S(2)}) collective-permute-start(bf16[16,384]{1,0:T(8,128)(2,1)S(1)} %get-tuple-element.30.f_0), channel_id=1, source_target_pairs={{2,0},{3,1},{4,2},{5,3},{6,4},{7,5},{8,6},{9,7},{10,8},{11,9},{12,... | collective-permute-start | bytes 36872 | tf_op jit(solution)/shard_map/ppermute | solution.py:25
  38.8 2.6 %collective-permute-start.9 = (bf16[16,384]{1,0:T(8,128)(2,1)S(1)}, bf16[16,384]{1,0:T(8,128)(2,1)S(1)}, u32[]{:S(2)}, u32[]{:S(2)}) collective-permute-start(bf16[16,384]{1,0:T(8,128)(2,1)S(1)} %get-tuple-element.30.f_0), channel_id=1, source_target_pairs={{1,0},{2,1},{3,2},{4,3},{5,4},{6,5},{7,6},{8,7},{9,8},{10,9},{11,1... | collective-permute-start | bytes 36872 | tf_op jit(solution)/shard_map/ppermute | solution.py:25

commit v5 on v4

--- a/solution.py
+++ b/solution.py
@@ -431,8 +431,8 @@
             pltpu.VMEM((nodes, features), BF16),
             pltpu.SemaphoreType.DMA((4,)),
         ],
-        flops=6 * nodes * channels * n_points,
-        bytes_accessed=2 << 20,
+        flops=2 * K * nodes * features * features,
+        bytes_accessed=8 << 20,
         name="plain",
     )
     latent, surface, placed = call(

time: 42.9 us -> 38.9 us (0.907); the launches traced: 42.6 us -> 38.1 us
  local copies, waits for them, and re-layouts: 4.72 us -> 0.1 us
    unnamed x42 -> x36, local copies, waits for them, and re-layouts: 4.72 us -> 0.1 us
  transfers between devices with their start and end apart: 10 -> 10, of which waited for: 0 -> 0; matrix products, arithmetic and copies ran while one was open for 0% -> 0% of each run, Pallas kernels for 19% -> 22%
where the time goes in v5:
time: 38.9 us; the launch traced here: 38.1 us
  Pallas kernels  18.9 us (49%)
  starting transfers between devices  18.2 us (47%)
  between operations  0.97 us (2%)
    pallas_call x8, Pallas kernels, call(): pl.pallas_call(kernel, out_shape=[jax.ShapeDtypeStruct(s, t) for s, t in...  18.9 us
    ppermute x10, starting transfers between devices, shifted(): lax.ppermute(block, AXES, [((i - distance) % count, i) for i in range(cou...  18.2 us
  transfers between devices with their start and end apart: 10, of which 0 were waited for; matrix products, arithmetic and copies ran while one was open for 0% of the time, Pallas kernels for 22%

profile of v5, /device:TPU:0, one launch (start us, length us, event | category | flops | bytes accessed | tf_op | source)
XLA Modules:
  0.0 38.1 jit_solution(16631384814019333331)
XLA Ops:
  0.6 0.0 copy-start
  0.6 0.0 copy-start.4
  0.7 0.0 copy-start.7
  0.7 1.3 %pack.1 = (bf16[112,384]{1,0:T(8,128)(2,1)S(1)}, bf16[112,384]{1,0:T(8,128)(2,1)S(1)}, bf16[16,384]{1,0:T(8,128)(2,1)S(1)}) custom-call(s32[1,4]{1,0:T(1,128)} %counts_in.1, f32[9,8,384]{2,1,0:T(8,128)} %bitcast.16, f32[9,8,384]{2,1,0:T(8,128)} %bitcast.18, f32[9,8,384]{2,1,0:T(8,128)} %bitcast.20, s32[9,384]{1,0:T(8,128)} %mask.1), custom_call_target="tpu_custom_call" | custom-call | bytes 1048576 | tf_op jit(solution)/shard_map/pack/pallas_call | solution.py:357
  2.0 0.5 %collective-permute-start = (bf16[112,384]{1,0:T(8,128)(2,1)S(1)}, bf16[112,384]{1,0:T(8,128)(2,1)S(1)}, u32[]{:S(2)}, u32[]{:S(2)}) collective-permute-start(bf16[112,384]{1,0:T(8,128)(2,1)S(1)} %get-tuple-element.20), channel_id=1, source_target_pairs={{15,0},{0,1},{1,2},{2,3},{3,4},{4,5},{5,6},{6,7},{7,8},{8,9},{9,10... | collective-permute-start | bytes 258056 | tf_op jit(solution)/shard_map/ppermute | solution.py:25
  2.5 5.0 %collective-permute-start.1 = (bf16[112,384]{1,0:T(8,128)(2,1)S(1)}, bf16[112,384]{1,0:T(8,128)(2,1)S(1)}, u32[]{:S(2)}, u32[]{:S(2)}) collective-permute-start(bf16[112,384]{1,0:T(8,128)(2,1)S(1)} %get-tuple-element.21), channel_id=1, source_target_pairs={{1,0},{2,1},{3,2},{4,3},{5,4},{6,5},{7,6},{8,7},{9,8},{10,9},{11,1... | collective-permute-start | bytes 258056 | tf_op jit(solution)/shard_map/ppermute | solution.py:25
  7.6 2.2 %collective-permute-start.2 = (bf16[16,384]{1,0:T(8,128)(2,1)S(1)}, bf16[16,384]{1,0:T(8,128)(2,1)S(1)}, u32[]{:S(2)}, u32[]{:S(2)}) collective-permute-start(bf16[16,384]{1,0:T(8,128)(2,1)S(1)} %get-tuple-element.22.own), channel_id=1, source_target_pairs={{2,0},{3,1},{4,2},{5,3},{6,4},{7,5},{8,6},{9,7},{10,8},{11,9},{12,... | collective-permute-start | bytes 36872 | tf_op jit(solution)/shard_map/ppermute | solution.py:25
  9.8 0.0 copy-start.9
  9.8 0.0 copy-start.10
  9.8 0.0 copy-start.13
  9.8 0.0 copy-start.14
  9.9 0.0 copy-start.15
  9.9 2.1 %plain.1 = f32[320,512]{1,0:T(8,128)S(1)} custom-call(bf16[227,512]{1,0:T(8,128)(2,1)} %bitcast.12, bf16[227,512]{1,0:T(8,128)(2,1)} %w_encode.1, s32[1,512]{1,0:T(1,128)} %bitcast.24, bf16[320,512]{1,0:T(8,128)(2,1)} %mesh_state_in.1), custom_call_target="tpu_custom_call" | custom-call | flops 1342177280 | bytes 8388608 | tf_op jit(solution)/shard_map/plain/pallas_call | solution.py:357
  12.0 0.0 collective-permute-done.2.far
  12.0 1.0 %latents.1 = (bf16[320,512]{1,0:T(8,128)(2,1)S(1)}, f32[1,512]{1,0:T(1,128)S(1)}, s32[1,1536]{1,0:T(1,128)S(1)}) custom-call(bf16[112,384]{1,0:T(8,128)(2,1)S(1)} %collective-permute-done.below.low, bf16[112,384]{1,0:T(8,128)(2,1)S(1)} %collective-permute-done.1.above.high, bf16[16,384]{1,0:T(8,128)(2,1)S(1)} %collective-permute-done.2.far, ...), custom_call_target="tpu_custom_call" | custom-call | bytes 1048576 | tf_op jit(solution)/shard_map/latents/pallas_call | solution.py:357
  13.1 0.1 collective-permute-start.3
  13.2 4.4 %collective-permute-start.4 = (bf16[320,512]{1,0:T(8,128)(2,1)S(1)}, bf16[320,512]{1,0:T(8,128)(2,1)S(1)}, u32[]{:S(2)}, u32[]{:S(2)}) collective-permute-start(bf16[320,512]{1,0:T(8,128)(2,1)S(1)} %get-tuple-element.23.latent), channel_id=1, source_target_pairs={{1,0},{2,1},{3,2},{4,3},{5,4},{6,5},{7,6},{8,7},{9,8},{10,9},{11,1... | collective-permute-start | bytes 983048 | tf_op jit(solution)/shard_map/ppermute | solution.py:25
  17.6 0.2 ready.1
  17.8 0.0 copy-start.5
  17.9 0.0 copy-start.11
  17.9 0.0 copy-start.12
  17.9 0.0 copy-start.16
  17.9 0.0 copy-start.17
  17.9 4.6 %own.1 = (bf16[8,320,512]{2,1,0:T(8,128)(2,1)S(1)}, f32[320,512]{1,0:T(8,128)S(1)}, f32[320,512]{1,0:T(8,128)S(1)}) custom-call(bf16[320,512]{1,0:T(8,128)(2,1)S(1)} %get-tuple-element.23.latent, bf16[1536,512]{1,0:T(8,128)(2,1)S(1)} %copy-done.9, bf16[4,2560]{1,0:T(4,128)(2,1)S(1)} %copy-done.13, bf16[4,512]{1,0:T(4,128)(2,1)S(1)} %copy-done.15, ...), custom_call_target="tpu_custom_call" | custom-call | flops 2181038080 | bytes 10485760 | tf_op jit(solution)/shard_map/own/pallas_call | solution.py:357
  22.6 6.9 %mesh.1 = (bf16[320,512]{1,0:T(8,128)(2,1)S(1)}, bf16[16,384]{1,0:T(8,128)(2,1)S(1)}) custom-call(bf16[320,512]{1,0:T(8,128)(2,1)S(1)} %collective-permute-done.3.low, bf16[320,512]{1,0:T(8,128)(2,1)S(1)} %collective-permute-done.4.high, bf16[320,512]{1,0:T(8,128)(2,1)S(1)} %get-tuple-element.23.latent, bf16[1536,512]{1,0:T(8,128)(2,1)S(1)} %copy-done.9, ...), custom_call_target="tpu_custom_call" | custom-call | flops 2516582400 | bytes 10485760 | tf_op jit(solution)/shard_map/mesh/pallas_call | solution.py:357
  29.5 0.5 %collective-permute-start.5 = (bf16[16,384]{1,0:T(8,128)(2,1)S(1)}, bf16[16,384]{1,0:T(8,128)(2,1)S(1)}, u32[]{:S(2)}, u32[]{:S(2)}) collective-permute-start(bf16[16,384]{1,0:T(8,128)(2,1)S(1)} %get-tuple-element.30.f_0), channel_id=1, source_target_pairs={{15,0},{0,1},{1,2},{2,3},{3,4},{4,5},{5,6},{6,7},{7,8},{8,9},{9,10... | collective-permute-start | bytes 36872 | tf_op jit(solution)/shard_map/ppermute | solution.py:25
  30.0 2.4 %collective-permute-start.7 = (bf16[16,384]{1,0:T(8,128)(2,1)S(1)}, bf16[16,384]{1,0:T(8,128)(2,1)S(1)}, u32[]{:S(2)}, u32[]{:S(2)}) collective-permute-start(bf16[16,384]{1,0:T(8,128)(2,1)S(1)} %get-tuple-element.30.f_0), channel_id=1, source_target_pairs={{13,0},{14,1},{15,2},{0,3},{1,4},{2,5},{3,6},{4,7},{5,8},{6,9},{7,... | collective-permute-start | bytes 36872 | tf_op jit(solution)/shard_map/ppermute | solution.py:25
  32.4 2.4 %collective-permute-start.8 = (bf16[16,384]{1,0:T(8,128)(2,1)S(1)}, bf16[16,384]{1,0:T(8,128)(2,1)S(1)}, u32[]{:S(2)}, u32[]{:S(2)}) collective-permute-start(bf16[16,384]{1,0:T(8,128)(2,1)S(1)} %get-tuple-element.30.f_0), channel_id=1, source_target_pairs={{2,0},{3,1},{4,2},{5,3},{6,4},{7,5},{8,6},{9,7},{10,8},{11,9},{12,... | collective-permute-start | bytes 36872 | tf_op jit(solution)/shard_map/ppermute | solution.py:25
  34.7 0.7 %collective-permute-start.9 = (bf16[16,384]{1,0:T(8,128)(2,1)S(1)}, bf16[16,384]{1,0:T(8,128)(2,1)S(1)}, u32[]{:S(2)}, u32[]{:S(2)}) collective-permute-start(bf16[16,384]{1,0:T(8,128)(2,1)S(1)} %get-tuple-element.30.f_0), channel_id=1, source_target_pairs={{1,0},{2,1},{3,2},{4,3},{5,4},{6,5},{7,6},{8,7},{9,8},{10,9},{11,1... | collective-permute-start | bytes 36872 | tf_op jit(solution)/shard_map/ppermute | solution.py:25
  35.4 1.4 %decode.1 = bf16[227,512]{1,0:T(8,128)(2,1)} custom-call(bf16[320,512]{1,0:T(8,128)(2,1)S(1)} %get-tuple-element.28.node_new, bf16[227,512]{1,0:T(8,128)(2,1)S(1)} %bitcast.23, s32[1,512]{1,0:T(1,128)S(1)} %bitcast.27, bf16[227,512]{1,0:T(8,128)(2,1)S(1)} %bitcast.15, f32[1,512]{1,0:T(1,128)S(1)} %get-tuple-element.29.surface), custom_call_target="tpu_custom_call" | custom-call | flops 223150080 | bytes 1048576 | tf_op jit(solution)/shard_map/decode/pallas_call | solution.py:357
  36.8 0.0 collective-permute-done.9.f_p1
  36.8 1.3 %ocean.1 = f32[9,8,384]{2,1,0:T(8,128)} custom-call(bf16[16,384]{1,0:T(8,128)(2,1)S(1)} %collective-permute-done.5.f_m1, bf16[16,384]{1,0:T(8,128)(2,1)S(1)} %collective-permute-done.6.f_m2, bf16[16,384]{1,0:T(8,128)(2,1)S(1)} %collective-permute-done.7.f_m3, bf16[16,384]{1,0:T(8,128)(2,1)S(1)} %collective-permute-done.8.f_p2, ...), custom_call_target="tpu_custom_call" | custom-call | bytes 4194304 | tf_op jit(solution)/shard_map/ocean/pallas_call | solution.py:357
  (32 shorter events, 0.1 us)
Async XLA Ops:
  0.6 11.4 %copy-start = (bf16[512,227]{0,1:T(8,128)(2,1)S(1)}, bf16[512,227]{0,1:T(8,128)(2,1)}, u32[]{:S(2)}) copy-start(bf16[512,227]{0,1:T(8,128)(2,1)} %param.20) | copy-start | bytes 697348
  0.6 11.4 %copy-start.4 = (bf16[227,512]{1,0:T(8,128)(2,1)S(1)}, bf16[227,512]{1,0:T(8,128)(2,1)}, u32[]{:S(2)}) copy-start(bf16[227,512]{1,0:T(8,128)(2,1)} %w_encode.1) | copy-start | bytes 697348
  0.7 11.4 %copy-start.7 = (s32[512]{0:T(512)S(1)}, s32[512]{0:T(512)}, u32[]{:S(2)}) copy-start(s32[512]{0:T(512)} %param.24) | copy-start | bytes 6148
  0.7 11.4 %copy-start.8 = (s32[1,4,192]{2,1,0:T(4,128)S(1)}, s32[1,4,192]{2,1,0:T(4,128)}, u32[]{:S(2)}) copy-start(s32[1,4,192]{2,1,0:T(4,128)} %param.29) | copy-start | bytes 9220
  2.0 10.0 %collective-permute-start = (bf16[112,384]{1,0:T(8,128)(2,1)S(1)}, bf16[112,384]{1,0:T(8,128)(2,1)S(1)}, u32[]{:S(2)}, u32[]{:S(2)}) collective-permute-start(bf16[112,384]{1,0:T(8,128)(2,1)S(1)} %get-tuple-element.20), channel_id=1, source_target_pairs={{15,0},{0,1},{1,2},{2,3},{3,4},{4,5},{5,6},{6,7},{7,8},{8,9},{9,10... | collective-permute-start | bytes 258056 | tf_op jit(solution)/shard_map/ppermute | solution.py:25
  2.5 9.5 %collective-permute-start.1 = (bf16[112,384]{1,0:T(8,128)(2,1)S(1)}, bf16[112,384]{1,0:T(8,128)(2,1)S(1)}, u32[]{:S(2)}, u32[]{:S(2)}) collective-permute-start(bf16[112,384]{1,0:T(8,128)(2,1)S(1)} %get-tuple-element.21), channel_id=1, source_target_pairs={{1,0},{2,1},{3,2},{4,3},{5,4},{6,5},{7,6},{8,7},{9,8},{10,9},{11,1... | collective-permute-start | bytes 258056 | tf_op jit(solution)/shard_map/ppermute | solution.py:25
  7.6 4.4 %collective-permute-start.2 = (bf16[16,384]{1,0:T(8,128)(2,1)S(1)}, bf16[16,384]{1,0:T(8,128)(2,1)S(1)}, u32[]{:S(2)}, u32[]{:S(2)}) collective-permute-start(bf16[16,384]{1,0:T(8,128)(2,1)S(1)} %get-tuple-element.22.own), channel_id=1, source_target_pairs={{2,0},{3,1},{4,2},{5,3},{6,4},{7,5},{8,6},{9,7},{10,8},{11,9},{12,... | collective-permute-start | bytes 36872 | tf_op jit(solution)/shard_map/ppermute | solution.py:25
  9.8 7.8 %copy-start.1 = (f32[8,9,384]{2,0,1:T(8,128)S(1)}, f32[8,9,384]{2,0,1:T(8,128)}, u32[]{:S(2)}) copy-start(f32[8,9,384]{2,0,1:T(8,128)} %param.25) | copy-start | bytes 331780
  9.8 7.8 %copy-start.2 = (f32[8,9,384]{2,0,1:T(8,128)S(1)}, f32[8,9,384]{2,0,1:T(8,128)}, u32[]{:S(2)}) copy-start(f32[8,9,384]{2,0,1:T(8,128)} %param.26) | copy-start | bytes 331780
  9.8 7.8 %copy-start.3 = (f32[8,9,384]{2,0,1:T(8,128)S(1)}, f32[8,9,384]{2,0,1:T(8,128)}, u32[]{:S(2)}) copy-start(f32[8,9,384]{2,0,1:T(8,128)} %param.27) | copy-start | bytes 331780
  9.8 7.8 %copy-start.6 = (s32[9,384]{1,0:T(8,128)S(1)}, s32[9,384]{1,0:T(8,128)}, u32[]{:S(2)}) copy-start(s32[9,384]{1,0:T(8,128)} %mask.1) | copy-start | bytes 41476
  9.8 8.0 %copy-start.9 = (bf16[1536,512]{1,0:T(8,128)(2,1)S(1)}, bf16[1536,512]{1,0:T(8,128)(2,1)}, u32[]{:S(2)}) copy-start(bf16[1536,512]{1,0:T(8,128)(2,1)} %w_in.3) | copy-start | bytes 4718596
  9.8 8.0 %copy-start.10 = (bf16[1024,512]{1,0:T(8,128)(2,1)S(1)}, bf16[1024,512]{1,0:T(8,128)(2,1)}, u32[]{:S(2)}) copy-start(bf16[1024,512]{1,0:T(8,128)(2,1)} %w_node_in.3) | copy-start | bytes 3145732
  9.8 8.0 %copy-start.13 = (bf16[4,2560]{1,0:T(4,128)(2,1)S(1)}, bf16[4,2560]{1,0:T(4,128)(2,1)}, u32[]{:S(2)}) copy-start(bf16[4,2560]{1,0:T(4,128)(2,1)} %geometry.1) | copy-start | bytes 61444
  9.8 8.0 %copy-start.14 = (s32[320,8]{0,1:T(8,128)S(1)}, s32[320,8]{0,1:T(8,128)}, u32[]{:S(2)}) copy-start(s32[320,8]{0,1:T(8,128)} %param.23) | copy-start | bytes 30724
  9.9 8.0 %copy-start.15 = (bf16[4,512]{1,0:T(4,128)(2,1)S(1)}, bf16[4,512]{1,0:T(4,128)(2,1)}, u32[]{:S(2)}) copy-start(bf16[4,512]{1,0:T(4,128)(2,1)} %w_geometry.1) | copy-start | bytes 12292
  13.1 9.4 %collective-permute-start.3 = (bf16[320,512]{1,0:T(8,128)(2,1)S(1)}, bf16[320,512]{1,0:T(8,128)(2,1)S(1)}, u32[]{:S(2)}, u32[]{:S(2)}) collective-permute-start(bf16[320,512]{1,0:T(8,128)(2,1)S(1)} %get-tuple-element.23.latent), channel_id=1, source_target_pairs={{15,0},{0,1},{1,2},{2,3},{3,4},{4,5},{5,6},{6,7},{7,8},{8,9},{9,10... | collective-permute-start | bytes 983048 | tf_op jit(solution)/shard_map/ppermute | solution.py:25
  13.2 9.4 %collective-permute-start.4 = (bf16[320,512]{1,0:T(8,128)(2,1)S(1)}, bf16[320,512]{1,0:T(8,128)(2,1)S(1)}, u32[]{:S(2)}, u32[]{:S(2)}) collective-permute-start(bf16[320,512]{1,0:T(8,128)(2,1)S(1)} %get-tuple-element.23.latent), channel_id=1, source_target_pairs={{1,0},{2,1},{3,2},{4,3},{5,4},{6,5},{7,6},{8,7},{9,8},{10,9},{11,1... | collective-permute-start | bytes 983048 | tf_op jit(solution)/shard_map/ppermute | solution.py:25
  17.8 4.7 %copy-start.5 = (bf16[512,227]{0,1:T(8,128)(2,1)S(1)}, bf16[512,227]{0,1:T(8,128)(2,1)}, u32[]{:S(2)}) copy-start(bf16[512,227]{0,1:T(8,128)(2,1)} %param.37) | copy-start | bytes 697348
  17.9 4.7 %copy-start.11 = (bf16[512,512]{1,0:T(8,128)(2,1)S(1)}, bf16[512,512]{1,0:T(8,128)(2,1)}, u32[]{:S(2)}) copy-start(bf16[512,512]{1,0:T(8,128)(2,1)} %w_out.1) | copy-start | bytes 1572868
  17.9 4.7 %copy-start.12 = (bf16[512,512]{1,0:T(8,128)(2,1)S(1)}, bf16[512,512]{1,0:T(8,128)(2,1)}, u32[]{:S(2)}) copy-start(bf16[512,512]{1,0:T(8,128)(2,1)} %w_node_out.1) | copy-start | bytes 1572868
  17.9 4.7 %copy-start.16 = (f32[512]{0:T(512)S(1)}, f32[512]{0:T(512)}, u32[]{:S(2)}) copy-start(f32[512]{0:T(512)} %param.38) | copy-start | bytes 6148
  17.9 4.7 %copy-start.17 = (f32[512]{0:T(512)S(1)}, f32[512]{0:T(512)}, u32[]{:S(2)}) copy-start(f32[512]{0:T(512)} %param.39) | copy-start | bytes 6148
  29.5 7.3 %collective-permute-start.5 = (bf16[16,384]{1,0:T(8,128)(2,1)S(1)}, bf16[16,384]{1,0:T(8,128)(2,1)S(1)}, u32[]{:S(2)}, u32[]{:S(2)}) collective-permute-start(bf16[16,384]{1,0:T(8,128)(2,1)S(1)} %get-tuple-element.30.f_0), channel_id=1, source_target_pairs={{15,0},{0,1},{1,2},{2,3},{3,4},{4,5},{5,6},{6,7},{7,8},{8,9},{9,10... | collective-permute-start | bytes 36872 | tf_op jit(solution)/shard_map/ppermute | solution.py:25
  30.0 6.8 %collective-permute-start.6 = (bf16[16,384]{1,0:T(8,128)(2,1)S(1)}, bf16[16,384]{1,0:T(8,128)(2,1)S(1)}, u32[]{:S(2)}, u32[]{:S(2)}) collective-permute-start(bf16[16,384]{1,0:T(8,128)(2,1)S(1)} %get-tuple-element.30.f_0), channel_id=1, source_target_pairs={{14,0},{15,1},{0,2},{1,3},{2,4},{3,5},{4,6},{5,7},{6,8},{7,9},{8,1... | collective-permute-start | bytes 36872 | tf_op jit(solution)/shard_map/ppermute | solution.py:25
  30.0 6.8 %collective-permute-start.7 = (bf16[16,384]{1,0:T(8,128)(2,1)S(1)}, bf16[16,384]{1,0:T(8,128)(2,1)S(1)}, u32[]{:S(2)}, u32[]{:S(2)}) collective-permute-start(bf16[16,384]{1,0:T(8,128)(2,1)S(1)} %get-tuple-element.30.f_0), channel_id=1, source_target_pairs={{13,0},{14,1},{15,2},{0,3},{1,4},{2,5},{3,6},{4,7},{5,8},{6,9},{7,... | collective-permute-start | bytes 36872 | tf_op jit(solution)/shard_map/ppermute | solution.py:25
  32.4 4.4 %collective-permute-start.8 = (bf16[16,384]{1,0:T(8,128)(2,1)S(1)}, bf16[16,384]{1,0:T(8,128)(2,1)S(1)}, u32[]{:S(2)}, u32[]{:S(2)}) collective-permute-start(bf16[16,384]{1,0:T(8,128)(2,1)S(1)} %get-tuple-element.30.f_0), channel_id=1, source_target_pairs={{2,0},{3,1},{4,2},{5,3},{6,4},{7,5},{8,6},{9,7},{10,8},{11,9},{12,... | collective-permute-start | bytes 36872 | tf_op jit(solution)/shard_map/ppermute | solution.py:25
  34.7 2.1 %collective-permute-start.9 = (bf16[16,384]{1,0:T(8,128)(2,1)S(1)}, bf16[16,384]{1,0:T(8,128)(2,1)S(1)}, u32[]{:S(2)}, u32[]{:S(2)}) collective-permute-start(bf16[16,384]{1,0:T(8,128)(2,1)S(1)} %get-tuple-element.30.f_0), channel_id=1, source_target_pairs={{1,0},{2,1},{3,2},{4,3},{5,4},{6,5},{7,6},{8,7},{9,8},{10,9},{11,1... | collective-permute-start | bytes 36872 | tf_op jit(solution)/shard_map/ppermute | solution.py:25

commit v6 on v5

--- a/solution.py
+++ b/solution.py
@@ -20,9 +20,22 @@
 AXES = ("tile", "comp")
 
 
-def shifted(block, distance):
+INNER, OUTER = (1, -1), (-1, 1)
+NEAR, FAR = (2, 2, -2, -2), (-2, -2, 2, 2)
+
+
+def sent(block, offsets):
     count = lax.axis_size(AXES)
-    return lax.ppermute(block, AXES, [((i - distance) % count, i) for i in range(count)])
+    route = [(i, (i + offsets[i % len(offsets)]) % count) for i in range(count)]
+    return lax.ppermute(block, AXES, route)
+
+
+def is_even():
+    return lax.axis_index("comp") == 0
+
+
+def pair_is_even():
+    return lax.rem(lax.axis_index("tile"), 2) == 0
 
 
 def dot(a, b):
@@ -53,7 +66,7 @@
 
 
 def pack_kernel(
-    counts_in, heat_in, east_in, north_in, mask_in, low_out, high_out, blocks_out,
+    counts_in, heat_in, east_in, north_in, mask_in, inner_out, outer_out, blocks_out,
     counts, heat, east, north, mask, sems,
 ):
     copies = started(
@@ -96,10 +109,14 @@
         [mean_high, mean - mean_high, flags, held, jnp.zeros((4, rows), F32)], axis=0
     )
     blank = jnp.zeros((4, rows), F32)
-    for out, begin in ((low_out, 0), (high_out, columns - EDGE)):
+    ends = []
+    for begin in (0, columns - EDGE):
         pieces = [source[c] for source in (heat, east, north) for c in range(begin, begin + EDGE)]
         pieces += [wet[begin : begin + EDGE], blank, bundle]
-        out[...] = jnp.concatenate(pieces, axis=0).astype(BF16)
+        ends.append(jnp.concatenate(pieces, axis=0))
+    even = is_even()
+    inner_out[...] = jnp.where(even, ends[1], ends[0]).astype(BF16)
+    outer_out[...] = jnp.where(even, ends[0], ends[1]).astype(BF16)
     blocks_out[...] = jnp.concatenate([bundle, jnp.zeros((8, rows), F32)], axis=0).astype(BF16)
 
 
@@ -147,14 +164,16 @@
 
 
 def latent_kernel(
-    below, above, far, own, points, atmosphere, w_encode, grid_row, plain,
+    outer, far, inner, own, points, atmosphere, w_encode, grid_row, plain,
     latent_out, surface_out, placed_out,
 ):
+    pair = [x[...].astype(F32)[-8:] for x in (inner, outer)]
+    even = is_even()
     parts = [
         far[...].astype(F32)[:8],
-        above[...].astype(F32)[-8:],
+        jnp.where(even, pair[0], pair[1]),
         own[...].astype(F32)[:8],
-        below[...].astype(F32)[-8:],
+        jnp.where(even, pair[1], pair[0]),
     ]
     starts = [0, before(parts[1], 1), before(parts[2], 2), before(parts[3], 3)]
     placed = jnp.concatenate(rolled_points(points, starts), axis=1)
@@ -216,19 +235,22 @@
 
 
 def mesh_kernel(
-    low, high, latent, w_in, w_out, pre, base, node_part, neighbours, w_node_in, w_node_out, w_decode,
+    inner, outer, latent, w_in, w_out, pre, base, node_part, neighbours, w_node_in, w_node_out, w_decode,
     gain_edge, gain_node, grid_row, atmosphere, placed, node_out, flux_out, sender, total,
 ):
     nodes, features = latent.shape
     w_sender = w_in[features : 2 * features]
-    sender[:nodes] = dot(low[...], w_sender).astype(BF16)
-    sender[nodes:] = dot(high[...], w_sender).astype(BF16)
+    sender[:nodes] = dot(inner[...], w_sender).astype(BF16)
+    sender[nodes:] = dot(outer[...], w_sender).astype(BF16)
+    below = jnp.where(is_even(), nodes, 0)
+    above = nodes - below
     listed = listed_slots(neighbours)
     total[...] = jnp.zeros((nodes, features), F32)
 
     def step(k, carry):
         at = slot_senders(listed, k)
-        place = jnp.where(at < nodes, at, jnp.where(at >= 2 * nodes, at - nodes, -1))
+        place = jnp.where(at < nodes, at + below, jnp.where(at >= 2 * nodes, at - 2 * nodes + above, -1))
+        place = jnp.where(at < 3 * nodes, place, -1)
         match = one_hot(iota((nodes, 2 * nodes), 1) == place)
         hidden = silu(pre[k].astype(F32) + dot(match, sender[...])).astype(BF16)
         centred, scale = normal(dot(hidden, w_out[...]))
@@ -269,10 +291,12 @@
     state_out[...] = (state + dot(change_high, member) + dot(change_low, member)).astype(BF16)
 
 
-def ready_kernel(heat, east, north, mask, low, high, field_out, wet_out, px_out, qx_out, py_out, qy_out, mix_out):
+def ready_kernel(heat, east, north, mask, inner, outer, field_out, wet_out, px_out, qx_out, py_out, qy_out, mix_out):
     columns, rows = mask.shape
     levels = heat.shape[1]
-    below, above = low[...].astype(F32), high[...].astype(F32)
+    pair = inner[...].astype(F32), outer[...].astype(F32)
+    even = is_even()
+    below, above = jnp.where(even, pair[1], pair[0]), jnp.where(even, pair[0], pair[1])
     own_wet = mask[...].astype(F32)
 
     def wide(source, at):
@@ -304,12 +328,23 @@
         qy_out[c] = opened * (face - COEFF_H)
 
 
-def ocean_kernel(f_m1, f_m2, f_m3, f_p2, f_p1, f_0, field_in, wet, px, qx, py, qy, mix, out):
+def ocean_kernel(third, far, outer, near, inner, here_flux, field_in, wet, px, qx, py, qy, mix, out):
     count, levels, rows = field_in.shape
     columns = count - 2 * EDGE
     triples = columns // 3
     span = rows // 3
-    fluxes = [f[...].astype(F32) for f in (f_m3, f_m2, f_m1, f_0, f_p1, f_p2)]
+    third, far, outer, near, inner, here_flux = (
+        x[...].astype(F32) for x in (third, far, outer, near, inner, here_flux)
+    )
+    even, pair_even = is_even(), pair_is_even()
+    fluxes = [
+        third,
+        jnp.where(pair_even, far, near),
+        jnp.where(even, outer, inner),
+        here_flux,
+        jnp.where(even, inner, outer),
+        jnp.where(pair_even, near, far),
+    ]
 
     def gathered(begin):
         return sum(fluxes[begin + o][o : o + 1] for o in range(W))
@@ -401,7 +436,7 @@
     ends = (3 * levels * EDGE + 16, rows)
     few = (16, rows)
     own_ocean = (columns, levels, rows)
-    low, high, blocks = call(
+    to_inner, to_outer, blocks = call(
         pack_kernel,
         [(ends, BF16), (ends, BF16), (few, BF16)],
         [intersection_counts, heat, east, north, ocean_mask],
@@ -416,9 +451,9 @@
         ],
         name="pack",
     )
-    below = shifted(high, 1)
-    above = shifted(low, -1)
-    far = shifted(blocks, -2)
+    outer = sent(to_outer, OUTER)
+    far = sent(blocks, (-2,))
+    inner = sent(to_inner, INNER)
     (plain,) = call(
         plain_kernel,
         [((nodes, features), F32)],
@@ -438,11 +473,11 @@
     latent, surface, placed = call(
         latent_kernel,
         [((nodes, features), BF16), ((1, n_points), F32), ((1, W * rows), jnp.int32)],
-        [below, above, far, blocks, intersection_points[0], atmosphere_t, w_encode, grid_row, plain],
+        [outer, far, inner, blocks, intersection_points[0], atmosphere_t, w_encode, grid_row, plain],
         name="latents",
     )
-    latent_low = shifted(latent, 1)
-    latent_high = shifted(latent, -1)
+    latent_inner = sent(latent, INNER)
+    latent_outer = sent(latent, OUTER)
     pre, base, node_part = call(
         own_kernel,
         [((K, nodes, features), BF16), ((nodes, features), F32), ((nodes, features), F32)],
@@ -456,7 +491,7 @@
     ready = call(
         ready_kernel,
         [(wide, F32)] * 7,
-        [heat, east, north, ocean_mask, below, above],
+        [heat, east, north, ocean_mask, inner, outer],
         bytes_accessed=4 << 20,
         name="ready",
     )
@@ -464,7 +499,7 @@
         mesh_kernel,
         [((nodes, features), BF16), (few, BF16)],
         [
-            latent_low, latent_high, latent, w_edge_in, w_edge_out, pre, base, node_part, slots,
+            latent_inner, latent_outer, latent, w_edge_in, w_edge_out, pre, base, node_part, slots,
             w_node_in, w_node_out, decode_t, gain_edge.reshape(1, features),
             gain_node.reshape(1, features), grid_row, atmosphere_t, placed,
         ],
@@ -473,9 +508,7 @@
         bytes_accessed=10 << 20,
         name="mesh",
     )
-    sent = {d: shifted(flux, d) for d in (1, 2, 3, -1, -2)}
-    sent[0] = flux
-    arrived = [sent[d] for d in (1, 2, 3, -2, -1, 0)]
+    arrived = [sent(flux, route) for route in ((3,), FAR, OUTER, NEAR, INNER)]
     (state,) = call(
         decode_kernel,
         [((channels, n_points), BF16)],
@@ -486,7 +519,7 @@
     (ocean_new,) = call(
         ocean_kernel,
         [(own_ocean, F32)],
-        [*arrived, *ready],
+        [*arrived, flux, *ready],
         bytes_accessed=4 << 20,
         name="ocean",
     )

time: 38.9 us -> 41.6 us (1.069); the launches traced: 38.1 us -> 41.4 us
  waiting for transfers between devices: 0.03 us -> 5.17 us
  starting transfers between devices: 18.2 us -> 16.2 us
    ppermute x10, waiting for transfers between devices: 0.03 us -> 5.17 us  [sent(): return lax.ppermute(block, AXES, route)]
    ppermute x10, starting transfers between devices: 18.2 us -> 16.2 us  [sent(): return lax.ppermute(block, AXES, route)]
  transfers between devices with their start and end apart: 10 -> 10, of which waited for: 0 -> 3; matrix products, arithmetic and copies ran while one was open for 0% -> 0% of each run, Pallas kernels for 22% -> 20%
where the time goes in v6:
time: 41.6 us; the launch traced here: 41.4 us
  Pallas kernels  19 us (46%)
  starting transfers between devices  16.2 us (39%)
  waiting for transfers between devices  5.17 us (12%)
  between operations  0.9 us (2%)
    pallas_call x8, Pallas kernels, call(): pl.pallas_call(kernel, out_shape=[jax.ShapeDtypeStruct(s, t) for s, t in...  19 us
    ppermute x10, starting transfers between devices, sent(): return lax.ppermute(block, AXES, route)  16.2 us
    ppermute x10, waiting for transfers between devices, sent(): return lax.ppermute(block, AXES, route)  5.17 us
  transfers between devices with their start and end apart: 10, of which 3 were waited for; matrix products, arithmetic and copies ran while one was open for 0% of the time, Pallas kernels for 20%

profile of v6, /device:TPU:0, one launch (start us, length us, event | category | flops | bytes accessed | tf_op | source)
XLA Modules:
  0.0 41.4 jit_solution(6890139510395890052)
XLA Ops:
  0.6 0.0 copy-start
  0.6 0.0 copy-start.4
  0.7 0.0 copy-start.7
  0.7 1.4 %pack.1 = (bf16[112,384]{1,0:T(8,128)(2,1)S(1)}, bf16[112,384]{1,0:T(8,128)(2,1)S(1)}, bf16[16,384]{1,0:T(8,128)(2,1)S(1)}) custom-call(s32[1,4]{1,0:T(1,128)} %counts_in.1, f32[9,8,384]{2,1,0:T(8,128)} %bitcast.16, f32[9,8,384]{2,1,0:T(8,128)} %bitcast.18, f32[9,8,384]{2,1,0:T(8,128)} %bitcast.20, s32[9,384]{1,0:T(8,128)} %mask.1), custom_call_target="tpu_custom_call" | custom-call | bytes 1048576 | tf_op jit(solution)/shard_map/pack/pallas_call | solution.py:392
  2.0 5.5 %collective-permute-start = (bf16[112,384]{1,0:T(8,128)(2,1)S(1)}, bf16[112,384]{1,0:T(8,128)(2,1)S(1)}, u32[]{:S(2)}, u32[]{:S(2)}) collective-permute-start(bf16[112,384]{1,0:T(8,128)(2,1)S(1)} %get-tuple-element.20), channel_id=1, source_target_pairs={{0,15},{1,2},{2,1},{3,4},{4,3},{5,6},{6,5},{7,8},{8,7},{9,10},{10,... | collective-permute-start | bytes 258056 | tf_op jit(solution)/shard_map/ppermute | solution.py:30
  7.5 0.0 collective-permute-start.2
  7.5 0.7 %collective-permute-start.1 = (bf16[16,384]{1,0:T(8,128)(2,1)S(1)}, bf16[16,384]{1,0:T(8,128)(2,1)S(1)}, u32[]{:S(2)}, u32[]{:S(2)}) collective-permute-start(bf16[16,384]{1,0:T(8,128)(2,1)S(1)} %get-tuple-element.21.own), channel_id=1, source_target_pairs={{0,14},{1,15},{2,0},{3,1},{4,2},{5,3},{6,4},{7,5},{8,6},{9,7},{10,... | collective-permute-start | bytes 36872 | tf_op jit(solution)/shard_map/ppermute | solution.py:30
  8.2 0.0 copy-start.9
  8.2 0.0 copy-start.10
  8.3 0.0 copy-start.13
  8.3 0.0 copy-start.14
  8.3 0.0 copy-start.15
  8.3 2.1 %plain.1 = f32[320,512]{1,0:T(8,128)S(1)} custom-call(bf16[227,512]{1,0:T(8,128)(2,1)} %bitcast.12, bf16[227,512]{1,0:T(8,128)(2,1)} %w_encode.1, s32[1,512]{1,0:T(1,128)} %bitcast.24, bf16[320,512]{1,0:T(8,128)(2,1)} %mesh_state_in.1), custom_call_target="tpu_custom_call" | custom-call | flops 1342177280 | bytes 8388608 | tf_op jit(solution)/shard_map/plain/pallas_call | solution.py:392
  10.4 0.8 %collective-permute-done.1.far = bf16[16,384]{1,0:T(8,128)(2,1)S(1)} collective-permute-done((bf16[16,384]{1,0:T(8,128)(2,1)S(1)}, bf16[16,384]{1,0:T(8,128)(2,1)S(1)}, u32[]{:S(2)}, u32[]{:S(2)}) %collective-permute-start.1) | collective-permute-done | bytes 12320 | tf_op jit(solution)/shard_map/ppermute | solution.py:30
  11.3 1.1 %latents.1 = (bf16[320,512]{1,0:T(8,128)(2,1)S(1)}, f32[1,512]{1,0:T(1,128)S(1)}, s32[1,1536]{1,0:T(1,128)S(1)}) custom-call(bf16[112,384]{1,0:T(8,128)(2,1)S(1)} %collective-permute-done.outer, bf16[16,384]{1,0:T(8,128)(2,1)S(1)} %collective-permute-done.1.far, bf16[112,384]{1,0:T(8,128)(2,1)S(1)} %collective-permute-done.2.inner, ...), custom_call_target="tpu_custom_call" | custom-call | bytes 1048576 | tf_op jit(solution)/shard_map/latents/pallas_call | solution.py:392
  12.3 0.1 collective-permute-start.3
  12.4 3.8 %collective-permute-start.4 = (bf16[320,512]{1,0:T(8,128)(2,1)S(1)}, bf16[320,512]{1,0:T(8,128)(2,1)S(1)}, u32[]{:S(2)}, u32[]{:S(2)}) collective-permute-start(bf16[320,512]{1,0:T(8,128)(2,1)S(1)} %get-tuple-element.23.latent), channel_id=1, source_target_pairs={{0,15},{1,2},{2,1},{3,4},{4,3},{5,6},{6,5},{7,8},{8,7},{9,10},{10,... | collective-permute-start | bytes 983048 | tf_op jit(solution)/shard_map/ppermute | solution.py:30
  16.3 0.2 ready.1
  16.5 0.0 copy-start.5
  16.5 0.0 copy-start.11
  16.5 0.0 copy-start.12
  16.5 0.0 copy-start.16
  16.6 0.0 copy-start.17
  16.6 4.6 %own.1 = (bf16[8,320,512]{2,1,0:T(8,128)(2,1)S(1)}, f32[320,512]{1,0:T(8,128)S(1)}, f32[320,512]{1,0:T(8,128)S(1)}) custom-call(bf16[320,512]{1,0:T(8,128)(2,1)S(1)} %get-tuple-element.23.latent, bf16[1536,512]{1,0:T(8,128)(2,1)S(1)} %copy-done.9, bf16[4,2560]{1,0:T(4,128)(2,1)S(1)} %copy-done.13, bf16[4,512]{1,0:T(4,128)(2,1)S(1)} %copy-done.15, ...), custom_call_target="tpu_custom_call" | custom-call | flops 2181038080 | bytes 10485760 | tf_op jit(solution)/shard_map/own/pallas_call | solution.py:392
  21.2 0.0 collective-permute-done.3.inner
  21.2 0.6 %collective-permute-done.4.outer = bf16[320,512]{1,0:T(8,128)(2,1)S(1)} collective-permute-done((bf16[320,512]{1,0:T(8,128)(2,1)S(1)}, bf16[320,512]{1,0:T(8,128)(2,1)S(1)}, u32[]{:S(2)}, u32[]{:S(2)}) %collective-permute-start.4) | collective-permute-done | bytes 327712 | tf_op jit(solution)/shard_map/ppermute | solution.py:30
  21.8 7.0 %mesh.1 = (bf16[320,512]{1,0:T(8,128)(2,1)S(1)}, bf16[16,384]{1,0:T(8,128)(2,1)S(1)}) custom-call(bf16[320,512]{1,0:T(8,128)(2,1)S(1)} %collective-permute-done.3.inner, bf16[320,512]{1,0:T(8,128)(2,1)S(1)} %collective-permute-done.4.outer, bf16[320,512]{1,0:T(8,128)(2,1)S(1)} %get-tuple-element.23.latent, bf16[1536,512]{1,0:T(8,128)(2,1)S(1)} %copy-done.9, ...), custom_call_target="tpu_custom_call" | custom-call | flops 2516582400 | bytes 10485760 | tf_op jit(solution)/shard_map/mesh/pallas_call | solution.py:392
  28.8 5.5 %collective-permute-start.6 = (bf16[16,384]{1,0:T(8,128)(2,1)S(1)}, bf16[16,384]{1,0:T(8,128)(2,1)S(1)}, u32[]{:S(2)}, u32[]{:S(2)}) collective-permute-start(bf16[16,384]{1,0:T(8,128)(2,1)S(1)} %get-tuple-element.30.here_flux), channel_id=1, source_target_pairs={{0,14},{1,15},{2,4},{3,5},{4,2},{5,3},{6,8},{7,9},{8,6},{9,7},{10,... | collective-permute-start | bytes 36872 | tf_op jit(solution)/shard_map/ppermute | solution.py:30
  34.3 0.7 %collective-permute-start.8 = (bf16[16,384]{1,0:T(8,128)(2,1)S(1)}, bf16[16,384]{1,0:T(8,128)(2,1)S(1)}, u32[]{:S(2)}, u32[]{:S(2)}) collective-permute-start(bf16[16,384]{1,0:T(8,128)(2,1)S(1)} %get-tuple-element.30.here_flux), channel_id=1, source_target_pairs={{0,2},{1,3},{2,0},{3,1},{4,6},{5,7},{6,4},{7,5},{8,10},{9,11},{10,... | collective-permute-start | bytes 36872 | tf_op jit(solution)/shard_map/ppermute | solution.py:30
  34.9 1.4 %decode.1 = bf16[227,512]{1,0:T(8,128)(2,1)} custom-call(bf16[320,512]{1,0:T(8,128)(2,1)S(1)} %get-tuple-element.28.node_new, bf16[227,512]{1,0:T(8,128)(2,1)S(1)} %bitcast.23, s32[1,512]{1,0:T(1,128)S(1)} %bitcast.27, bf16[227,512]{1,0:T(8,128)(2,1)S(1)} %bitcast.15, f32[1,512]{1,0:T(1,128)S(1)} %get-tuple-element.29.surface), custom_call_target="tpu_custom_call" | custom-call | flops 223150080 | bytes 1048576 | tf_op jit(solution)/shard_map/decode/pallas_call | solution.py:392
  36.3 3.8 %collective-permute-done.7.outer = bf16[16,384]{1,0:T(8,128)(2,1)S(1)} collective-permute-done((bf16[16,384]{1,0:T(8,128)(2,1)S(1)}, bf16[16,384]{1,0:T(8,128)(2,1)S(1)}, u32[]{:S(2)}, u32[]{:S(2)}) %collective-permute-start.7) | collective-permute-done | bytes 12320 | tf_op jit(solution)/shard_map/ppermute | solution.py:30
  40.1 1.3 %ocean.1 = f32[9,8,384]{2,1,0:T(8,128)} custom-call(bf16[16,384]{1,0:T(8,128)(2,1)S(1)} %collective-permute-done.5.third, bf16[16,384]{1,0:T(8,128)(2,1)S(1)} %collective-permute-done.6.far, bf16[16,384]{1,0:T(8,128)(2,1)S(1)} %collective-permute-done.7.outer, bf16[16,384]{1,0:T(8,128)(2,1)S(1)} %collective-permute-done.8.near, ...), custom_call_target="tpu_custom_call" | custom-call | bytes 4194304 | tf_op jit(solution)/shard_map/ocean/pallas_call | solution.py:392
  (32 shorter events, 0.1 us)
Async XLA Ops:
  0.6 10.6 %copy-start = (bf16[512,227]{0,1:T(8,128)(2,1)S(1)}, bf16[512,227]{0,1:T(8,128)(2,1)}, u32[]{:S(2)}) copy-start(bf16[512,227]{0,1:T(8,128)(2,1)} %param.20) | copy-start | bytes 697348
  0.6 10.6 %copy-start.4 = (bf16[227,512]{1,0:T(8,128)(2,1)S(1)}, bf16[227,512]{1,0:T(8,128)(2,1)}, u32[]{:S(2)}) copy-start(bf16[227,512]{1,0:T(8,128)(2,1)} %w_encode.1) | copy-start | bytes 697348
  0.7 10.6 %copy-start.7 = (s32[512]{0:T(512)S(1)}, s32[512]{0:T(512)}, u32[]{:S(2)}) copy-start(s32[512]{0:T(512)} %param.24) | copy-start | bytes 6148
  0.7 10.6 %copy-start.8 = (s32[1,4,192]{2,1,0:T(4,128)S(1)}, s32[1,4,192]{2,1,0:T(4,128)}, u32[]{:S(2)}) copy-start(s32[1,4,192]{2,1,0:T(4,128)} %param.29) | copy-start | bytes 9220
  2.0 9.2 %collective-permute-start = (bf16[112,384]{1,0:T(8,128)(2,1)S(1)}, bf16[112,384]{1,0:T(8,128)(2,1)S(1)}, u32[]{:S(2)}, u32[]{:S(2)}) collective-permute-start(bf16[112,384]{1,0:T(8,128)(2,1)S(1)} %get-tuple-element.20), channel_id=1, source_target_pairs={{0,15},{1,2},{2,1},{3,4},{4,3},{5,6},{6,5},{7,8},{8,7},{9,10},{10,... | collective-permute-start | bytes 258056 | tf_op jit(solution)/shard_map/ppermute | solution.py:30
  7.5 3.7 %collective-permute-start.2 = (bf16[112,384]{1,0:T(8,128)(2,1)S(1)}, bf16[112,384]{1,0:T(8,128)(2,1)S(1)}, u32[]{:S(2)}, u32[]{:S(2)}) collective-permute-start(bf16[112,384]{1,0:T(8,128)(2,1)S(1)} %get-tuple-element.22), channel_id=1, source_target_pairs={{0,1},{1,0},{2,3},{3,2},{4,5},{5,4},{6,7},{7,6},{8,9},{9,8},{10,11... | collective-permute-start | bytes 258056 | tf_op jit(solution)/shard_map/ppermute | solution.py:30
  7.5 3.7 %collective-permute-start.1 = (bf16[16,384]{1,0:T(8,128)(2,1)S(1)}, bf16[16,384]{1,0:T(8,128)(2,1)S(1)}, u32[]{:S(2)}, u32[]{:S(2)}) collective-permute-start(bf16[16,384]{1,0:T(8,128)(2,1)S(1)} %get-tuple-element.21.own), channel_id=1, source_target_pairs={{0,14},{1,15},{2,0},{3,1},{4,2},{5,3},{6,4},{7,5},{8,6},{9,7},{10,... | collective-permute-start | bytes 36872 | tf_op jit(solution)/shard_map/ppermute | solution.py:30
  8.2 8.0 %copy-start.1 = (f32[8,9,384]{2,0,1:T(8,128)S(1)}, f32[8,9,384]{2,0,1:T(8,128)}, u32[]{:S(2)}) copy-start(f32[8,9,384]{2,0,1:T(8,128)} %param.25) | copy-start | bytes 331780
  8.2 8.0 %copy-start.2 = (f32[8,9,384]{2,0,1:T(8,128)S(1)}, f32[8,9,384]{2,0,1:T(8,128)}, u32[]{:S(2)}) copy-start(f32[8,9,384]{2,0,1:T(8,128)} %param.26) | copy-start | bytes 331780
  8.2 8.0 %copy-start.3 = (f32[8,9,384]{2,0,1:T(8,128)S(1)}, f32[8,9,384]{2,0,1:T(8,128)}, u32[]{:S(2)}) copy-start(f32[8,9,384]{2,0,1:T(8,128)} %param.27) | copy-start | bytes 331780
  8.2 8.0 %copy-start.6 = (s32[9,384]{1,0:T(8,128)S(1)}, s32[9,384]{1,0:T(8,128)}, u32[]{:S(2)}) copy-start(s32[9,384]{1,0:T(8,128)} %mask.1) | copy-start | bytes 41476
  8.2 8.2 %copy-start.9 = (bf16[1536,512]{1,0:T(8,128)(2,1)S(1)}, bf16[1536,512]{1,0:T(8,128)(2,1)}, u32[]{:S(2)}) copy-start(bf16[1536,512]{1,0:T(8,128)(2,1)} %w_in.3) | copy-start | bytes 4718596
  8.2 8.2 %copy-start.10 = (bf16[1024,512]{1,0:T(8,128)(2,1)S(1)}, bf16[1024,512]{1,0:T(8,128)(2,1)}, u32[]{:S(2)}) copy-start(bf16[1024,512]{1,0:T(8,128)(2,1)} %w_node_in.3) | copy-start | bytes 3145732
  8.3 8.2 %copy-start.13 = (bf16[4,2560]{1,0:T(4,128)(2,1)S(1)}, bf16[4,2560]{1,0:T(4,128)(2,1)}, u32[]{:S(2)}) copy-start(bf16[4,2560]{1,0:T(4,128)(2,1)} %geometry.1) | copy-start | bytes 61444
  8.3 8.2 %copy-start.14 = (s32[320,8]{0,1:T(8,128)S(1)}, s32[320,8]{0,1:T(8,128)}, u32[]{:S(2)}) copy-start(s32[320,8]{0,1:T(8,128)} %param.23) | copy-start | bytes 30724
  8.3 8.2 %copy-start.15 = (bf16[4,512]{1,0:T(4,128)(2,1)S(1)}, bf16[4,512]{1,0:T(4,128)(2,1)}, u32[]{:S(2)}) copy-start(bf16[4,512]{1,0:T(4,128)(2,1)} %w_geometry.1) | copy-start | bytes 12292
  12.3 8.9 %collective-permute-start.3 = (bf16[320,512]{1,0:T(8,128)(2,1)S(1)}, bf16[320,512]{1,0:T(8,128)(2,1)S(1)}, u32[]{:S(2)}, u32[]{:S(2)}) collective-permute-start(bf16[320,512]{1,0:T(8,128)(2,1)S(1)} %get-tuple-element.23.latent), channel_id=1, source_target_pairs={{0,1},{1,0},{2,3},{3,2},{4,5},{5,4},{6,7},{7,6},{8,9},{9,8},{10,11... | collective-permute-start | bytes 983048 | tf_op jit(solution)/shard_map/ppermute | solution.py:30
  12.4 9.4 %collective-permute-start.4 = (bf16[320,512]{1,0:T(8,128)(2,1)S(1)}, bf16[320,512]{1,0:T(8,128)(2,1)S(1)}, u32[]{:S(2)}, u32[]{:S(2)}) collective-permute-start(bf16[320,512]{1,0:T(8,128)(2,1)S(1)} %get-tuple-element.23.latent), channel_id=1, source_target_pairs={{0,15},{1,2},{2,1},{3,4},{4,3},{5,6},{6,5},{7,8},{8,7},{9,10},{10,... | collective-permute-start | bytes 983048 | tf_op jit(solution)/shard_map/ppermute | solution.py:30
  16.5 5.3 %copy-start.5 = (bf16[512,227]{0,1:T(8,128)(2,1)S(1)}, bf16[512,227]{0,1:T(8,128)(2,1)}, u32[]{:S(2)}) copy-start(bf16[512,227]{0,1:T(8,128)(2,1)} %param.37) | copy-start | bytes 697348
  16.5 5.2 %copy-start.11 = (bf16[512,512]{1,0:T(8,128)(2,1)S(1)}, bf16[512,512]{1,0:T(8,128)(2,1)}, u32[]{:S(2)}) copy-start(bf16[512,512]{1,0:T(8,128)(2,1)} %w_out.1) | copy-start | bytes 1572868
  16.5 5.2 %copy-start.12 = (bf16[512,512]{1,0:T(8,128)(2,1)S(1)}, bf16[512,512]{1,0:T(8,128)(2,1)}, u32[]{:S(2)}) copy-start(bf16[512,512]{1,0:T(8,128)(2,1)} %w_node_out.1) | copy-start | bytes 1572868
  16.5 5.2 %copy-start.16 = (f32[512]{0:T(512)S(1)}, f32[512]{0:T(512)}, u32[]{:S(2)}) copy-start(f32[512]{0:T(512)} %param.38) | copy-start | bytes 6148
  16.6 5.2 %copy-start.17 = (f32[512]{0:T(512)S(1)}, f32[512]{0:T(512)}, u32[]{:S(2)}) copy-start(f32[512]{0:T(512)} %param.39) | copy-start | bytes 6148
  28.8 7.5 %collective-permute-start.5 = (bf16[16,384]{1,0:T(8,128)(2,1)S(1)}, bf16[16,384]{1,0:T(8,128)(2,1)S(1)}, u32[]{:S(2)}, u32[]{:S(2)}) collective-permute-start(bf16[16,384]{1,0:T(8,128)(2,1)S(1)} %get-tuple-element.30.here_flux), channel_id=1, source_target_pairs={{0,3},{1,4},{2,5},{3,6},{4,7},{5,8},{6,9},{7,10},{8,11},{9,12},{10... | collective-permute-start | bytes 36872 | tf_op jit(solution)/shard_map/ppermute | solution.py:30
  28.8 7.5 %collective-permute-start.6 = (bf16[16,384]{1,0:T(8,128)(2,1)S(1)}, bf16[16,384]{1,0:T(8,128)(2,1)S(1)}, u32[]{:S(2)}, u32[]{:S(2)}) collective-permute-start(bf16[16,384]{1,0:T(8,128)(2,1)S(1)} %get-tuple-element.30.here_flux), channel_id=1, source_target_pairs={{0,14},{1,15},{2,4},{3,5},{4,2},{5,3},{6,8},{7,9},{8,6},{9,7},{10,... | collective-permute-start | bytes 36872 | tf_op jit(solution)/shard_map/ppermute | solution.py:30
  34.3 5.8 %collective-permute-start.7 = (bf16[16,384]{1,0:T(8,128)(2,1)S(1)}, bf16[16,384]{1,0:T(8,128)(2,1)S(1)}, u32[]{:S(2)}, u32[]{:S(2)}) collective-permute-start(bf16[16,384]{1,0:T(8,128)(2,1)S(1)} %get-tuple-element.30.here_flux), channel_id=1, source_target_pairs={{0,15},{1,2},{2,1},{3,4},{4,3},{5,6},{6,5},{7,8},{8,7},{9,10},{10,... | collective-permute-start | bytes 36872 | tf_op jit(solution)/shard_map/ppermute | solution.py:30
  34.3 5.8 %collective-permute-start.8 = (bf16[16,384]{1,0:T(8,128)(2,1)S(1)}, bf16[16,384]{1,0:T(8,128)(2,1)S(1)}, u32[]{:S(2)}, u32[]{:S(2)}) collective-permute-start(bf16[16,384]{1,0:T(8,128)(2,1)S(1)} %get-tuple-element.30.here_flux), channel_id=1, source_target_pairs={{0,2},{1,3},{2,0},{3,1},{4,6},{5,7},{6,4},{7,5},{8,10},{9,11},{10,... | collective-permute-start | bytes 36872 | tf_op jit(solution)/shard_map/ppermute | solution.py:30
  34.9 5.2 %collective-permute-start.9 = (bf16[16,384]{1,0:T(8,128)(2,1)S(1)}, bf16[16,384]{1,0:T(8,128)(2,1)S(1)}, u32[]{:S(2)}, u32[]{:S(2)}) collective-permute-start(bf16[16,384]{1,0:T(8,128)(2,1)S(1)} %get-tuple-element.30.here_flux), channel_id=1, source_target_pairs={{0,1},{1,0},{2,3},{3,2},{4,5},{5,4},{6,7},{7,6},{8,9},{9,8},{10,11... | collective-permute-start | bytes 36872 | tf_op jit(solution)/shard_map/ppermute | solution.py:30

commit v7 on v6

--- a/solution.py
+++ b/solution.py
@@ -47,7 +47,8 @@
 
 
 def silu(v):
-    return 0.5 * v * (1.0 + jnp.tanh(0.5 * v))
+    half = 0.5 * v
+    return half + half * jnp.tanh(half)
 
 
 def one_hot(test):
@@ -124,21 +125,7 @@
     return one_hot(iota((nodes, grid_row.shape[1]), 0) == grid_row)
 
 
-def plain_kernel(
-    atmosphere_in, w_encode_in, grid_row_in, mesh_state_in, plain_out,
-    atmosphere, w_encode, grid_row, mesh_state, sems,
-):
-    copies = started(
-        (
-            (grid_row_in, grid_row),
-            (atmosphere_in, atmosphere),
-            (w_encode_in, w_encode),
-            (mesh_state_in, mesh_state),
-        ),
-        sems,
-    )
-    for copy in copies:
-        copy.wait()
+def plain_kernel(atmosphere, w_encode, grid_row, mesh_state, plain_out):
     member = members(mesh_state.shape[0], grid_row[...])
     population = jnp.sum(member.astype(F32), axis=1, keepdims=True)
     state = atmosphere[...]
@@ -252,7 +239,7 @@
         place = jnp.where(at < nodes, at + below, jnp.where(at >= 2 * nodes, at - 2 * nodes + above, -1))
         place = jnp.where(at < 3 * nodes, place, -1)
         match = one_hot(iota((nodes, 2 * nodes), 1) == place)
-        hidden = silu(pre[k].astype(F32) + dot(match, sender[...])).astype(BF16)
+        hidden = silu((pre[k].astype(F32) + dot(match, sender[...])).astype(BF16))
         centred, scale = normal(dot(hidden, w_out[...]))
         total[...] += centred * jnp.where(at < 3 * nodes, scale, 0.0)
         return carry
@@ -328,23 +315,17 @@
         qy_out[c] = opened * (face - COEFF_H)
 
 
-def ocean_kernel(third, far, outer, near, inner, here_flux, field_in, wet, px, qx, py, qy, mix, out):
+def ocean_kernel(before_1, before_3, far, after_1, near, here_flux, field_in, wet, px, qx, py, qy, mix, out):
     count, levels, rows = field_in.shape
     columns = count - 2 * EDGE
     triples = columns // 3
     span = rows // 3
-    third, far, outer, near, inner, here_flux = (
-        x[...].astype(F32) for x in (third, far, outer, near, inner, here_flux)
-    )
-    even, pair_even = is_even(), pair_is_even()
-    fluxes = [
-        third,
-        jnp.where(pair_even, far, near),
-        jnp.where(even, outer, inner),
-        here_flux,
-        jnp.where(even, inner, outer),
-        jnp.where(pair_even, near, far),
-    ]
+    before_1, before_3, far, after_1, near, here_flux = (
+        x[...].astype(F32) for x in (before_1, before_3, far, after_1, near, here_flux)
+    )
+    even = pair_is_even()
+    before_2, after_2 = jnp.where(even, far, near), jnp.where(even, near, far)
+    fluxes = [before_3, before_2, before_1, here_flux, after_1, after_2]
 
     def gathered(begin):
         return sum(fluxes[begin + o][o : o + 1] for o in range(W))
@@ -449,6 +430,8 @@
             pltpu.VMEM((columns, rows), jnp.int32),
             pltpu.SemaphoreType.DMA((5,)),
         ],
+        flops=2 * K * nodes * features * features,
+        bytes_accessed=8 << 20,
         name="pack",
     )
     outer = sent(to_outer, OUTER)
@@ -458,14 +441,6 @@
         plain_kernel,
         [((nodes, features), F32)],
         [atmosphere_t, w_encode, grid_row, mesh_state],
-        spec=HBM,
-        scratch=[
-            pltpu.VMEM((channels, n_points), BF16),
-            pltpu.VMEM(w_encode.shape, BF16),
-            pltpu.VMEM((1, n_points), jnp.int32),
-            pltpu.VMEM((nodes, features), BF16),
-            pltpu.SemaphoreType.DMA((4,)),
-        ],
         flops=2 * K * nodes * features * features,
         bytes_accessed=8 << 20,
         name="plain",
@@ -508,7 +483,7 @@
         bytes_accessed=10 << 20,
         name="mesh",
     )
-    arrived = [sent(flux, route) for route in ((3,), FAR, OUTER, NEAR, INNER)]
+    arrived = [sent(flux, route) for route in ((1,), (3,), FAR, (-1,), NEAR)]
     (state,) = call(
         decode_kernel,
         [((channels, n_points), BF16)],

time: 41.6 us -> 39.1 us (0.940)
  Pallas kernels: 19 us -> 17.3 us
  waiting for transfers between devices: 5.17 us -> 4.3 us
    pallas_call x8, Pallas kernels: 19 us -> 17.3 us  [call(): pl.pallas_call(kernel, out_shape=[jax.ShapeDtypeStruct(s, t) for s, t in...]
    ppermute x10, waiting for transfers between devices: 5.17 us -> 4.3 us  [sent(): return lax.ppermute(block, AXES, route)]
  transfers between devices with their start and end apart: 10 -> 10, of which waited for: 3 -> 3; matrix products, arithmetic and copies ran while one was open for 0% -> 0% of each run, Pallas kernels for 20% -> 18%
where the time goes in v7:
time: 39.1 us; the launch traced here: 38.9 us
  Pallas kernels  17.3 us (44%)
  starting transfers between devices  16.3 us (42%)
  waiting for transfers between devices  4.3 us (11%)
  between operations  0.92 us (2%)
    pallas_call x8, Pallas kernels, call(): pl.pallas_call(kernel, out_shape=[jax.ShapeDtypeStruct(s, t) for s, t in...  17.3 us
    ppermute x10, starting transfers between devices, sent(): return lax.ppermute(block, AXES, route)  16.3 us
    ppermute x10, waiting for transfers between devices, sent(): return lax.ppermute(block, AXES, route)  4.3 us
  transfers between devices with their start and end apart: 10, of which 3 were waited for; matrix products, arithmetic and copies ran while one was open for 0% of the time, Pallas kernels for 18%

profile of v7, /device:TPU:0, one launch (start us, length us, event | category | flops | bytes accessed | tf_op | source)
XLA Modules:
  0.0 38.9 jit_solution(12895306196824479107)
XLA Ops:
  0.7 1.4 %pack.1 = (bf16[112,384]{1,0:T(8,128)(2,1)S(1)}, bf16[112,384]{1,0:T(8,128)(2,1)S(1)}, bf16[16,384]{1,0:T(8,128)(2,1)S(1)}) custom-call(s32[1,4]{1,0:T(1,128)} %counts_in.1, f32[9,8,384]{2,1,0:T(8,128)} %bitcast.18, f32[9,8,384]{2,1,0:T(8,128)} %bitcast.20, f32[9,8,384]{2,1,0:T(8,128)} %bitcast.22, s32[9,384]{1,0:T(8,128)} %mask.1), custom_call_target="tpu_custom_call" | custom-call | flops 1342177280 | bytes 8388608 | tf_op jit(solution)/shard_map/pack/pallas_call | solution.py:373
  2.0 0.0 copy-start.8
  2.0 5.5 %collective-permute-start = (bf16[112,384]{1,0:T(8,128)(2,1)S(1)}, bf16[112,384]{1,0:T(8,128)(2,1)S(1)}, u32[]{:S(2)}, u32[]{:S(2)}) collective-permute-start(bf16[112,384]{1,0:T(8,128)(2,1)S(1)} %get-tuple-element.20), channel_id=1, source_target_pairs={{0,15},{1,2},{2,1},{3,4},{4,3},{5,6},{6,5},{7,8},{8,7},{9,10},{10,... | collective-permute-start | bytes 258056 | tf_op jit(solution)/shard_map/ppermute | solution.py:30
  7.5 0.7 %collective-permute-start.1 = (bf16[16,384]{1,0:T(8,128)(2,1)S(1)}, bf16[16,384]{1,0:T(8,128)(2,1)S(1)}, u32[]{:S(2)}, u32[]{:S(2)}) collective-permute-start(bf16[16,384]{1,0:T(8,128)(2,1)S(1)} %get-tuple-element.21.own), channel_id=1, source_target_pairs={{0,14},{1,15},{2,0},{3,1},{4,2},{5,3},{6,4},{7,5},{8,6},{9,7},{10,... | collective-permute-start | bytes 36872 | tf_op jit(solution)/shard_map/ppermute | solution.py:30
  8.2 0.0 copy-start.3
  8.3 0.0 copy-start.4
  8.3 0.0 copy-start.5
  8.3 0.0 copy-start.6
  8.3 0.0 copy-start.9
  8.3 0.0 copy-start.10
  8.3 0.0 copy-start.14
  8.3 0.0 copy-start.15
  8.3 0.0 copy-start.16
  8.4 0.7 %plain.1 = f32[320,512]{1,0:T(8,128)S(1)} custom-call(bf16[227,512]{1,0:T(8,128)(2,1)S(1)} %bitcast.12, bf16[227,512]{1,0:T(8,128)(2,1)S(1)} %copy-done.1, s32[1,512]{1,0:T(1,128)S(1)} %bitcast.24, bf16[320,512]{1,0:T(8,128)(2,1)S(1)} %copy-done.13), custom_call_target="tpu_custom_call" | custom-call | flops 1342177280 | bytes 8388608 | tf_op jit(solution)/shard_map/plain/pallas_call | solution.py:373
  9.1 2.2 %collective-permute-done.1.far = bf16[16,384]{1,0:T(8,128)(2,1)S(1)} collective-permute-done((bf16[16,384]{1,0:T(8,128)(2,1)S(1)}, bf16[16,384]{1,0:T(8,128)(2,1)S(1)}, u32[]{:S(2)}, u32[]{:S(2)}) %collective-permute-start.1) | collective-permute-done | bytes 12320 | tf_op jit(solution)/shard_map/ppermute | solution.py:30
  11.2 1.1 %latents.1 = (bf16[320,512]{1,0:T(8,128)(2,1)S(1)}, f32[1,512]{1,0:T(1,128)S(1)}, s32[1,1536]{1,0:T(1,128)S(1)}) custom-call(bf16[112,384]{1,0:T(8,128)(2,1)S(1)} %collective-permute-done.outer, bf16[16,384]{1,0:T(8,128)(2,1)S(1)} %collective-permute-done.1.far, bf16[112,384]{1,0:T(8,128)(2,1)S(1)} %collective-permute-done.2.inner, ...), custom_call_target="tpu_custom_call" | custom-call | bytes 1048576 | tf_op jit(solution)/shard_map/latents/pallas_call | solution.py:373
  12.3 0.1 collective-permute-start.3
  12.4 3.8 %collective-permute-start.4 = (bf16[320,512]{1,0:T(8,128)(2,1)S(1)}, bf16[320,512]{1,0:T(8,128)(2,1)S(1)}, u32[]{:S(2)}, u32[]{:S(2)}) collective-permute-start(bf16[320,512]{1,0:T(8,128)(2,1)S(1)} %get-tuple-element.23.latent), channel_id=1, source_target_pairs={{0,15},{1,2},{2,1},{3,4},{4,3},{5,6},{6,5},{7,8},{8,7},{9,10},{10,... | collective-permute-start | bytes 983048 | tf_op jit(solution)/shard_map/ppermute | solution.py:30
  16.2 0.2 ready.1
  16.5 0.0 copy-start.2
  16.5 0.0 copy-start.11
  16.5 0.0 copy-start.12
  16.5 0.0 copy-start.17
  16.6 4.6 %own.1 = (bf16[8,320,512]{2,1,0:T(8,128)(2,1)S(1)}, f32[320,512]{1,0:T(8,128)S(1)}, f32[320,512]{1,0:T(8,128)S(1)}) custom-call(bf16[320,512]{1,0:T(8,128)(2,1)S(1)} %get-tuple-element.23.latent, bf16[1536,512]{1,0:T(8,128)(2,1)S(1)} %copy-done.9, bf16[4,2560]{1,0:T(4,128)(2,1)S(1)} %copy-done.14, bf16[4,512]{1,0:T(4,128)(2,1)S(1)} %copy-done.16, ...), custom_call_target="tpu_custom_call" | custom-call | flops 2181038080 | bytes 10485760 | tf_op jit(solution)/shard_map/own/pallas_call | solution.py:373
  21.2 0.5 %collective-permute-done.4.outer = bf16[320,512]{1,0:T(8,128)(2,1)S(1)} collective-permute-done((bf16[320,512]{1,0:T(8,128)(2,1)S(1)}, bf16[320,512]{1,0:T(8,128)(2,1)S(1)}, u32[]{:S(2)}, u32[]{:S(2)}) %collective-permute-start.4) | collective-permute-done | bytes 327712 | tf_op jit(solution)/shard_map/ppermute | solution.py:30
  21.8 6.7 %mesh.1 = (bf16[320,512]{1,0:T(8,128)(2,1)S(1)}, bf16[16,384]{1,0:T(8,128)(2,1)S(1)}) custom-call(bf16[320,512]{1,0:T(8,128)(2,1)S(1)} %collective-permute-done.3.inner, bf16[320,512]{1,0:T(8,128)(2,1)S(1)} %collective-permute-done.4.outer, bf16[320,512]{1,0:T(8,128)(2,1)S(1)} %get-tuple-element.23.latent, bf16[1536,512]{1,0:T(8,128)(2,1)S(1)} %copy-done.9, ...), custom_call_target="tpu_custom_call" | custom-call | flops 2516582400 | bytes 10485760 | tf_op jit(solution)/shard_map/mesh/pallas_call | solution.py:373
  28.4 1.1 %collective-permute-start.5 = (bf16[16,384]{1,0:T(8,128)(2,1)S(1)}, bf16[16,384]{1,0:T(8,128)(2,1)S(1)}, u32[]{:S(2)}, u32[]{:S(2)}) collective-permute-start(bf16[16,384]{1,0:T(8,128)(2,1)S(1)} %get-tuple-element.30.here_flux), channel_id=1, source_target_pairs={{0,1},{1,2},{2,3},{3,4},{4,5},{5,6},{6,7},{7,8},{8,9},{9,10},{10,1... | collective-permute-start | bytes 36872 | tf_op jit(solution)/shard_map/ppermute | solution.py:30
  29.6 4.3 %collective-permute-start.7 = (bf16[16,384]{1,0:T(8,128)(2,1)S(1)}, bf16[16,384]{1,0:T(8,128)(2,1)S(1)}, u32[]{:S(2)}, u32[]{:S(2)}) collective-permute-start(bf16[16,384]{1,0:T(8,128)(2,1)S(1)} %get-tuple-element.30.here_flux), channel_id=1, source_target_pairs={{0,14},{1,15},{2,4},{3,5},{4,2},{5,3},{6,8},{7,9},{8,6},{9,7},{10,... | collective-permute-start | bytes 36872 | tf_op jit(solution)/shard_map/ppermute | solution.py:30
  33.9 0.7 %collective-permute-start.9 = (bf16[16,384]{1,0:T(8,128)(2,1)S(1)}, bf16[16,384]{1,0:T(8,128)(2,1)S(1)}, u32[]{:S(2)}, u32[]{:S(2)}) collective-permute-start(bf16[16,384]{1,0:T(8,128)(2,1)S(1)} %get-tuple-element.30.here_flux), channel_id=1, source_target_pairs={{0,2},{1,3},{2,0},{3,1},{4,6},{5,7},{6,4},{7,5},{8,10},{9,11},{10,... | collective-permute-start | bytes 36872 | tf_op jit(solution)/shard_map/ppermute | solution.py:30
  34.6 1.4 %decode.1 = bf16[227,512]{1,0:T(8,128)(2,1)} custom-call(bf16[320,512]{1,0:T(8,128)(2,1)S(1)} %get-tuple-element.28.node_new, bf16[227,512]{1,0:T(8,128)(2,1)S(1)} %bitcast.17, s32[1,512]{1,0:T(1,128)S(1)} %bitcast.27, bf16[227,512]{1,0:T(8,128)(2,1)S(1)} %bitcast.15, f32[1,512]{1,0:T(1,128)S(1)} %get-tuple-element.29.surface), custom_call_target="tpu_custom_call" | custom-call | flops 223150080 | bytes 1048576 | tf_op jit(solution)/shard_map/decode/pallas_call | solution.py:373
  36.0 1.6 %collective-permute-done.9.near = bf16[16,384]{1,0:T(8,128)(2,1)S(1)} collective-permute-done((bf16[16,384]{1,0:T(8,128)(2,1)S(1)}, bf16[16,384]{1,0:T(8,128)(2,1)S(1)}, u32[]{:S(2)}, u32[]{:S(2)}) %collective-permute-start.9) | collective-permute-done | bytes 12320 | tf_op jit(solution)/shard_map/ppermute | solution.py:30
  37.6 1.3 %ocean.1 = f32[9,8,384]{2,1,0:T(8,128)} custom-call(bf16[16,384]{1,0:T(8,128)(2,1)S(1)} %collective-permute-done.5.before_1, bf16[16,384]{1,0:T(8,128)(2,1)S(1)} %collective-permute-done.6.before_3, bf16[16,384]{1,0:T(8,128)(2,1)S(1)} %collective-permute-done.7.far, bf16[16,384]{1,0:T(8,128)(2,1)S(1)} %collective-permute-done.8.after_1, ...), custom_call_target="tpu_custom_call" | custom-call | bytes 4194304 | tf_op jit(solution)/shard_map/ocean/pallas_call | solution.py:373
  (34 shorter events, 0.1 us)
Async XLA Ops:
  0.6 7.6 %copy-start = (bf16[512,227]{0,1:T(8,128)(2,1)S(1)}, bf16[512,227]{0,1:T(8,128)(2,1)}, u32[]{:S(2)}) copy-start(bf16[512,227]{0,1:T(8,128)(2,1)} %param.20) | copy-start | bytes 697348
  0.6 7.6 %copy-start.7 = (s32[512]{0:T(512)S(1)}, s32[512]{0:T(512)}, u32[]{:S(2)}) copy-start(s32[512]{0:T(512)} %param.24) | copy-start | bytes 6148
  0.7 7.6 %copy-start.13 = (bf16[320,512]{1,0:T(8,128)(2,1)S(1)}, bf16[320,512]{1,0:T(8,128)(2,1)}, u32[]{:S(2)}) copy-start(bf16[320,512]{1,0:T(8,128)(2,1)} %mesh_state.1) | copy-start | bytes 983044
  0.7 7.6 %copy-start.1 = (bf16[227,512]{1,0:T(8,128)(2,1)S(1)}, bf16[227,512]{1,0:T(8,128)(2,1)}, u32[]{:S(2)}) copy-start(bf16[227,512]{1,0:T(8,128)(2,1)} %w_encode.3) | copy-start | bytes 697348
  2.0 9.2 %copy-start.8 = (s32[1,4,192]{2,1,0:T(4,128)S(1)}, s32[1,4,192]{2,1,0:T(4,128)}, u32[]{:S(2)}) copy-start(s32[1,4,192]{2,1,0:T(4,128)} %param.29) | copy-start | bytes 9220
  2.0 9.2 %collective-permute-start = (bf16[112,384]{1,0:T(8,128)(2,1)S(1)}, bf16[112,384]{1,0:T(8,128)(2,1)S(1)}, u32[]{:S(2)}, u32[]{:S(2)}) collective-permute-start(bf16[112,384]{1,0:T(8,128)(2,1)S(1)} %get-tuple-element.20), channel_id=1, source_target_pairs={{0,15},{1,2},{2,1},{3,4},{4,3},{5,6},{6,5},{7,8},{8,7},{9,10},{10,... | collective-permute-start | bytes 258056 | tf_op jit(solution)/shard_map/ppermute | solution.py:30
  7.5 3.7 %collective-permute-start.2 = (bf16[112,384]{1,0:T(8,128)(2,1)S(1)}, bf16[112,384]{1,0:T(8,128)(2,1)S(1)}, u32[]{:S(2)}, u32[]{:S(2)}) collective-permute-start(bf16[112,384]{1,0:T(8,128)(2,1)S(1)} %get-tuple-element.22), channel_id=1, source_target_pairs={{0,1},{1,0},{2,3},{3,2},{4,5},{5,4},{6,7},{7,6},{8,9},{9,8},{10,11... | collective-permute-start | bytes 258056 | tf_op jit(solution)/shard_map/ppermute | solution.py:30
  7.5 3.7 %collective-permute-start.1 = (bf16[16,384]{1,0:T(8,128)(2,1)S(1)}, bf16[16,384]{1,0:T(8,128)(2,1)S(1)}, u32[]{:S(2)}, u32[]{:S(2)}) collective-permute-start(bf16[16,384]{1,0:T(8,128)(2,1)S(1)} %get-tuple-element.21.own), channel_id=1, source_target_pairs={{0,14},{1,15},{2,0},{3,1},{4,2},{5,3},{6,4},{7,5},{8,6},{9,7},{10,... | collective-permute-start | bytes 36872 | tf_op jit(solution)/shard_map/ppermute | solution.py:30
  8.2 8.0 %copy-start.3 = (f32[8,9,384]{2,0,1:T(8,128)S(1)}, f32[8,9,384]{2,0,1:T(8,128)}, u32[]{:S(2)}) copy-start(f32[8,9,384]{2,0,1:T(8,128)} %param.25) | copy-start | bytes 331780
  8.3 8.0 %copy-start.4 = (f32[8,9,384]{2,0,1:T(8,128)S(1)}, f32[8,9,384]{2,0,1:T(8,128)}, u32[]{:S(2)}) copy-start(f32[8,9,384]{2,0,1:T(8,128)} %param.26) | copy-start | bytes 331780
  8.3 8.0 %copy-start.5 = (f32[8,9,384]{2,0,1:T(8,128)S(1)}, f32[8,9,384]{2,0,1:T(8,128)}, u32[]{:S(2)}) copy-start(f32[8,9,384]{2,0,1:T(8,128)} %param.27) | copy-start | bytes 331780
  8.3 7.9 %copy-start.6 = (s32[9,384]{1,0:T(8,128)S(1)}, s32[9,384]{1,0:T(8,128)}, u32[]{:S(2)}) copy-start(s32[9,384]{1,0:T(8,128)} %mask.1) | copy-start | bytes 41476
  8.3 8.2 %copy-start.9 = (bf16[1536,512]{1,0:T(8,128)(2,1)S(1)}, bf16[1536,512]{1,0:T(8,128)(2,1)}, u32[]{:S(2)}) copy-start(bf16[1536,512]{1,0:T(8,128)(2,1)} %w_in.3) | copy-start | bytes 4718596
  8.3 8.1 %copy-start.10 = (bf16[1024,512]{1,0:T(8,128)(2,1)S(1)}, bf16[1024,512]{1,0:T(8,128)(2,1)}, u32[]{:S(2)}) copy-start(bf16[1024,512]{1,0:T(8,128)(2,1)} %w_node_in.3) | copy-start | bytes 3145732
  8.3 8.1 %copy-start.14 = (bf16[4,2560]{1,0:T(4,128)(2,1)S(1)}, bf16[4,2560]{1,0:T(4,128)(2,1)}, u32[]{:S(2)}) copy-start(bf16[4,2560]{1,0:T(4,128)(2,1)} %geometry.1) | copy-start | bytes 61444
  8.3 8.1 %copy-start.15 = (s32[320,8]{0,1:T(8,128)S(1)}, s32[320,8]{0,1:T(8,128)}, u32[]{:S(2)}) copy-start(s32[320,8]{0,1:T(8,128)} %param.23) | copy-start | bytes 30724
  8.3 8.1 %copy-start.16 = (bf16[4,512]{1,0:T(4,128)(2,1)S(1)}, bf16[4,512]{1,0:T(4,128)(2,1)}, u32[]{:S(2)}) copy-start(bf16[4,512]{1,0:T(4,128)(2,1)} %w_geometry.1) | copy-start | bytes 12292
  12.3 8.9 %collective-permute-start.3 = (bf16[320,512]{1,0:T(8,128)(2,1)S(1)}, bf16[320,512]{1,0:T(8,128)(2,1)S(1)}, u32[]{:S(2)}, u32[]{:S(2)}) collective-permute-start(bf16[320,512]{1,0:T(8,128)(2,1)S(1)} %get-tuple-element.23.latent), channel_id=1, source_target_pairs={{0,1},{1,0},{2,3},{3,2},{4,5},{5,4},{6,7},{7,6},{8,9},{9,8},{10,11... | collective-permute-start | bytes 983048 | tf_op jit(solution)/shard_map/ppermute | solution.py:30
  12.4 9.4 %collective-permute-start.4 = (bf16[320,512]{1,0:T(8,128)(2,1)S(1)}, bf16[320,512]{1,0:T(8,128)(2,1)S(1)}, u32[]{:S(2)}, u32[]{:S(2)}) collective-permute-start(bf16[320,512]{1,0:T(8,128)(2,1)S(1)} %get-tuple-element.23.latent), channel_id=1, source_target_pairs={{0,15},{1,2},{2,1},{3,4},{4,3},{5,6},{6,5},{7,8},{8,7},{9,10},{10,... | collective-permute-start | bytes 983048 | tf_op jit(solution)/shard_map/ppermute | solution.py:30
  16.5 5.3 %copy-start.2 = (bf16[512,227]{0,1:T(8,128)(2,1)S(1)}, bf16[512,227]{0,1:T(8,128)(2,1)}, u32[]{:S(2)}) copy-start(bf16[512,227]{0,1:T(8,128)(2,1)} %param.37) | copy-start | bytes 697348
  16.5 5.2 %copy-start.11 = (bf16[512,512]{1,0:T(8,128)(2,1)S(1)}, bf16[512,512]{1,0:T(8,128)(2,1)}, u32[]{:S(2)}) copy-start(bf16[512,512]{1,0:T(8,128)(2,1)} %w_out.1) | copy-start | bytes 1572868
  16.5 5.2 %copy-start.12 = (bf16[512,512]{1,0:T(8,128)(2,1)S(1)}, bf16[512,512]{1,0:T(8,128)(2,1)}, u32[]{:S(2)}) copy-start(bf16[512,512]{1,0:T(8,128)(2,1)} %w_node_out.1) | copy-start | bytes 1572868
  16.5 5.2 %copy-start.17 = (f32[512]{0:T(512)S(1)}, f32[512]{0:T(512)}, u32[]{:S(2)}) copy-start(f32[512]{0:T(512)} %param.38) | copy-start | bytes 6148
  16.5 5.2 %copy-start.18 = (f32[512]{0:T(512)S(1)}, f32[512]{0:T(512)}, u32[]{:S(2)}) copy-start(f32[512]{0:T(512)} %param.39) | copy-start | bytes 6148
  28.4 7.6 %collective-permute-start.5 = (bf16[16,384]{1,0:T(8,128)(2,1)S(1)}, bf16[16,384]{1,0:T(8,128)(2,1)S(1)}, u32[]{:S(2)}, u32[]{:S(2)}) collective-permute-start(bf16[16,384]{1,0:T(8,128)(2,1)S(1)} %get-tuple-element.30.here_flux), channel_id=1, source_target_pairs={{0,1},{1,2},{2,3},{3,4},{4,5},{5,6},{6,7},{7,8},{8,9},{9,10},{10,1... | collective-permute-start | bytes 36872 | tf_op jit(solution)/shard_map/ppermute | solution.py:30
  29.6 6.4 %collective-permute-start.6 = (bf16[16,384]{1,0:T(8,128)(2,1)S(1)}, bf16[16,384]{1,0:T(8,128)(2,1)S(1)}, u32[]{:S(2)}, u32[]{:S(2)}) collective-permute-start(bf16[16,384]{1,0:T(8,128)(2,1)S(1)} %get-tuple-element.30.here_flux), channel_id=1, source_target_pairs={{0,3},{1,4},{2,5},{3,6},{4,7},{5,8},{6,9},{7,10},{8,11},{9,12},{10... | collective-permute-start | bytes 36872 | tf_op jit(solution)/shard_map/ppermute | solution.py:30
  29.6 6.4 %collective-permute-start.7 = (bf16[16,384]{1,0:T(8,128)(2,1)S(1)}, bf16[16,384]{1,0:T(8,128)(2,1)S(1)}, u32[]{:S(2)}, u32[]{:S(2)}) collective-permute-start(bf16[16,384]{1,0:T(8,128)(2,1)S(1)} %get-tuple-element.30.here_flux), channel_id=1, source_target_pairs={{0,14},{1,15},{2,4},{3,5},{4,2},{5,3},{6,8},{7,9},{8,6},{9,7},{10,... | collective-permute-start | bytes 36872 | tf_op jit(solution)/shard_map/ppermute | solution.py:30
  33.9 2.1 %collective-permute-start.8 = (bf16[16,384]{1,0:T(8,128)(2,1)S(1)}, bf16[16,384]{1,0:T(8,128)(2,1)S(1)}, u32[]{:S(2)}, u32[]{:S(2)}) collective-permute-start(bf16[16,384]{1,0:T(8,128)(2,1)S(1)} %get-tuple-element.30.here_flux), channel_id=1, source_target_pairs={{0,15},{1,0},{2,1},{3,2},{4,3},{5,4},{6,5},{7,6},{8,7},{9,8},{10,9... | collective-permute-start | bytes 36872 | tf_op jit(solution)/shard_map/ppermute | solution.py:30
  33.9 3.7 %collective-permute-start.9 = (bf16[16,384]{1,0:T(8,128)(2,1)S(1)}, bf16[16,384]{1,0:T(8,128)(2,1)S(1)}, u32[]{:S(2)}, u32[]{:S(2)}) collective-permute-start(bf16[16,384]{1,0:T(8,128)(2,1)S(1)} %get-tuple-element.30.here_flux), channel_id=1, source_target_pairs={{0,2},{1,3},{2,0},{3,1},{4,6},{5,7},{6,4},{7,5},{8,10},{9,11},{10,... | collective-permute-start | bytes 36872 | tf_op jit(solution)/shard_map/ppermute | solution.py:30

commit v8 on v7

--- a/solution.py
+++ b/solution.py
@@ -125,7 +125,8 @@
     return one_hot(iota((nodes, grid_row.shape[1]), 0) == grid_row)
 
 
-def plain_kernel(atmosphere, w_encode, grid_row, mesh_state, plain_out):
+def plain_kernel(after, atmosphere, w_encode, grid_row, mesh_state, plain_out, early_out):
+    del after
     member = members(mesh_state.shape[0], grid_row[...])
     population = jnp.sum(member.astype(F32), axis=1, keepdims=True)
     state = atmosphere[...]
@@ -134,7 +135,9 @@
     pooled_high = pooled.astype(BF16)
     pooled_low = (pooled - pooled_high.astype(F32)).astype(BF16)
     encode = w_encode[...]
-    plain_out[...] = mesh_state[...].astype(F32) + dot(pooled_high, encode) + dot(pooled_low, encode)
+    plain = mesh_state[...].astype(F32) + dot(pooled_high, encode) + dot(pooled_low, encode)
+    plain_out[...] = plain
+    early_out[...] = plain.astype(BF16)
 
 
 def rolled_points(points, starts):
@@ -152,7 +155,7 @@
 
 def latent_kernel(
     outer, far, inner, own, points, atmosphere, w_encode, grid_row, plain,
-    latent_out, surface_out, placed_out,
+    latent_out, share_out, surface_out, placed_out,
 ):
     pair = [x[...].astype(F32)[-8:] for x in (inner, outer)]
     even = is_even()
@@ -176,7 +179,11 @@
     )
     surface_out[...] = surface
     pair = jnp.concatenate([surface, jnp.ones((7, n_points), F32)], axis=0).astype(BF16)
-    pooled = dot_nt(members(plain.shape[0], grid_row[...]), pair)
+    member = members(plain.shape[0], grid_row[...])
+    pooled = dot_nt(pair, member)
+    share = two_parts(pooled[0:1] / jnp.maximum(pooled[1:2], 1.0)).astype(F32)
+    share_out[...] = jnp.concatenate([share, jnp.zeros(share.shape, F32)], axis=0).astype(BF16)
+    pooled = dot_nt(member, pair)
     share = pooled[:, 0:1] / jnp.maximum(pooled[:, 1:2], 1.0)
     latent_out[...] = (plain[...] + share * w_encode[0:16].astype(F32)[0:1]).astype(BF16)
 
@@ -222,13 +229,16 @@
 
 
 def mesh_kernel(
-    inner, outer, latent, w_in, w_out, pre, base, node_part, neighbours, w_node_in, w_node_out, w_decode,
+    inner, outer, inner_share, outer_share, w_encode, latent, w_in, w_out, pre, base, node_part, neighbours, w_node_in, w_node_out, w_decode,
     gain_edge, gain_node, grid_row, atmosphere, placed, node_out, flux_out, sender, total,
 ):
     nodes, features = latent.shape
     w_sender = w_in[features : 2 * features]
-    sender[:nodes] = dot(inner[...], w_sender).astype(BF16)
-    sender[nodes:] = dot(outer[...], w_sender).astype(BF16)
+    surface_sender = dot(w_encode[0:16], w_sender)[0:1]
+    for begin, early, share in ((0, inner, inner_share), (nodes, outer, outer_share)):
+        parts = share[...].astype(F32)[:8].T
+        product = dot(early[...], w_sender) + (parts[:, 0:1] + parts[:, 1:2]) * surface_sender
+        sender[begin : begin + nodes] = product.astype(BF16)
     below = jnp.where(is_even(), nodes, 0)
     above = nodes - below
     listed = listed_slots(neighbours)
@@ -315,13 +325,13 @@
         qy_out[c] = opened * (face - COEFF_H)
 
 
-def ocean_kernel(before_1, before_3, far, after_1, near, here_flux, field_in, wet, px, qx, py, qy, mix, out):
+def ocean_kernel(far, after_1, near, before_1, before_3, here_flux, field_in, wet, px, qx, py, qy, mix, out):
     count, levels, rows = field_in.shape
     columns = count - 2 * EDGE
     triples = columns // 3
     span = rows // 3
-    before_1, before_3, far, after_1, near, here_flux = (
-        x[...].astype(F32) for x in (before_1, before_3, far, after_1, near, here_flux)
+    far, after_1, near, before_1, before_3, here_flux = (
+        x[...].astype(F32) for x in (far, after_1, near, before_1, before_3, here_flux)
     )
     even = pair_is_even()
     before_2, after_2 = jnp.where(even, far, near), jnp.where(even, near, far)
@@ -437,28 +447,29 @@
     outer = sent(to_outer, OUTER)
     far = sent(blocks, (-2,))
     inner = sent(to_inner, INNER)
-    (plain,) = call(
+    plain, early = call(
         plain_kernel,
-        [((nodes, features), F32)],
-        [atmosphere_t, w_encode, grid_row, mesh_state],
+        [((nodes, features), F32), ((nodes, features), BF16)],
+        [blocks, atmosphere_t, w_encode, grid_row, mesh_state],
         flops=2 * K * nodes * features * features,
         bytes_accessed=8 << 20,
         name="plain",
     )
-    latent, surface, placed = call(
+    early_inner, early_outer = sent(early, INNER), sent(early, OUTER)
+    latent, share, surface, placed = call(
         latent_kernel,
-        [((nodes, features), BF16), ((1, n_points), F32), ((1, W * rows), jnp.int32)],
+        [((nodes, features), BF16), ((16, nodes), BF16), ((1, n_points), F32), ((1, W * rows), jnp.int32)],
         [outer, far, inner, blocks, intersection_points[0], atmosphere_t, w_encode, grid_row, plain],
+        flops=8 * K * nodes * features * features,
         name="latents",
     )
-    latent_inner = sent(latent, INNER)
-    latent_outer = sent(latent, OUTER)
+    share_inner, share_outer = sent(share, INNER), sent(share, OUTER)
     pre, base, node_part = call(
         own_kernel,
         [((K, nodes, features), BF16), ((nodes, features), F32), ((nodes, features), F32)],
         [latent, w_edge_in, edge_geometry, w_geometry, slots, w_node_in],
         scratch=[pltpu.VMEM((nodes, features), BF16), pltpu.VMEM((K * nodes, 128), F32)],
-        flops=2 * K * nodes * (nodes + features) * features,
+        flops=8 * 2 * K * nodes * (nodes + features) * features,
         bytes_accessed=10 << 20,
         name="own",
     )
@@ -474,7 +485,7 @@
         mesh_kernel,
         [((nodes, features), BF16), (few, BF16)],
         [
-            latent_inner, latent_outer, latent, w_edge_in, w_edge_out, pre, base, node_part, slots,
+            early_inner, early_outer, share_inner, share_outer, w_encode, latent, w_edge_in, w_edge_out, pre, base, node_part, slots,
             w_node_in, w_node_out, decode_t, gain_edge.reshape(1, features),
             gain_node.reshape(1, features), grid_row, atmosphere_t, placed,
         ],
@@ -483,7 +494,7 @@
         bytes_accessed=10 << 20,
         name="mesh",
     )
-    arrived = [sent(flux, route) for route in ((1,), (3,), FAR, (-1,), NEAR)]
+    arrived = [sent(flux, route) for route in (FAR, (-1,), NEAR, (1,), (3,))]
     (state,) = call(
         decode_kernel,
         [((channels, n_points), BF16)],

time: 39.1 us -> 39.9 us (1.020)
  starting transfers between devices: 16.3 us -> 17.4 us
  waiting for transfers between devices: 4.3 us -> 3.26 us
  Pallas kernels: 17.3 us -> 17.7 us
    ppermute x10 -> x12, starting transfers between devices: 16.3 us -> 17.4 us  [sent(): return lax.ppermute(block, AXES, route)]
    ppermute x10 -> x12, waiting for transfers between devices: 4.3 us -> 3.26 us  [sent(): return lax.ppermute(block, AXES, route)]
  transfers between devices with their start and end apart: 10 -> 12, of which waited for: 3 -> 3; matrix products, arithmetic and copies ran while one was open for 0% -> 0% of each run, Pallas kernels for 18% -> 20%
where the time goes in v8:
time: 39.9 us; the launch traced here: 39.7 us
  Pallas kernels  17.7 us (44%)
  starting transfers between devices  17.4 us (44%)
  waiting for transfers between devices  3.26 us (8%)
  between operations  0.95 us (2%)
  local copies, waits for them, and re-layouts  0.47 us (1%)
    pallas_call x8, Pallas kernels, call(): pl.pallas_call(kernel, out_shape=[jax.ShapeDtypeStruct(s, t) for s, t in...  17.7 us
    ppermute x12, starting transfers between devices, sent(): return lax.ppermute(block, AXES, route)  17.4 us
    ppermute x12, waiting for transfers between devices, sent(): return lax.ppermute(block, AXES, route)  3.26 us
  transfers between devices with their start and end apart: 12, of which 3 were waited for; matrix products, arithmetic and copies ran while one was open for 0% of the time, Pallas kernels for 20%

profile of v8, /device:TPU:0, one launch (start us, length us, event | category | flops | bytes accessed | tf_op | source)
XLA Modules:
  0.0 39.7 jit_solution(2563644697305440964)
XLA Ops:
  0.7 1.4 %pack.1 = (bf16[112,384]{1,0:T(8,128)(2,1)S(1)}, bf16[112,384]{1,0:T(8,128)(2,1)S(1)}, bf16[16,384]{1,0:T(8,128)(2,1)S(1)}) custom-call(s32[1,4]{1,0:T(1,128)} %counts_in.1, f32[9,8,384]{2,1,0:T(8,128)} %bitcast.18, f32[9,8,384]{2,1,0:T(8,128)} %bitcast.20, f32[9,8,384]{2,1,0:T(8,128)} %bitcast.22, s32[9,384]{1,0:T(8,128)} %mask.1), custom_call_target="tpu_custom_call" | custom-call | flops 1342177280 | bytes 8388608 | tf_op jit(solution)/shard_map/pack/pallas_call | solution.py:383
  2.0 0.0 copy-start.17
  2.0 6.0 %collective-permute-start.3 = (bf16[16,384]{1,0:T(8,128)(2,1)S(1)}, bf16[16,384]{1,0:T(8,128)(2,1)S(1)}, u32[]{:S(2)}, u32[]{:S(2)}) collective-permute-start(bf16[16,384]{1,0:T(8,128)(2,1)S(1)} %get-tuple-element.23.after.own), channel_id=1, source_target_pairs={{0,14},{1,15},{2,0},{3,1},{4,2},{5,3},{6,4},{7,5},{8,6},{9,7},{10,... | collective-permute-start | bytes 36872 | tf_op jit(solution)/shard_map/ppermute | solution.py:30
  8.1 0.7 %plain.1 = (f32[320,512]{1,0:T(8,128)S(1)}, bf16[320,512]{1,0:T(8,128)(2,1)S(1)}) custom-call(bf16[16,384]{1,0:T(8,128)(2,1)S(1)} %get-tuple-element.23.after.own, bf16[227,512]{1,0:T(8,128)(2,1)S(1)} %bitcast.12, bf16[227,512]{1,0:T(8,128)(2,1)S(1)} %copy-done.6, s32[1,512]{1,0:T(1,128)S(1)} %bitcast.26, bf16[320,512]{1,0:T(8,128)(2,1)S(1)} %copy-done.15), custom_call_target="tpu_custom_call" | custom-call | flops 1342177280 | bytes 8388608 | tf_op jit(solution)/shard_map/plain/pallas_call | solution.py:383
  8.8 0.6 %collective-permute-start = (bf16[320,512]{1,0:T(8,128)(2,1)S(1)}, bf16[320,512]{1,0:T(8,128)(2,1)S(1)}, u32[]{:S(2)}, u32[]{:S(2)}) collective-permute-start(bf16[320,512]{1,0:T(8,128)(2,1)S(1)} %get-tuple-element.24), channel_id=1, source_target_pairs={{0,1},{1,0},{2,3},{3,2},{4,5},{5,4},{6,7},{7,6},{8,9},{9,8},{10,11... | collective-permute-start | bytes 983048 | tf_op jit(solution)/shard_map/ppermute | solution.py:30
  9.4 4.4 %collective-permute-start.1 = (bf16[320,512]{1,0:T(8,128)(2,1)S(1)}, bf16[320,512]{1,0:T(8,128)(2,1)S(1)}, u32[]{:S(2)}, u32[]{:S(2)}) collective-permute-start(bf16[320,512]{1,0:T(8,128)(2,1)S(1)} %get-tuple-element.24), channel_id=1, source_target_pairs={{0,15},{1,2},{2,1},{3,4},{4,3},{5,6},{6,5},{7,8},{8,7},{9,10},{10,... | collective-permute-start | bytes 983048 | tf_op jit(solution)/shard_map/ppermute | solution.py:30
  13.8 1.0 %collective-permute-done.2.outer = bf16[112,384]{1,0:T(8,128)(2,1)S(1)} collective-permute-done((bf16[112,384]{1,0:T(8,128)(2,1)S(1)}, bf16[112,384]{1,0:T(8,128)(2,1)S(1)}, u32[]{:S(2)}, u32[]{:S(2)}) %collective-permute-start.2) | collective-permute-done | bytes 86048 | tf_op jit(solution)/shard_map/ppermute | solution.py:30
  14.8 0.0 copy-start.1
  14.8 0.0 copy-start.11
  14.8 0.0 copy-start.16
  14.8 0.0 copy-start.18
  14.8 1.1 %latents.1 = (bf16[320,512]{1,0:T(8,128)(2,1)S(1)}, bf16[16,320]{1,0:T(8,128)(2,1)S(1)}, f32[1,512]{1,0:T(1,128)S(1)}, s32[1,1536]{1,0:T(1,128)S(1)}) custom-call(bf16[112,384]{1,0:T(8,128)(2,1)S(1)} %collective-permute-done.2.outer, bf16[16,384]{1,0:T(8,128)(2,1)S(1)} %collective-permute-done.3.far, bf16[112,384]{1,0:T(8,128)(2,1)S(1)} %collective-permute-done.4.inner, ...), custom_call_target="tpu_custom_call" | custom-call | flops 5368709120 | bytes 1048576 | tf_op jit(solution)/shard_map/latents/pallas_call | solution.py:383
  16.0 0.1 collective-permute-start.5
  16.0 0.1 collective-permute-start.6
  16.1 0.1 copy-done
  16.2 0.3 copy-done.1
  16.5 0.0 copy-start.8
  16.5 0.0 copy-start.9
  16.5 0.0 copy-start.10
  16.5 0.0 copy-start.3
  16.6 0.0 copy-start.4
  16.6 0.0 copy-start.14
  16.6 4.6 %own.1 = (bf16[8,320,512]{2,1,0:T(8,128)(2,1)S(1)}, f32[320,512]{1,0:T(8,128)S(1)}, f32[320,512]{1,0:T(8,128)S(1)}) custom-call(bf16[320,512]{1,0:T(8,128)(2,1)S(1)} %get-tuple-element.29.latent, bf16[1536,512]{1,0:T(8,128)(2,1)S(1)} %copy-done, bf16[4,2560]{1,0:T(4,128)(2,1)S(1)} %copy-done.16, bf16[4,512]{1,0:T(4,128)(2,1)S(1)} %copy-done.18, ...), custom_call_target="tpu_custom_call" | custom-call | flops 17448304640 | bytes 10485760 | tf_op jit(solution)/shard_map/own/pallas_call | solution.py:383
  21.3 0.2 ready.1
  21.5 0.4 %collective-permute-done.6.outer_share = bf16[16,320]{1,0:T(8,128)(2,1)S(1)} collective-permute-done((bf16[16,320]{1,0:T(8,128)(2,1)S(1)}, bf16[16,320]{1,0:T(8,128)(2,1)S(1)}, u32[]{:S(2)}, u32[]{:S(2)}) %collective-permute-start.6) | collective-permute-done | bytes 10272 | tf_op jit(solution)/shard_map/ppermute | solution.py:30
  22.0 6.9 %mesh.1 = (bf16[320,512]{1,0:T(8,128)(2,1)S(1)}, bf16[16,384]{1,0:T(8,128)(2,1)S(1)}) custom-call(bf16[320,512]{1,0:T(8,128)(2,1)S(1)} %collective-permute-done.inner, bf16[320,512]{1,0:T(8,128)(2,1)S(1)} %collective-permute-done.1.outer, bf16[16,320]{1,0:T(8,128)(2,1)S(1)} %collective-permute-done.5.inner_share, ...), custom_call_target="tpu_custom_call" | custom-call | flops 2516582400 | bytes 10485760 | tf_op jit(solution)/shard_map/mesh/pallas_call | solution.py:383
  28.9 0.0 collective-permute-start.11
  28.9 5.7 %collective-permute-start.7 = (bf16[16,384]{1,0:T(8,128)(2,1)S(1)}, bf16[16,384]{1,0:T(8,128)(2,1)S(1)}, u32[]{:S(2)}, u32[]{:S(2)}) collective-permute-start(bf16[16,384]{1,0:T(8,128)(2,1)S(1)} %get-tuple-element.36.here_flux), channel_id=1, source_target_pairs={{0,14},{1,15},{2,4},{3,5},{4,2},{5,3},{6,8},{7,9},{8,6},{9,7},{10,... | collective-permute-start | bytes 36872 | tf_op jit(solution)/shard_map/ppermute | solution.py:30
  34.7 0.4 %collective-permute-start.9 = (bf16[16,384]{1,0:T(8,128)(2,1)S(1)}, bf16[16,384]{1,0:T(8,128)(2,1)S(1)}, u32[]{:S(2)}, u32[]{:S(2)}) collective-permute-start(bf16[16,384]{1,0:T(8,128)(2,1)S(1)} %get-tuple-element.36.here_flux), channel_id=1, source_target_pairs={{0,2},{1,3},{2,0},{3,1},{4,6},{5,7},{6,4},{7,5},{8,10},{9,11},{10,... | collective-permute-start | bytes 36872 | tf_op jit(solution)/shard_map/ppermute | solution.py:30
  35.1 1.4 %decode.1 = bf16[227,512]{1,0:T(8,128)(2,1)} custom-call(bf16[320,512]{1,0:T(8,128)(2,1)S(1)} %get-tuple-element.34.node_new, bf16[227,512]{1,0:T(8,128)(2,1)S(1)} %bitcast.17, s32[1,512]{1,0:T(1,128)S(1)} %bitcast.29, bf16[227,512]{1,0:T(8,128)(2,1)S(1)} %bitcast.15, f32[1,512]{1,0:T(1,128)S(1)} %get-tuple-element.35.surface), custom_call_target="tpu_custom_call" | custom-call | flops 223150080 | bytes 1048576 | tf_op jit(solution)/shard_map/decode/pallas_call | solution.py:383
  36.5 1.9 %collective-permute-done.9.near = bf16[16,384]{1,0:T(8,128)(2,1)S(1)} collective-permute-done((bf16[16,384]{1,0:T(8,128)(2,1)S(1)}, bf16[16,384]{1,0:T(8,128)(2,1)S(1)}, u32[]{:S(2)}, u32[]{:S(2)}) %collective-permute-start.9) | collective-permute-done | bytes 12320 | tf_op jit(solution)/shard_map/ppermute | solution.py:30
  38.4 1.3 %ocean.1 = f32[9,8,384]{2,1,0:T(8,128)} custom-call(bf16[16,384]{1,0:T(8,128)(2,1)S(1)} %collective-permute-done.7.far, bf16[16,384]{1,0:T(8,128)(2,1)S(1)} %collective-permute-done.8.after_1, bf16[16,384]{1,0:T(8,128)(2,1)S(1)} %collective-permute-done.9.near, bf16[16,384]{1,0:T(8,128)(2,1)S(1)} %collective-permute-done.10.before_1, ...), custom_call_target="tpu_custom_call" | custom-call | bytes 4194304 | tf_op jit(solution)/shard_map/ocean/pallas_call | solution.py:383
  (38 shorter events, 0.1 us)
Async XLA Ops:
  0.6 7.5 %copy-start.2 = (bf16[512,227]{0,1:T(8,128)(2,1)S(1)}, bf16[512,227]{0,1:T(8,128)(2,1)}, u32[]{:S(2)}) copy-start(bf16[512,227]{0,1:T(8,128)(2,1)} %param.20) | copy-start | bytes 697348
  0.6 7.5 %copy-start.12 = (s32[512]{0:T(512)S(1)}, s32[512]{0:T(512)}, u32[]{:S(2)}) copy-start(s32[512]{0:T(512)} %param.24) | copy-start | bytes 6148
  0.7 7.5 %copy-start.15 = (bf16[320,512]{1,0:T(8,128)(2,1)S(1)}, bf16[320,512]{1,0:T(8,128)(2,1)}, u32[]{:S(2)}) copy-start(bf16[320,512]{1,0:T(8,128)(2,1)} %mesh_state.1) | copy-start | bytes 983044
  0.7 7.5 %copy-start.6 = (bf16[227,512]{1,0:T(8,128)(2,1)S(1)}, bf16[227,512]{1,0:T(8,128)(2,1)}, u32[]{:S(2)}) copy-start(bf16[227,512]{1,0:T(8,128)(2,1)} %w_encode.5) | copy-start | bytes 697348
  2.0 12.8 %copy-start.17 = (s32[1,4,192]{2,1,0:T(4,128)S(1)}, s32[1,4,192]{2,1,0:T(4,128)}, u32[]{:S(2)}) copy-start(s32[1,4,192]{2,1,0:T(4,128)} %param.29) | copy-start | bytes 9220
  2.0 11.8 %collective-permute-start.3 = (bf16[16,384]{1,0:T(8,128)(2,1)S(1)}, bf16[16,384]{1,0:T(8,128)(2,1)S(1)}, u32[]{:S(2)}, u32[]{:S(2)}) collective-permute-start(bf16[16,384]{1,0:T(8,128)(2,1)S(1)} %get-tuple-element.23.after.own), channel_id=1, source_target_pairs={{0,14},{1,15},{2,0},{3,1},{4,2},{5,3},{6,4},{7,5},{8,6},{9,7},{10,... | collective-permute-start | bytes 36872 | tf_op jit(solution)/shard_map/ppermute | solution.py:30
  8.1 6.7 %collective-permute-start.2 = (bf16[112,384]{1,0:T(8,128)(2,1)S(1)}, bf16[112,384]{1,0:T(8,128)(2,1)S(1)}, u32[]{:S(2)}, u32[]{:S(2)}) collective-permute-start(bf16[112,384]{1,0:T(8,128)(2,1)S(1)} %get-tuple-element.25), channel_id=1, source_target_pairs={{0,15},{1,2},{2,1},{3,4},{4,3},{5,6},{6,5},{7,8},{8,7},{9,10},{10,... | collective-permute-start | bytes 258056 | tf_op jit(solution)/shard_map/ppermute | solution.py:30
  8.1 6.7 %collective-permute-start.4 = (bf16[112,384]{1,0:T(8,128)(2,1)S(1)}, bf16[112,384]{1,0:T(8,128)(2,1)S(1)}, u32[]{:S(2)}, u32[]{:S(2)}) collective-permute-start(bf16[112,384]{1,0:T(8,128)(2,1)S(1)} %get-tuple-element.26), channel_id=1, source_target_pairs={{0,1},{1,0},{2,3},{3,2},{4,5},{5,4},{6,7},{7,6},{8,9},{9,8},{10,11... | collective-permute-start | bytes 258056 | tf_op jit(solution)/shard_map/ppermute | solution.py:30
  8.8 13.1 %collective-permute-start = (bf16[320,512]{1,0:T(8,128)(2,1)S(1)}, bf16[320,512]{1,0:T(8,128)(2,1)S(1)}, u32[]{:S(2)}, u32[]{:S(2)}) collective-permute-start(bf16[320,512]{1,0:T(8,128)(2,1)S(1)} %get-tuple-element.24), channel_id=1, source_target_pairs={{0,1},{1,0},{2,3},{3,2},{4,5},{5,4},{6,7},{7,6},{8,9},{9,8},{10,11... | collective-permute-start | bytes 983048 | tf_op jit(solution)/shard_map/ppermute | solution.py:30
  9.4 12.5 %collective-permute-start.1 = (bf16[320,512]{1,0:T(8,128)(2,1)S(1)}, bf16[320,512]{1,0:T(8,128)(2,1)S(1)}, u32[]{:S(2)}, u32[]{:S(2)}) collective-permute-start(bf16[320,512]{1,0:T(8,128)(2,1)S(1)} %get-tuple-element.24), channel_id=1, source_target_pairs={{0,15},{1,2},{2,1},{3,4},{4,3},{5,6},{6,5},{7,8},{8,7},{9,10},{10,... | collective-permute-start | bytes 983048 | tf_op jit(solution)/shard_map/ppermute | solution.py:30
  14.8 1.4 %copy-start = (bf16[1536,512]{1,0:T(8,128)(2,1)S(1)}, bf16[1536,512]{1,0:T(8,128)(2,1)}, u32[]{:S(2)}) copy-start(bf16[1536,512]{1,0:T(8,128)(2,1)} %w_in.3) | copy-start | bytes 4718596
  14.8 1.7 %copy-start.1 = (bf16[1024,512]{1,0:T(8,128)(2,1)S(1)}, bf16[1024,512]{1,0:T(8,128)(2,1)}, u32[]{:S(2)}) copy-start(bf16[1024,512]{1,0:T(8,128)(2,1)} %w_node_in.3) | copy-start | bytes 3145732
  14.8 1.7 %copy-start.11 = (s32[320,8]{0,1:T(8,128)S(1)}, s32[320,8]{0,1:T(8,128)}, u32[]{:S(2)}) copy-start(s32[320,8]{0,1:T(8,128)} %param.23) | copy-start | bytes 30724
  14.8 1.7 %copy-start.16 = (bf16[4,2560]{1,0:T(4,128)(2,1)S(1)}, bf16[4,2560]{1,0:T(4,128)(2,1)}, u32[]{:S(2)}) copy-start(bf16[4,2560]{1,0:T(4,128)(2,1)} %geometry.1) | copy-start | bytes 61444
  14.8 1.7 %copy-start.18 = (bf16[4,512]{1,0:T(4,128)(2,1)S(1)}, bf16[4,512]{1,0:T(4,128)(2,1)}, u32[]{:S(2)}) copy-start(bf16[4,512]{1,0:T(4,128)(2,1)} %w_geometry.1) | copy-start | bytes 12292
  16.0 5.5 %collective-permute-start.5 = (bf16[16,320]{1,0:T(8,128)(2,1)S(1)}, bf16[16,320]{1,0:T(8,128)(2,1)S(1)}, u32[]{:S(2)}, u32[]{:S(2)}) collective-permute-start(bf16[16,320]{1,0:T(8,128)(2,1)S(1)} %get-tuple-element.28), channel_id=1, source_target_pairs={{0,1},{1,0},{2,3},{3,2},{4,5},{5,4},{6,7},{7,6},{8,9},{9,8},{10,11... | collective-permute-start | bytes 30728 | tf_op jit(solution)/shard_map/ppermute | solution.py:30
  16.0 5.9 %collective-permute-start.6 = (bf16[16,320]{1,0:T(8,128)(2,1)S(1)}, bf16[16,320]{1,0:T(8,128)(2,1)S(1)}, u32[]{:S(2)}, u32[]{:S(2)}) collective-permute-start(bf16[16,320]{1,0:T(8,128)(2,1)S(1)} %get-tuple-element.28), channel_id=1, source_target_pairs={{0,15},{1,2},{2,1},{3,4},{4,3},{5,6},{6,5},{7,8},{8,7},{9,10},{10,... | collective-permute-start | bytes 30728 | tf_op jit(solution)/shard_map/ppermute | solution.py:30
  16.5 4.8 %copy-start.7 = (f32[8,9,384]{2,0,1:T(8,128)S(1)}, f32[8,9,384]{2,0,1:T(8,128)}, u32[]{:S(2)}) copy-start(f32[8,9,384]{2,0,1:T(8,128)} %param.25) | copy-start | bytes 331780
  16.5 4.8 %copy-start.8 = (f32[8,9,384]{2,0,1:T(8,128)S(1)}, f32[8,9,384]{2,0,1:T(8,128)}, u32[]{:S(2)}) copy-start(f32[8,9,384]{2,0,1:T(8,128)} %param.26) | copy-start | bytes 331780
  16.5 4.8 %copy-start.9 = (f32[8,9,384]{2,0,1:T(8,128)S(1)}, f32[8,9,384]{2,0,1:T(8,128)}, u32[]{:S(2)}) copy-start(f32[8,9,384]{2,0,1:T(8,128)} %param.27) | copy-start | bytes 331780
  16.5 4.8 %copy-start.10 = (s32[9,384]{1,0:T(8,128)S(1)}, s32[9,384]{1,0:T(8,128)}, u32[]{:S(2)}) copy-start(s32[9,384]{1,0:T(8,128)} %mask.1) | copy-start | bytes 41476
  16.5 5.4 %copy-start.3 = (bf16[512,227]{0,1:T(8,128)(2,1)S(1)}, bf16[512,227]{0,1:T(8,128)(2,1)}, u32[]{:S(2)}) copy-start(bf16[512,227]{0,1:T(8,128)(2,1)} %param.37) | copy-start | bytes 697348
  16.6 5.4 %copy-start.4 = (bf16[512,512]{1,0:T(8,128)(2,1)S(1)}, bf16[512,512]{1,0:T(8,128)(2,1)}, u32[]{:S(2)}) copy-start(bf16[512,512]{1,0:T(8,128)(2,1)} %w_out.1) | copy-start | bytes 1572868
  16.6 5.4 %copy-start.5 = (bf16[512,512]{1,0:T(8,128)(2,1)S(1)}, bf16[512,512]{1,0:T(8,128)(2,1)}, u32[]{:S(2)}) copy-start(bf16[512,512]{1,0:T(8,128)(2,1)} %w_node_out.1) | copy-start | bytes 1572868
  16.6 5.4 %copy-start.13 = (f32[512]{0:T(512)S(1)}, f32[512]{0:T(512)}, u32[]{:S(2)}) copy-start(f32[512]{0:T(512)} %param.38) | copy-start | bytes 6148
  16.6 5.4 %copy-start.14 = (f32[512]{0:T(512)S(1)}, f32[512]{0:T(512)}, u32[]{:S(2)}) copy-start(f32[512]{0:T(512)} %param.39) | copy-start | bytes 6148
  28.9 7.6 %collective-permute-start.10 = (bf16[16,384]{1,0:T(8,128)(2,1)S(1)}, bf16[16,384]{1,0:T(8,128)(2,1)S(1)}, u32[]{:S(2)}, u32[]{:S(2)}) collective-permute-start(bf16[16,384]{1,0:T(8,128)(2,1)S(1)} %get-tuple-element.36.here_flux), channel_id=1, source_target_pairs={{0,1},{1,2},{2,3},{3,4},{4,5},{5,6},{6,7},{7,8},{8,9},{9,10},{10,1... | collective-permute-start | bytes 36872 | tf_op jit(solution)/shard_map/ppermute | solution.py:30
  28.9 7.6 %collective-permute-start.11 = (bf16[16,384]{1,0:T(8,128)(2,1)S(1)}, bf16[16,384]{1,0:T(8,128)(2,1)S(1)}, u32[]{:S(2)}, u32[]{:S(2)}) collective-permute-start(bf16[16,384]{1,0:T(8,128)(2,1)S(1)} %get-tuple-element.36.here_flux), channel_id=1, source_target_pairs={{0,3},{1,4},{2,5},{3,6},{4,7},{5,8},{6,9},{7,10},{8,11},{9,12},{10... | collective-permute-start | bytes 36872 | tf_op jit(solution)/shard_map/ppermute | solution.py:30
  28.9 7.6 %collective-permute-start.7 = (bf16[16,384]{1,0:T(8,128)(2,1)S(1)}, bf16[16,384]{1,0:T(8,128)(2,1)S(1)}, u32[]{:S(2)}, u32[]{:S(2)}) collective-permute-start(bf16[16,384]{1,0:T(8,128)(2,1)S(1)} %get-tuple-element.36.here_flux), channel_id=1, source_target_pairs={{0,14},{1,15},{2,4},{3,5},{4,2},{5,3},{6,8},{7,9},{8,6},{9,7},{10,... | collective-permute-start | bytes 36872 | tf_op jit(solution)/shard_map/ppermute | solution.py:30
  34.7 1.8 %collective-permute-start.8 = (bf16[16,384]{1,0:T(8,128)(2,1)S(1)}, bf16[16,384]{1,0:T(8,128)(2,1)S(1)}, u32[]{:S(2)}, u32[]{:S(2)}) collective-permute-start(bf16[16,384]{1,0:T(8,128)(2,1)S(1)} %get-tuple-element.36.here_flux), channel_id=1, source_target_pairs={{0,15},{1,0},{2,1},{3,2},{4,3},{5,4},{6,5},{7,6},{8,7},{9,8},{10,9... | collective-permute-start | bytes 36872 | tf_op jit(solution)/shard_map/ppermute | solution.py:30
  34.7 3.7 %collective-permute-start.9 = (bf16[16,384]{1,0:T(8,128)(2,1)S(1)}, bf16[16,384]{1,0:T(8,128)(2,1)S(1)}, u32[]{:S(2)}, u32[]{:S(2)}) collective-permute-start(bf16[16,384]{1,0:T(8,128)(2,1)S(1)} %get-tuple-element.36.here_flux), channel_id=1, source_target_pairs={{0,2},{1,3},{2,0},{3,1},{4,6},{5,7},{6,4},{7,5},{8,10},{9,11},{10,... | collective-permute-start | bytes 36872 | tf_op jit(solution)/shard_map/ppermute | solution.py:30

commit v9 on v7

--- a/solution.py
+++ b/solution.py
@@ -222,7 +222,7 @@
 
 
 def mesh_kernel(
-    inner, outer, latent, w_in, w_out, pre, base, node_part, neighbours, w_node_in, w_node_out, w_decode,
+    outer, inner, latent, w_in, w_out, pre, base, node_part, neighbours, w_node_in, w_node_out, w_decode,
     gain_edge, gain_node, grid_row, atmosphere, placed, node_out, flux_out, sender, total,
 ):
     nodes, features = latent.shape
@@ -451,8 +451,8 @@
         [outer, far, inner, blocks, intersection_points[0], atmosphere_t, w_encode, grid_row, plain],
         name="latents",
     )
+    latent_outer = sent(latent, OUTER)
     latent_inner = sent(latent, INNER)
-    latent_outer = sent(latent, OUTER)
     pre, base, node_part = call(
         own_kernel,
         [((K, nodes, features), BF16), ((nodes, features), F32), ((nodes, features), F32)],
@@ -474,7 +474,7 @@
         mesh_kernel,
         [((nodes, features), BF16), (few, BF16)],
         [
-            latent_inner, latent_outer, latent, w_edge_in, w_edge_out, pre, base, node_part, slots,
+            latent_outer, latent_inner, latent, w_edge_in, w_edge_out, pre, base, node_part, slots,
             w_node_in, w_node_out, decode_t, gain_edge.reshape(1, features),
             gain_node.reshape(1, features), grid_row, atmosphere_t, placed,
         ],

time: 39.1 us -> 38.8 us (level)
  starting transfers between devices: 16.3 us -> 15.5 us
  waiting for transfers between devices: 4.3 us -> 4.83 us
    ppermute x10, starting transfers between devices: 16.3 us -> 15.5 us  [sent(): return lax.ppermute(block, AXES, route)]
    ppermute x10, waiting for transfers between devices: 4.3 us -> 4.83 us  [sent(): return lax.ppermute(block, AXES, route)]
where the time goes in v9:
time: 38.8 us; the launch traced here: 38.6 us
  Pallas kernels  17.3 us (45%)
  starting transfers between devices  15.5 us (40%)
  waiting for transfers between devices  4.83 us (12%)
  between operations  0.93 us (2%)
    pallas_call x8, Pallas kernels, call(): pl.pallas_call(kernel, out_shape=[jax.ShapeDtypeStruct(s, t) for s, t in...  17.3 us
    ppermute x10, starting transfers between devices, sent(): return lax.ppermute(block, AXES, route)  15.5 us
    ppermute x10, waiting for transfers between devices, sent(): return lax.ppermute(block, AXES, route)  4.83 us
  transfers between devices with their start and end apart: 10, of which 3 were waited for; matrix products, arithmetic and copies ran while one was open for 0% of the time, Pallas kernels for 18%

profile of v9, /device:TPU:0, one launch (start us, length us, event | category | flops | bytes accessed | tf_op | source)
XLA Modules:
  0.0 38.6 jit_solution(9621352664774650216)
XLA Ops:
  0.7 1.4 %pack.1 = (bf16[112,384]{1,0:T(8,128)(2,1)S(1)}, bf16[112,384]{1,0:T(8,128)(2,1)S(1)}, bf16[16,384]{1,0:T(8,128)(2,1)S(1)}) custom-call(s32[1,4]{1,0:T(1,128)} %counts_in.1, f32[9,8,384]{2,1,0:T(8,128)} %bitcast.18, f32[9,8,384]{2,1,0:T(8,128)} %bitcast.20, f32[9,8,384]{2,1,0:T(8,128)} %bitcast.22, s32[9,384]{1,0:T(8,128)} %mask.1), custom_call_target="tpu_custom_call" | custom-call | flops 1342177280 | bytes 8388608 | tf_op jit(solution)/shard_map/pack/pallas_call | solution.py:373
  2.0 0.0 copy-start.8
  2.0 5.5 %collective-permute-start = (bf16[112,384]{1,0:T(8,128)(2,1)S(1)}, bf16[112,384]{1,0:T(8,128)(2,1)S(1)}, u32[]{:S(2)}, u32[]{:S(2)}) collective-permute-start(bf16[112,384]{1,0:T(8,128)(2,1)S(1)} %get-tuple-element.20), channel_id=1, source_target_pairs={{0,15},{1,2},{2,1},{3,4},{4,3},{5,6},{6,5},{7,8},{8,7},{9,10},{10,... | collective-permute-start | bytes 258056 | tf_op jit(solution)/shard_map/ppermute | solution.py:30
  7.5 0.7 %collective-permute-start.1 = (bf16[16,384]{1,0:T(8,128)(2,1)S(1)}, bf16[16,384]{1,0:T(8,128)(2,1)S(1)}, u32[]{:S(2)}, u32[]{:S(2)}) collective-permute-start(bf16[16,384]{1,0:T(8,128)(2,1)S(1)} %get-tuple-element.21.own), channel_id=1, source_target_pairs={{0,14},{1,15},{2,0},{3,1},{4,2},{5,3},{6,4},{7,5},{8,6},{9,7},{10,... | collective-permute-start | bytes 36872 | tf_op jit(solution)/shard_map/ppermute | solution.py:30
  8.2 0.0 copy-start.3
  8.3 0.0 copy-start.4
  8.3 0.0 copy-start.5
  8.3 0.0 copy-start.6
  8.3 0.0 copy-start.9
  8.3 0.0 copy-start.10
  8.3 0.0 copy-start.14
  8.3 0.0 copy-start.15
  8.3 0.0 copy-start.16
  8.4 0.7 %plain.1 = f32[320,512]{1,0:T(8,128)S(1)} custom-call(bf16[227,512]{1,0:T(8,128)(2,1)S(1)} %bitcast.12, bf16[227,512]{1,0:T(8,128)(2,1)S(1)} %copy-done.1, s32[1,512]{1,0:T(1,128)S(1)} %bitcast.24, bf16[320,512]{1,0:T(8,128)(2,1)S(1)} %copy-done.13), custom_call_target="tpu_custom_call" | custom-call | flops 1342177280 | bytes 8388608 | tf_op jit(solution)/shard_map/plain/pallas_call | solution.py:373
  9.1 2.2 %collective-permute-done.1.far = bf16[16,384]{1,0:T(8,128)(2,1)S(1)} collective-permute-done((bf16[16,384]{1,0:T(8,128)(2,1)S(1)}, bf16[16,384]{1,0:T(8,128)(2,1)S(1)}, u32[]{:S(2)}, u32[]{:S(2)}) %collective-permute-start.1) | collective-permute-done | bytes 12320 | tf_op jit(solution)/shard_map/ppermute | solution.py:30
  11.2 1.1 %latents.1 = (bf16[320,512]{1,0:T(8,128)(2,1)S(1)}, f32[1,512]{1,0:T(1,128)S(1)}, s32[1,1536]{1,0:T(1,128)S(1)}) custom-call(bf16[112,384]{1,0:T(8,128)(2,1)S(1)} %collective-permute-done.outer, bf16[16,384]{1,0:T(8,128)(2,1)S(1)} %collective-permute-done.1.far, bf16[112,384]{1,0:T(8,128)(2,1)S(1)} %collective-permute-done.2.inner, ...), custom_call_target="tpu_custom_call" | custom-call | bytes 1048576 | tf_op jit(solution)/shard_map/latents/pallas_call | solution.py:373
  12.3 3.1 %collective-permute-start.3 = (bf16[320,512]{1,0:T(8,128)(2,1)S(1)}, bf16[320,512]{1,0:T(8,128)(2,1)S(1)}, u32[]{:S(2)}, u32[]{:S(2)}) collective-permute-start(bf16[320,512]{1,0:T(8,128)(2,1)S(1)} %get-tuple-element.23.latent), channel_id=1, source_target_pairs={{0,15},{1,2},{2,1},{3,4},{4,3},{5,6},{6,5},{7,8},{8,7},{9,10},{10,... | collective-permute-start | bytes 983048 | tf_op jit(solution)/shard_map/ppermute | solution.py:30
  15.4 0.2 ready.1
  15.7 0.0 copy-start.2
  15.7 0.0 copy-start.11
  15.7 0.0 copy-start.12
  15.7 0.0 copy-start.17
  15.7 0.0 copy-start.18
  15.7 4.7 %own.1 = (bf16[8,320,512]{2,1,0:T(8,128)(2,1)S(1)}, f32[320,512]{1,0:T(8,128)S(1)}, f32[320,512]{1,0:T(8,128)S(1)}) custom-call(bf16[320,512]{1,0:T(8,128)(2,1)S(1)} %get-tuple-element.23.latent, bf16[1536,512]{1,0:T(8,128)(2,1)S(1)} %copy-done.9, bf16[4,2560]{1,0:T(4,128)(2,1)S(1)} %copy-done.14, bf16[4,512]{1,0:T(4,128)(2,1)S(1)} %copy-done.16, ...), custom_call_target="tpu_custom_call" | custom-call | flops 2181038080 | bytes 10485760 | tf_op jit(solution)/shard_map/own/pallas_call | solution.py:373
  20.4 1.3 %collective-permute-done.3.outer = bf16[320,512]{1,0:T(8,128)(2,1)S(1)} collective-permute-done((bf16[320,512]{1,0:T(8,128)(2,1)S(1)}, bf16[320,512]{1,0:T(8,128)(2,1)S(1)}, u32[]{:S(2)}, u32[]{:S(2)}) %collective-permute-start.3) | collective-permute-done | bytes 327712 | tf_op jit(solution)/shard_map/ppermute | solution.py:30
  21.7 6.6 %mesh.1 = (bf16[320,512]{1,0:T(8,128)(2,1)S(1)}, bf16[16,384]{1,0:T(8,128)(2,1)S(1)}) custom-call(bf16[320,512]{1,0:T(8,128)(2,1)S(1)} %collective-permute-done.3.outer, bf16[320,512]{1,0:T(8,128)(2,1)S(1)} %collective-permute-done.4.inner, bf16[320,512]{1,0:T(8,128)(2,1)S(1)} %get-tuple-element.23.latent, bf16[1536,512]{1,0:T(8,128)(2,1)S(1)} %copy-done.9, ...), custom_call_target="tpu_custom_call" | custom-call | flops 2516582400 | bytes 10485760 | tf_op jit(solution)/shard_map/mesh/pallas_call | solution.py:373
  28.3 0.1 collective-permute-start.5
  28.4 5.2 %collective-permute-start.7 = (bf16[16,384]{1,0:T(8,128)(2,1)S(1)}, bf16[16,384]{1,0:T(8,128)(2,1)S(1)}, u32[]{:S(2)}, u32[]{:S(2)}) collective-permute-start(bf16[16,384]{1,0:T(8,128)(2,1)S(1)} %get-tuple-element.30.here_flux), channel_id=1, source_target_pairs={{0,14},{1,15},{2,4},{3,5},{4,2},{5,3},{6,8},{7,9},{8,6},{9,7},{10,... | collective-permute-start | bytes 36872 | tf_op jit(solution)/shard_map/ppermute | solution.py:30
  33.6 0.9 %collective-permute-start.9 = (bf16[16,384]{1,0:T(8,128)(2,1)S(1)}, bf16[16,384]{1,0:T(8,128)(2,1)S(1)}, u32[]{:S(2)}, u32[]{:S(2)}) collective-permute-start(bf16[16,384]{1,0:T(8,128)(2,1)S(1)} %get-tuple-element.30.here_flux), channel_id=1, source_target_pairs={{0,2},{1,3},{2,0},{3,1},{4,6},{5,7},{6,4},{7,5},{8,10},{9,11},{10,... | collective-permute-start | bytes 36872 | tf_op jit(solution)/shard_map/ppermute | solution.py:30
  34.5 1.4 %decode.1 = bf16[227,512]{1,0:T(8,128)(2,1)} custom-call(bf16[320,512]{1,0:T(8,128)(2,1)S(1)} %get-tuple-element.28.node_new, bf16[227,512]{1,0:T(8,128)(2,1)S(1)} %bitcast.17, s32[1,512]{1,0:T(1,128)S(1)} %bitcast.27, bf16[227,512]{1,0:T(8,128)(2,1)S(1)} %bitcast.15, f32[1,512]{1,0:T(1,128)S(1)} %get-tuple-element.29.surface), custom_call_target="tpu_custom_call" | custom-call | flops 223150080 | bytes 1048576 | tf_op jit(solution)/shard_map/decode/pallas_call | solution.py:373
  35.9 1.4 %collective-permute-done.9.near = bf16[16,384]{1,0:T(8,128)(2,1)S(1)} collective-permute-done((bf16[16,384]{1,0:T(8,128)(2,1)S(1)}, bf16[16,384]{1,0:T(8,128)(2,1)S(1)}, u32[]{:S(2)}, u32[]{:S(2)}) %collective-permute-start.9) | collective-permute-done | bytes 12320 | tf_op jit(solution)/shard_map/ppermute | solution.py:30
  37.3 1.3 %ocean.1 = f32[9,8,384]{2,1,0:T(8,128)} custom-call(bf16[16,384]{1,0:T(8,128)(2,1)S(1)} %collective-permute-done.5.before_1, bf16[16,384]{1,0:T(8,128)(2,1)S(1)} %collective-permute-done.6.before_3, bf16[16,384]{1,0:T(8,128)(2,1)S(1)} %collective-permute-done.7.far, bf16[16,384]{1,0:T(8,128)(2,1)S(1)} %collective-permute-done.8.after_1, ...), custom_call_target="tpu_custom_call" | custom-call | bytes 4194304 | tf_op jit(solution)/shard_map/ocean/pallas_call | solution.py:373
  (34 shorter events, 0.1 us)
Async XLA Ops:
  0.6 7.6 %copy-start = (bf16[512,227]{0,1:T(8,128)(2,1)S(1)}, bf16[512,227]{0,1:T(8,128)(2,1)}, u32[]{:S(2)}) copy-start(bf16[512,227]{0,1:T(8,128)(2,1)} %param.20) | copy-start | bytes 697348
  0.6 7.6 %copy-start.7 = (s32[512]{0:T(512)S(1)}, s32[512]{0:T(512)}, u32[]{:S(2)}) copy-start(s32[512]{0:T(512)} %param.24) | copy-start | bytes 6148
  0.7 7.6 %copy-start.13 = (bf16[320,512]{1,0:T(8,128)(2,1)S(1)}, bf16[320,512]{1,0:T(8,128)(2,1)}, u32[]{:S(2)}) copy-start(bf16[320,512]{1,0:T(8,128)(2,1)} %mesh_state.1) | copy-start | bytes 983044
  0.7 7.6 %copy-start.1 = (bf16[227,512]{1,0:T(8,128)(2,1)S(1)}, bf16[227,512]{1,0:T(8,128)(2,1)}, u32[]{:S(2)}) copy-start(bf16[227,512]{1,0:T(8,128)(2,1)} %w_encode.3) | copy-start | bytes 697348
  2.0 9.2 %copy-start.8 = (s32[1,4,192]{2,1,0:T(4,128)S(1)}, s32[1,4,192]{2,1,0:T(4,128)}, u32[]{:S(2)}) copy-start(s32[1,4,192]{2,1,0:T(4,128)} %param.29) | copy-start | bytes 9220
  2.0 9.2 %collective-permute-start = (bf16[112,384]{1,0:T(8,128)(2,1)S(1)}, bf16[112,384]{1,0:T(8,128)(2,1)S(1)}, u32[]{:S(2)}, u32[]{:S(2)}) collective-permute-start(bf16[112,384]{1,0:T(8,128)(2,1)S(1)} %get-tuple-element.20), channel_id=1, source_target_pairs={{0,15},{1,2},{2,1},{3,4},{4,3},{5,6},{6,5},{7,8},{8,7},{9,10},{10,... | collective-permute-start | bytes 258056 | tf_op jit(solution)/shard_map/ppermute | solution.py:30
  7.5 3.7 %collective-permute-start.2 = (bf16[112,384]{1,0:T(8,128)(2,1)S(1)}, bf16[112,384]{1,0:T(8,128)(2,1)S(1)}, u32[]{:S(2)}, u32[]{:S(2)}) collective-permute-start(bf16[112,384]{1,0:T(8,128)(2,1)S(1)} %get-tuple-element.22), channel_id=1, source_target_pairs={{0,1},{1,0},{2,3},{3,2},{4,5},{5,4},{6,7},{7,6},{8,9},{9,8},{10,11... | collective-permute-start | bytes 258056 | tf_op jit(solution)/shard_map/ppermute | solution.py:30
  7.5 3.7 %collective-permute-start.1 = (bf16[16,384]{1,0:T(8,128)(2,1)S(1)}, bf16[16,384]{1,0:T(8,128)(2,1)S(1)}, u32[]{:S(2)}, u32[]{:S(2)}) collective-permute-start(bf16[16,384]{1,0:T(8,128)(2,1)S(1)} %get-tuple-element.21.own), channel_id=1, source_target_pairs={{0,14},{1,15},{2,0},{3,1},{4,2},{5,3},{6,4},{7,5},{8,6},{9,7},{10,... | collective-permute-start | bytes 36872 | tf_op jit(solution)/shard_map/ppermute | solution.py:30
  8.2 7.1 %copy-start.3 = (f32[8,9,384]{2,0,1:T(8,128)S(1)}, f32[8,9,384]{2,0,1:T(8,128)}, u32[]{:S(2)}) copy-start(f32[8,9,384]{2,0,1:T(8,128)} %param.25) | copy-start | bytes 331780
  8.3 7.1 %copy-start.4 = (f32[8,9,384]{2,0,1:T(8,128)S(1)}, f32[8,9,384]{2,0,1:T(8,128)}, u32[]{:S(2)}) copy-start(f32[8,9,384]{2,0,1:T(8,128)} %param.26) | copy-start | bytes 331780
  8.3 7.1 %copy-start.5 = (f32[8,9,384]{2,0,1:T(8,128)S(1)}, f32[8,9,384]{2,0,1:T(8,128)}, u32[]{:S(2)}) copy-start(f32[8,9,384]{2,0,1:T(8,128)} %param.27) | copy-start | bytes 331780
  8.3 7.1 %copy-start.6 = (s32[9,384]{1,0:T(8,128)S(1)}, s32[9,384]{1,0:T(8,128)}, u32[]{:S(2)}) copy-start(s32[9,384]{1,0:T(8,128)} %mask.1) | copy-start | bytes 41476
  8.3 7.3 %copy-start.9 = (bf16[1536,512]{1,0:T(8,128)(2,1)S(1)}, bf16[1536,512]{1,0:T(8,128)(2,1)}, u32[]{:S(2)}) copy-start(bf16[1536,512]{1,0:T(8,128)(2,1)} %w_in.3) | copy-start | bytes 4718596
  8.3 7.3 %copy-start.10 = (bf16[1024,512]{1,0:T(8,128)(2,1)S(1)}, bf16[1024,512]{1,0:T(8,128)(2,1)}, u32[]{:S(2)}) copy-start(bf16[1024,512]{1,0:T(8,128)(2,1)} %w_node_in.3) | copy-start | bytes 3145732
  8.3 7.3 %copy-start.14 = (bf16[4,2560]{1,0:T(4,128)(2,1)S(1)}, bf16[4,2560]{1,0:T(4,128)(2,1)}, u32[]{:S(2)}) copy-start(bf16[4,2560]{1,0:T(4,128)(2,1)} %geometry.1) | copy-start | bytes 61444
  8.3 7.3 %copy-start.15 = (s32[320,8]{0,1:T(8,128)S(1)}, s32[320,8]{0,1:T(8,128)}, u32[]{:S(2)}) copy-start(s32[320,8]{0,1:T(8,128)} %param.23) | copy-start | bytes 30724
  8.3 7.3 %copy-start.16 = (bf16[4,512]{1,0:T(4,128)(2,1)S(1)}, bf16[4,512]{1,0:T(4,128)(2,1)}, u32[]{:S(2)}) copy-start(bf16[4,512]{1,0:T(4,128)(2,1)} %w_geometry.1) | copy-start | bytes 12292
  12.3 9.4 %collective-permute-start.3 = (bf16[320,512]{1,0:T(8,128)(2,1)S(1)}, bf16[320,512]{1,0:T(8,128)(2,1)S(1)}, u32[]{:S(2)}, u32[]{:S(2)}) collective-permute-start(bf16[320,512]{1,0:T(8,128)(2,1)S(1)} %get-tuple-element.23.latent), channel_id=1, source_target_pairs={{0,15},{1,2},{2,1},{3,4},{4,3},{5,6},{6,5},{7,8},{8,7},{9,10},{10,... | collective-permute-start | bytes 983048 | tf_op jit(solution)/shard_map/ppermute | solution.py:30
  15.4 6.3 %collective-permute-start.4 = (bf16[320,512]{1,0:T(8,128)(2,1)S(1)}, bf16[320,512]{1,0:T(8,128)(2,1)S(1)}, u32[]{:S(2)}, u32[]{:S(2)}) collective-permute-start(bf16[320,512]{1,0:T(8,128)(2,1)S(1)} %get-tuple-element.23.latent), channel_id=1, source_target_pairs={{0,1},{1,0},{2,3},{3,2},{4,5},{5,4},{6,7},{7,6},{8,9},{9,8},{10,11... | collective-permute-start | bytes 983048 | tf_op jit(solution)/shard_map/ppermute | solution.py:30
  15.7 6.0 %copy-start.2 = (bf16[512,227]{0,1:T(8,128)(2,1)S(1)}, bf16[512,227]{0,1:T(8,128)(2,1)}, u32[]{:S(2)}) copy-start(bf16[512,227]{0,1:T(8,128)(2,1)} %param.37) | copy-start | bytes 697348
  15.7 6.0 %copy-start.11 = (bf16[512,512]{1,0:T(8,128)(2,1)S(1)}, bf16[512,512]{1,0:T(8,128)(2,1)}, u32[]{:S(2)}) copy-start(bf16[512,512]{1,0:T(8,128)(2,1)} %w_out.1) | copy-start | bytes 1572868
  15.7 6.0 %copy-start.12 = (bf16[512,512]{1,0:T(8,128)(2,1)S(1)}, bf16[512,512]{1,0:T(8,128)(2,1)}, u32[]{:S(2)}) copy-start(bf16[512,512]{1,0:T(8,128)(2,1)} %w_node_out.1) | copy-start | bytes 1572868
  15.7 6.0 %copy-start.17 = (f32[512]{0:T(512)S(1)}, f32[512]{0:T(512)}, u32[]{:S(2)}) copy-start(f32[512]{0:T(512)} %param.38) | copy-start | bytes 6148
  15.7 6.0 %copy-start.18 = (f32[512]{0:T(512)S(1)}, f32[512]{0:T(512)}, u32[]{:S(2)}) copy-start(f32[512]{0:T(512)} %param.39) | copy-start | bytes 6148
  28.3 7.6 %collective-permute-start.5 = (bf16[16,384]{1,0:T(8,128)(2,1)S(1)}, bf16[16,384]{1,0:T(8,128)(2,1)S(1)}, u32[]{:S(2)}, u32[]{:S(2)}) collective-permute-start(bf16[16,384]{1,0:T(8,128)(2,1)S(1)} %get-tuple-element.30.here_flux), channel_id=1, source_target_pairs={{0,1},{1,2},{2,3},{3,4},{4,5},{5,6},{6,7},{7,8},{8,9},{9,10},{10,1... | collective-permute-start | bytes 36872 | tf_op jit(solution)/shard_map/ppermute | solution.py:30
  28.4 7.5 %collective-permute-start.6 = (bf16[16,384]{1,0:T(8,128)(2,1)S(1)}, bf16[16,384]{1,0:T(8,128)(2,1)S(1)}, u32[]{:S(2)}, u32[]{:S(2)}) collective-permute-start(bf16[16,384]{1,0:T(8,128)(2,1)S(1)} %get-tuple-element.30.here_flux), channel_id=1, source_target_pairs={{0,3},{1,4},{2,5},{3,6},{4,7},{5,8},{6,9},{7,10},{8,11},{9,12},{10... | collective-permute-start | bytes 36872 | tf_op jit(solution)/shard_map/ppermute | solution.py:30
  28.4 7.5 %collective-permute-start.7 = (bf16[16,384]{1,0:T(8,128)(2,1)S(1)}, bf16[16,384]{1,0:T(8,128)(2,1)S(1)}, u32[]{:S(2)}, u32[]{:S(2)}) collective-permute-start(bf16[16,384]{1,0:T(8,128)(2,1)S(1)} %get-tuple-element.30.here_flux), channel_id=1, source_target_pairs={{0,14},{1,15},{2,4},{3,5},{4,2},{5,3},{6,8},{7,9},{8,6},{9,7},{10,... | collective-permute-start | bytes 36872 | tf_op jit(solution)/shard_map/ppermute | solution.py:30
  33.6 2.3 %collective-permute-start.8 = (bf16[16,384]{1,0:T(8,128)(2,1)S(1)}, bf16[16,384]{1,0:T(8,128)(2,1)S(1)}, u32[]{:S(2)}, u32[]{:S(2)}) collective-permute-start(bf16[16,384]{1,0:T(8,128)(2,1)S(1)} %get-tuple-element.30.here_flux), channel_id=1, source_target_pairs={{0,15},{1,0},{2,1},{3,2},{4,3},{5,4},{6,5},{7,6},{8,7},{9,8},{10,9... | collective-permute-start | bytes 36872 | tf_op jit(solution)/shard_map/ppermute | solution.py:30
  33.6 3.7 %collective-permute-start.9 = (bf16[16,384]{1,0:T(8,128)(2,1)S(1)}, bf16[16,384]{1,0:T(8,128)(2,1)S(1)}, u32[]{:S(2)}, u32[]{:S(2)}) collective-permute-start(bf16[16,384]{1,0:T(8,128)(2,1)S(1)} %get-tuple-element.30.here_flux), channel_id=1, source_target_pairs={{0,2},{1,3},{2,0},{3,1},{4,6},{5,7},{6,4},{7,5},{8,10},{9,11},{10,... | collective-permute-start | bytes 36872 | tf_op jit(solution)/shard_map/ppermute | solution.py:30
